TPU v7x, 32 devices: a whole 2x2x4 slice. The times are simulated.
32 devices in a mesh: blk: 4 (over y, x), dom: 8 (over z, core).
Axes of the slice: x: 2, y: 2, z: 4, core: 2. Of those that a mesh axis runs over, the one named last changes fastest.
Arguments:
- positions: float32 [3, 32768], P(None, ('blk', 'dom')), may hold values from -6 to 6
- line_vectors: float32 [3, 32768], P(None, ('blk', 'dom')), may hold values from -6 to 6
- burgers: float32 [3, 32768], P(None, ('blk', 'dom')), may hold values from -6 to 6
- mobility: float32 [32768], P(('blk', 'dom')), may hold values from 0.5 to 2
- close_list: int32 [32, 32768], P(None, ('blk', 'dom')), may hold values from 0 to 256, as said below
- ghost_map: int32 [4, 16384], P(None, ('blk', 'dom')), may hold values from 0 to 1023, as said below
Outputs:
- new_positions: float32 [3, 32768], P(None, ('blk', 'dom'))
- velocity: float32 [3, 32768], P(None, ('blk', 'dom'))
Inputs may be any that keep to these rules, and one draw needn't show every extreme that they name: `close_list`: each entry is a place in the window of the segment's cell: below 128 a segment of the same cell, 128 + u the u-th row of the cell's ghost window, and 256 an empty slot. `ghost_map`: for each subcycle, each device's run of 512 entries holds first 256 distinct local segment numbers below 512 (the ghosts of the lower domain), the first of them 0, then 256 distinct local numbers of at least 1024 - 512 (the ghosts of the upper domain), the first of them 1024 - 1.
All inputs are finite; a program needn't handle non-finite values.
Results may differ from a plain program's by a relative error of at most 0.0005.
Values sent between devices are 32-bit elements; how exact they have to be, the bound alone decides.
No kernel may reach another device: no remote copies, remote signals or barrier semaphores. Data moves between devices by JAX's collectives and lax.ppermute only.
A program may use at most 64 MiB of HBM per device.

v0:
```python
import math

import jax
import jax.numpy as jnp
from jax import lax
from jax.sharding import PartitionSpec as P

CELL_SEGS = 128
SLOTS = 32
GHOSTS = 256
SUBS = 4


long_core = 1.0
short_core = 0.25
time_step = 0.05


def shifted(value, axis, steps):
    count = lax.axis_size(axis)
    pairs = [(source, (source + steps) % count) for source in range(count)]
    return lax.ppermute(value, axis, pairs)


def extended(cells, sides, width):
    for axis, dim in sides:
        count = lax.axis_size(axis)
        head = lax.slice_in_dim(cells, 0, width, axis=dim)
        tail = lax.slice_in_dim(cells, cells.shape[dim] - width, cells.shape[dim], axis=dim)
        cells = jnp.concatenate(
            [
                lax.ppermute(tail, axis, [(i, (i + 1) % count) for i in range(count)]),
                cells,
                lax.ppermute(head, axis, [((i + 1) % count, i) for i in range(count)]),
            ],
            axis=dim,
        )
    return cells


def pair_weights(target, source, core):
    delta_x = target[0][..., :, None] - source[0][..., None, :]
    delta_y = target[1][..., :, None] - source[1][..., None, :]
    delta_z = target[2][..., :, None] - source[2][..., None, :]
    radius = delta_x * delta_x + delta_y * delta_y + delta_z * delta_z + core * core
    inverse = lax.rsqrt(radius)
    line_dot = (
        target[3][..., :, None] * source[3][..., None, :]
        + target[4][..., :, None] * source[4][..., None, :]
        + target[5][..., :, None] * source[5][..., None, :]
    )
    burgers_dot = (
        target[6][..., :, None] * source[6][..., None, :]
        + target[7][..., :, None] * source[7][..., None, :]
        + target[8][..., :, None] * source[8][..., None, :]
    )
    weight = burgers_dot * line_dot * inverse * inverse * inverse
    return (weight, (delta_x, delta_y, delta_z))


def cell_force(target, source):
    weight, deltas = pair_weights(target, source, long_core)
    return jnp.stack([jnp.sum(weight * delta, axis=-1) for delta in deltas])


def as_cells(rows):
    return rows.reshape(rows.shape[0], -1, CELL_SEGS)


def flatten_cells(cell_rows):
    return cell_rows.reshape(cell_rows.shape[0], -1)


def slot_force(own_rows, partners):
    delta_x = own_rows[0][None] - partners[0]
    delta_y = own_rows[1][None] - partners[1]
    delta_z = own_rows[2][None] - partners[2]
    radius = delta_x * delta_x + delta_y * delta_y + delta_z * delta_z + short_core * short_core
    inverse = lax.rsqrt(radius)
    line_dot = (
        own_rows[3][None] * partners[3]
        + own_rows[4][None] * partners[4]
        + own_rows[5][None] * partners[5]
    )
    burgers_dot = (
        own_rows[6][None] * partners[6]
        + own_rows[7][None] * partners[7]
        + own_rows[8][None] * partners[8]
    )
    weight = burgers_dot * line_dot * inverse * inverse * inverse
    return jnp.stack(
        [jnp.sum(weight * delta_x, 0), jnp.sum(weight * delta_y, 0), jnp.sum(weight * delta_z, 0)]
    )


def local(positions, line_vectors, burgers, mobility, close_list, ghost_map):
    seg_count = positions.shape[1]
    statics = jnp.concatenate([line_vectors, burgers], 0)
    seg_state = jnp.concatenate([positions, statics], 0)
    cell_rows = as_cells(seg_state)
    blocks = lax.axis_size("blk")
    cycle_reach = blocks // 4
    forces = cell_force(cell_rows, cell_rows)
    upward = seg_state
    downward = seg_state
    for offset in range(cycle_reach):
        upward = shifted(upward, "blk", 1)
        downward = shifted(downward, "blk", -1)
        forces = (
            forces
            + cell_force(cell_rows, as_cells(upward))
            + cell_force(cell_rows, as_cells(downward))
        )
    long_force = flatten_cells(forces) * (1.0 / math.sqrt((2 * cycle_reach + 1) * CELL_SEGS))
    window_count = 2 * GHOSTS // CELL_SEGS
    seg_index = jnp.arange(seg_count, dtype=jnp.int32)
    cell_index = seg_index // CELL_SEGS
    own_place = cell_index[None, :] * CELL_SEGS + close_list
    ghost_place = (
        seg_count + cell_index[None, :] % window_count * CELL_SEGS + (close_list - CELL_SEGS)
    )
    empty_place = seg_count + 2 * GHOSTS
    places = jnp.where(
        close_list < CELL_SEGS,
        own_place,
        jnp.where(close_list < 2 * CELL_SEGS, ghost_place, empty_place),
    )

    def ghost_rows_of(current, subcycle):
        full_rows = jnp.concatenate([current, statics], 0)
        picked = jnp.take(full_rows, ghost_map[subcycle], axis=1)
        near_rows = extended(picked, (("dom", 1),), GHOSTS)
        from_lower = near_rows[:, :GHOSTS]
        from_upper = near_rows[:, 3 * GHOSTS :]
        return (full_rows, jnp.concatenate([from_lower, from_upper], 1))

    def short_force(full_rows, ghost_rows):
        extended_rows = jnp.concatenate([full_rows, ghost_rows], 1)
        partners = jnp.take(extended_rows, places, axis=1, mode="fill", fill_value=0.0)
        return slot_force(full_rows, partners) * (1.0 / math.sqrt(SLOTS))

    velocity = jnp.zeros_like(positions)
    for subcycle in range(SUBS):
        full_rows, ghost_rows = ghost_rows_of(positions, subcycle)
        first_vel = mobility * (long_force + short_force(full_rows, ghost_rows))
        guess_pos = positions + time_step * first_vel
        full_rows, ghost_rows = ghost_rows_of(guess_pos, subcycle)
        second = mobility * (long_force + short_force(full_rows, ghost_rows))
        velocity = 0.5 * (first_vel + second)
        positions = positions + time_step * velocity
    return (positions, velocity)


def solution(mesh):
    return jax.shard_map(
        local,
        mesh=mesh,
        in_specs=(
            P(None, ("blk", "dom")),
            P(None, ("blk", "dom")),
            P(None, ("blk", "dom")),
            P(("blk", "dom")),
            P(None, ("blk", "dom")),
            P(None, ("blk", "dom")),
        ),
        out_specs=(P(None, ("blk", "dom")), P(None, ("blk", "dom"))),
        check_vma=False,
    )
```

profile of v0, /device:TPU:0, one launch (start us, length us, event | category | flops | bytes accessed | tf_op | source)
XLA Modules:
  0.0 1030.9 jit_solution(8035574085219828067)
XLA Ops:
  0.7 0.8 pad_maximum_fusion.15
  1.5 3.9 collective-permute-start.1
  5.7 0.9 fusion.191
  6.6 1.0 gather_fusion
  7.8 3.5 collective-permute-start.3
  11.8 2.3 collective-permute-done.2
  14.2 108.2 %gather_fusion.1 = f32[32768,9]{1,0:T(8,128)} fusion(f32[9,1536]{0,1:T(8,128)S(1)} %pad_maximum_fusion, s32[32768]{0:T(1024)S(1)} %broadcast_clamp_fusion), kind=kCustom, calls=%fused_computation.1.clone | custom fusion | bytes 2490368 | tf_op jit(solution)/shard_map/jit(_take)/gather | solution.py:139
  122.4 10.0 copy.148
  132.8 2.6 fusion.18
  135.5 2.2 fusion.11
  138.0 1.0 gather_fusion.2
  139.2 1.2 collective-permute-start.4
  140.4 2.4 collective-permute-start.5
  142.9 3.5 collective-permute-done.4
  146.4 108.2 %gather_fusion.3 = f32[32768,9]{1,0:T(8,128)} fusion(f32[9,1536]{0,1:T(8,128)S(1)} %pad_maximum_fusion.1, s32[32768]{0:T(1024)S(1)} %broadcast_clamp_fusion), kind=kCustom, calls=%fused_computation.9.clone | custom fusion | bytes 2490368 | tf_op jit(solution)/shard_map/jit(_take)/gather | solution.py:139
  254.6 10.0 copy.151
  265.3 1.0 gather_fusion.4
  266.7 3.4 collective-permute-start.7
  270.1 3.8 collective-permute-done.6
  274.0 108.2 %gather_fusion.5 = f32[32768,9]{1,0:T(8,128)} fusion(f32[9,1536]{0,1:T(8,128)S(1)} %pad_maximum_fusion.2, s32[32768]{0:T(1024)S(1)} %broadcast_clamp_fusion), kind=kCustom, calls=%fused_computation.10.clone | custom fusion | bytes 2490368 | tf_op jit(solution)/shard_map/jit(_take)/gather | solution.py:139
  382.3 10.0 copy.154
  392.9 1.0 gather_fusion.6
  394.2 3.5 collective-permute-start.9
  397.7 3.5 collective-permute-done.8
  401.3 108.2 %gather_fusion.7 = f32[32768,9]{1,0:T(8,128)} fusion(f32[9,1536]{0,1:T(8,128)S(1)} %pad_maximum_fusion.3, s32[32768]{0:T(1024)S(1)} %broadcast_clamp_fusion), kind=kCustom, calls=%fused_computation.11.clone | custom fusion | bytes 2490368 | tf_op jit(solution)/shard_map/jit(_take)/gather | solution.py:139
  509.5 10.0 copy.157
  520.2 1.0 gather_fusion.8
  521.5 3.5 collective-permute-start.11
  525.0 3.8 collective-permute-done.10
  528.9 108.2 %gather_fusion.9 = f32[32768,9]{1,0:T(8,128)} fusion(f32[9,1536]{0,1:T(8,128)S(1)} %pad_maximum_fusion.4, s32[32768]{0:T(1024)S(1)} %broadcast_clamp_fusion), kind=kCustom, calls=%fused_computation.12.clone | custom fusion | bytes 2490368 | tf_op jit(solution)/shard_map/jit(_take)/gather | solution.py:139
  637.1 10.0 copy.160
  647.8 1.0 gather_fusion.10
  649.1 3.5 collective-permute-start.13
  652.6 3.5 collective-permute-done.12
  656.2 108.2 %gather_fusion.11 = f32[32768,9]{1,0:T(8,128)} fusion(f32[9,1536]{0,1:T(8,128)S(1)} %pad_maximum_fusion.5, s32[32768]{0:T(1024)S(1)} %broadcast_clamp_fusion), kind=kCustom, calls=%fused_computation.13.clone | custom fusion | bytes 2490368 | tf_op jit(solution)/shard_map/jit(_take)/gather | solution.py:139
  764.4 10.0 copy.163
  775.1 1.0 gather_fusion.12
  776.4 3.5 collective-permute-start.15
  779.9 3.8 collective-permute-done.14
  783.8 108.2 %gather_fusion.13 = f32[32768,9]{1,0:T(8,128)} fusion(f32[9,1536]{0,1:T(8,128)S(1)} %pad_maximum_fusion.6, s32[32768]{0:T(1024)S(1)} %broadcast_clamp_fusion), kind=kCustom, calls=%fused_computation.14.clone | custom fusion | bytes 2490368 | tf_op jit(solution)/shard_map/jit(_take)/gather | solution.py:139
  892.0 10.0 copy.166
  902.7 1.0 gather_fusion.14
  904.0 3.5 collective-permute-start.17
  907.5 3.5 collective-permute-done.16
  911.1 108.2 %gather_fusion.15 = f32[32768,9]{1,0:T(8,128)} fusion(f32[9,1536]{0,1:T(8,128)S(1)} %pad_maximum_fusion.7, s32[32768]{0:T(1024)S(1)} %broadcast_clamp_fusion), kind=kCustom, calls=%fused_computation.15.clone | custom fusion | bytes 2490368 | tf_op jit(solution)/shard_map/jit(_take)/gather | solution.py:139
  1019.3 10.0 copy.169
  1029.7 0.6 broadcast_multiply_fusion
  1030.3 0.6 multiply_add_fusion
  (119 shorter events, 7.4 us)
Async XLA Ops:
  0.6 10.8 %copy-start.4 = (f32[3,1024]{1,0:T(4,128)S(1)}, f32[3,1024]{1,0:T(4,128)}, u32[]{:S(2)}) copy-start(f32[3,1024]{1,0:T(4,128)} %param.10) | copy-start | bytes 36868
  0.6 10.7 %copy-start.1 = (f32[3,1024]{1,0:T(4,128)S(1)}, f32[3,1024]{1,0:T(4,128)}, u32[]{:S(2)}) copy-start(f32[3,1024]{1,0:T(4,128)} %param.11) | copy-start | bytes 36868
  0.7 10.7 %copy-start = (f32[3,1024]{1,0:T(4,128)S(1)}, f32[3,1024]{1,0:T(4,128)}, u32[]{:S(2)}) copy-start(f32[3,1024]{1,0:T(4,128)} %param.12) | copy-start | bytes 36868
  0.7 10.8 %copy-start.2 = (s32[32,1024]{1,0:T(8,128)S(1)}, s32[32,1024]{1,0:T(8,128)}, u32[]{:S(2)}) copy-start(s32[32,1024]{1,0:T(8,128)} %param.14) | copy-start | bytes 393220
  1.5 131.3 %collective-permute-start.1 = (f32[9,1024]{1,0:T(8,128)S(1)}, f32[9,1024]{1,0:T(8,128)S(1)}, u32[]{:S(2)}, u32[]{:S(2)}) collective-permute-start(f32[9,1024]{1,0:T(8,128)S(1)} %pad_maximum_fusion.15), channel_id=1, source_target_pairs={{0,24},{8,0},{16,8},{24,16},{1,25},{9,1},{17,9},{25,17},{2,26},{10... | collective-permute-start | bytes 110600 | tf_op jit(solution)/shard_map/ppermute | solution.py:22
  5.4 130.0 %collective-permute-start = (f32[9,1024]{1,0:T(8,128)S(1)}, f32[9,1024]{1,0:T(8,128)S(1)}, u32[]{:S(2)}, u32[]{:S(2)}) collective-permute-start(f32[9,1024]{1,0:T(8,128)S(1)} %pad_maximum_fusion.15), channel_id=1, source_target_pairs={{0,8},{8,16},{16,24},{24,0},{1,9},{9,17},{17,25},{25,1},{2,10},{10... | collective-permute-start | bytes 110600 | tf_op jit(solution)/shard_map/ppermute | solution.py:22
  7.8 6.3 collective-permute-start.2
  7.8 6.3 collective-permute-start.3
  132.6 5.1 copy-start.3
  139.2 7.1 collective-permute-start.4
  140.4 6.0 collective-permute-start.5
  266.5 7.5 collective-permute-start.6
  266.7 7.3 collective-permute-start.7
  394.1 7.1 collective-permute-start.8
  394.2 7.1 collective-permute-start.9
  521.4 7.5 collective-permute-start.10
  521.5 7.4 collective-permute-start.11
  649.0 7.1 collective-permute-start.12
  649.1 7.1 collective-permute-start.13
  776.3 7.5 collective-permute-start.14
  776.4 7.4 collective-permute-start.15
  903.9 7.1 collective-permute-start.16
  904.0 7.1 collective-permute-start.17
where the time goes:
time: 1030 us
  local copies, waits for them, and re-layouts  957 us (93%)
  starting transfers between devices  32.7 us (3%)
  waiting for transfers between devices  28 us (3%)
  other arithmetic  11.7 us (1%)
    gather x16, local copies, waits for them, and re-layouts, short_force(): jnp.take(extended_rows, places, axis=1, mode='fill', fill_value=0.0)  946 us
    ppermute x8, waiting for transfers between devices, extended(): lax.ppermute(tail, axis, [(i, (i + 1) % count) for i in range(count)])  27.9 us
    ppermute x8, starting transfers between devices, extended(): lax.ppermute(head, axis, [((i + 1) % count, i) for i in range(count)])  27 us
  transfers between devices with their start and end apart: 18, of which 8 were waited for; matrix products, arithmetic and copies ran while one was open for 12% of the time, Pallas kernels for 0%

commit v1 on v0

v1 whole, which is shorter than its diff:
```python
import math

import jax
import jax.numpy as jnp
from jax import lax
from jax.experimental import pallas as pl
from jax.experimental.pallas import tpu as pltpu
from jax.sharding import PartitionSpec as P

LANES = 128
ROWS = 8
long_core = 1.0
short_core = 0.25
time_step = 0.05


def lane_gather(row_block, places):
    return jnp.take_along_axis(row_block, places, axis=1, mode="promise_in_bounds")


def level_halves(domains, evals):
    levels = [{(0, 0), (0, 1)}]
    for _ in range(evals - 1):
        last = levels[-1]
        grown = set(last)
        for domain in {d for d, _ in last}:
            grown.add(((domain - 1) % domains, 1))
            grown.add(((domain + 1) % domains, 0))
        levels.append(grown)
    return [sorted(level) for level in levels[::-1]]


def step_kernel(domains, subs, ghosts, slots, tables, core_of, *refs):
    half = domains // 2
    pack_refs = refs[: 2 * half]
    close_refs = refs[2 * half : 4 * half]
    dom_table, half_table = refs[4 * half : 4 * half + 2]
    out_pos, out_vel = refs[4 * half + 2 : 4 * half + 4]
    pack, close, own_w, weight, pos, guess, first, long_, ghost, sem = refs[4 * half + 4 :]
    seg = pack.shape[2]
    cells = seg // LANES
    groups = slots // ROWS
    core = core_of()
    half_cells = cells // 2
    windows = 2 * ghosts // LANES
    scale = 1.0 / math.sqrt(slots)

    copies = []
    for j in range(half):
        for other in range(2):
            parity = core if other == 0 else 1 - core
            place = lax.rem(parity + 2 * j, domains)
            for which, (src, dst) in enumerate(((pack_refs, pack), (close_refs, close))):
                copy = pltpu.make_async_copy(src[other * half + j], dst.at[place], sem.at[which, other * half + j])
                copy.start()
                copies.append(copy)
    for copy in copies:
        copy.wait()

    row = lax.broadcasted_iota(jnp.int32, (ROWS, LANES), 0)
    even_row = lax.rem(row, 2) == 0
    x_rows = row < 2
    y_rows = row < 4

    def spread(source, d, at):
        return jnp.concatenate([jnp.broadcast_to(source[d, at + c : at + c + 1, :], (2, seg)) for c in (0, 1, 2, 2)], 0)

    def expand(d, carry):
        pos[d] = spread(pack, d, 0)
        long_[d] = spread(pack, d, 10)
        return carry

    lax.fori_loop(0, domains, expand, 0)

    def bcast(ref, d, at, lane):
        return jnp.broadcast_to(ref[d, at : at + 1, pl.ds(lane, LANES)], (ROWS, LANES))

    def ghost_places(d, sub, upper):
        at = 13 + sub // 2
        lane = (sub % 2) * 2 * ghosts + (0 if upper else ghosts)
        first_w = bcast(pack, d, at, lane)
        second_w = bcast(pack, d, at, lane + LANES)
        return jnp.where(even_row, first_w, second_w).astype(jnp.int32)

    def pick(source_cells, places, first_cell):
        lane = places & (LANES - 1)
        cell = places >> 7
        out = lane_gather(source_cells[0], lane)
        for k in range(1, len(source_cells)):
            out = jnp.where(cell == first_cell + k, lane_gather(source_cells[k], lane), out)
        return out

    def neighbours(d):
        return lax.rem(d + domains - 1, domains), lax.rem(d + 1, domains)

    def pick_ghosts(ref, d, sub):
        low, up = neighbours(d)
        lower = pick(
            [ref[low, :, pl.ds((half_cells + k) * LANES, LANES)] for k in range(half_cells)],
            ghost_places(low, sub, False), half_cells)
        upper = pick(
            [ref[up, :, pl.ds(k * LANES, LANES)] for k in range(half_cells)],
            ghost_places(up, sub, True), 0)
        return lower, upper

    def store_ghosts(ref, d, sub, slot):
        lower, upper = pick_ghosts(ref, d, sub)
        ghost[slot, d, 0] = lower
        ghost[slot, d, 1] = upper

    def dots(mine, theirs):
        return mine[0] * theirs[0] + mine[1] * theirs[1] + mine[2] * theirs[2]

    def own_weights(d, carry):
        for q in range(cells):
            lane = q * LANES
            mine = [bcast(pack, d, 3 + c, lane) for c in range(6)]
            for g in range(groups):
                places = close[d, g * ROWS : (g + 1) * ROWS, pl.ds(lane, LANES)] & (LANES - 1)
                theirs = [lane_gather(m, places) for m in mine]
                own_w[d, g * ROWS : (g + 1) * ROWS, pl.ds(lane, LANES)] = (
                    dots(mine[:3], theirs[:3]) * dots(mine[3:], theirs[3:]) * scale)
        return carry

    lax.fori_loop(0, domains, own_weights, 0)

    def ghost_rows(slot, d, w):
        side, pair = divmod(w, 2)
        return [jnp.broadcast_to(ghost[slot, d, side, 2 * c + pair : 2 * c + pair + 1, :], (ROWS, LANES)) for c in range(3)]

    def where_of(i):
        return lax.rem(dom_table[i] + core, domains), half_table[i]

    def sub_weights(sub, start, stop):
        def one(i, carry):
            d, side = where_of(i)
            low, up = neighbours(d)
            low_places, up_places = ghost_places(low, sub, False), ghost_places(up, sub, True)
            for slot, at in ((1, 3), (2, 6)):
                def cells_of(dom, cell):
                    return [jnp.concatenate([jnp.broadcast_to(pack[dom, at + c : at + c + 1, pl.ds((cell + k) * LANES, LANES)], (2, LANES)) for c in (0, 1, 2, 2)], 0) for k in range(half_cells)]
                ghost[slot, d, 0] = pick(cells_of(low, half_cells), low_places, half_cells)
                ghost[slot, d, 1] = pick(cells_of(up, 0), up_places, 0)
            for k in range(half_cells):
                lane = pl.multiple_of(side * (half_cells * LANES) + k * LANES, LANES)
                mine = [bcast(pack, d, 3 + c, lane) for c in range(6)]
                far = ghost_rows(1, d, k % windows) + ghost_rows(2, d, k % windows)
                for g in range(groups):
                    at = slice(g * ROWS, (g + 1) * ROWS)
                    entry = close[d, at, pl.ds(lane, LANES)]
                    places = entry & (LANES - 1)
                    theirs = [lane_gather(m, places) for m in far]
                    far_w = dots(mine[:3], theirs[:3]) * dots(mine[3:], theirs[3:]) * scale
                    near_w = own_w[d, at, pl.ds(lane, LANES)]
                    weight[d, at, pl.ds(lane, LANES)] = jnp.where(
                        entry < LANES, near_w, jnp.where(entry < 2 * LANES, far_w, 0.0))
            return carry
        lax.fori_loop(start, stop, one, 0)

    def total(block):
        for shift in (4, 2, 1):
            block = block + pltpu.roll(block, shift, 0)
        return block

    def force(ref, d, lane, window):
        mine = [bcast(ref, d, 2 * c, lane) for c in range(3)]
        far = ghost_rows(0, d, window)
        sums = [None] * 3
        for g in range(groups):
            at = slice(g * ROWS, (g + 1) * ROWS)
            entry = close[d, at, pl.ds(lane, LANES)]
            places = entry & (LANES - 1)
            near = entry < LANES
            delta = [m - jnp.where(near, lane_gather(m, places), lane_gather(f, places)) for m, f in zip(mine, far)]
            radius = delta[0] * delta[0] + delta[1] * delta[1] + delta[2] * delta[2] + short_core * short_core
            inverse = lax.rsqrt(radius)
            w = weight[d, at, pl.ds(lane, LANES)] * (inverse * inverse * inverse)
            for c in range(3):
                term = w * delta[c]
                sums[c] = term if sums[c] is None else sums[c] + term
        sums = [total(s) for s in sums]
        return jnp.where(x_rows, sums[0], jnp.where(y_rows, sums[1], sums[2]))

    at = 0
    for sub in range(subs):
        for stage in range(2):
            start, stop, doms = tables[2 * sub + stage]
            source = guess if stage else pos
            if stage == 0:
                sub_weights(sub, start, stop)

            def ghosts_one(i, carry):
                store_ghosts(source, lax.rem(dom_table[i] + core, domains), sub, 0)
                return carry

            lax.fori_loop(doms[0], doms[1], ghosts_one, 0)

            def one(i, carry):
                d, side = where_of(i)
                for k in range(half_cells):
                    lane = pl.multiple_of(side * (half_cells * LANES) + k * LANES, LANES)
                    here = pl.ds(lane, LANES)
                    mob = bcast(pack, d, 9, lane)
                    vel = mob * (long_[d, :, here] + force(source, d, lane, k % windows))
                    if stage == 0:
                        first[d, :, here] = vel
                        guess[d, :, here] = pos[d, :, here] + time_step * vel
                    else:
                        vel = 0.5 * (first[d, :, here] + vel)
                        first[d, :, here] = vel
                        pos[d, :, here] = pos[d, :, here] + time_step * vel
                return carry

            lax.fori_loop(start, stop, one, 0)

    for c in range(3):
        out_pos[c : c + 1, :] = pos[core, 2 * c : 2 * c + 1, :]
        out_vel[c : c + 1, :] = first[core, 2 * c : 2 * c + 1, :]


def step(packs, closes, subs, ghosts, core_of):
    domains = len(packs)
    slots, seg = closes[0].shape
    rows = packs[0].shape[0]
    dom_list, half_list, tables = [], [], []
    for level in level_halves(domains, 2 * subs):
        start = len(dom_list)
        dom_list += [d for d, _ in level]
        half_list += [h for _, h in level]
        stop = len(dom_list)
        doms = sorted({d for d, _ in level})
        dom_list += doms
        half_list += [0] * len(doms)
        tables.append((start, stop, (stop, len(dom_list))))
    table = pl.BlockSpec(memory_space=pltpu.SMEM)
    far = pl.BlockSpec(memory_space=pl.ANY)
    wide = pltpu.VMEM((domains, slots, seg), jnp.float32)
    state = pltpu.VMEM((domains, ROWS, seg), jnp.float32)

    def kernel(*refs):
        step_kernel(domains, subs, ghosts, slots, tables, core_of, *refs)

    return pl.pallas_call(
        kernel,
        out_shape=[jax.ShapeDtypeStruct((3, seg), jnp.float32)] * 2,
        in_specs=[far] * (2 * domains) + [table] * 2,
        out_specs=[pl.BlockSpec(memory_space=pltpu.VMEM)] * 2,
        scratch_shapes=[
            pltpu.VMEM((domains, rows, seg), jnp.float32),
            pltpu.VMEM((domains, slots, seg), jnp.int32),
            wide, wide, state, state, state, state,
            pltpu.VMEM((3, domains, 2, ROWS, LANES), jnp.float32),
            pltpu.SemaphoreType.DMA((2, domains)),
        ],
        compiler_params=pltpu.CompilerParams(vmem_limit_bytes=48 * 2**20),
        name="step",
    )(*packs, *closes, jnp.array(dom_list, jnp.int32), jnp.array(half_list, jnp.int32))


def long_kernel(sources, seg, *refs):
    own = refs[:3]
    mob, gmap = refs[3:5]
    others = refs[5 : 5 + sources]
    pack, tiles = refs[5 + sources :]
    cells = seg // LANES
    scale = 1.0 / math.sqrt((sources + 1) * LANES)
    for s in range(sources + 1):
        for c in range(9):
            for q in range(cells):
                src = own[c // 3][c % 3 : c % 3 + 1, q * LANES : (q + 1) * LANES] if s == 0 else others[s - 1][c : c + 1, q * LANES : (q + 1) * LANES]
                tiles[s * 9 + c, q : q + 1, :] = src
    mine = [tiles[c] for c in range(9)]

    def one(i, carry):
        forces, moved = carry
        forces = list(forces)
        for s in range(sources + 1):
            other = moved[s * 9 : s * 9 + 9]
            delta = [mine[c] - other[c] for c in range(3)]
            radius = delta[0] * delta[0] + delta[1] * delta[1] + delta[2] * delta[2] + long_core * long_core
            inverse = lax.rsqrt(radius)
            line = mine[3] * other[3] + mine[4] * other[4] + mine[5] * other[5]
            burg = mine[6] * other[6] + mine[7] * other[7] + mine[8] * other[8]
            w = burg * line * (inverse * inverse * inverse)
            for c in range(3):
                forces[c] = forces[c] + w * delta[c]
        return tuple(forces), tuple(pltpu.roll(m, 1, 1) for m in moved)

    zero = jnp.zeros_like(mine[0])
    moved = tuple(tiles[k] for k in range(9 * (sources + 1)))
    forces, _ = lax.fori_loop(0, LANES, one, ((zero,) * 3, moved))
    for c in range(9):
        pack[c : c + 1, :] = own[c // 3][c % 3 : c % 3 + 1, :]
    pack[9:10, :] = mob[...]
    for c in range(3):
        f = forces[c] * scale
        for q in range(cells):
            pack[10 + c : 11 + c, q * LANES : (q + 1) * LANES] = f[q : q + 1, :]
    subs, wide = gmap.shape
    per = seg // wide
    for t in range(subs):
        pack[13 + t // per : 14 + t // per, (t % per) * wide : (t % per + 1) * wide] = gmap[t : t + 1, :].astype(jnp.float32)


def long_range(positions, line_vectors, burgers, mobility, ghost_map, others):
    seg = positions.shape[1]
    return pl.pallas_call(
        lambda *refs: long_kernel(len(others), seg, *refs),
        out_shape=jax.ShapeDtypeStruct((16, seg), jnp.float32),
        in_specs=[pl.BlockSpec(memory_space=pltpu.VMEM)] * (5 + len(others)),
        out_specs=pl.BlockSpec(memory_space=pltpu.VMEM),
        scratch_shapes=[pltpu.VMEM((9 * (len(others) + 1), seg // LANES, LANES), jnp.float32)],
        name="long_range",
    )(positions, line_vectors, burgers, mobility.reshape(1, -1), ghost_map, *others)


def shifted(value, axis, steps):
    count = lax.axis_size(axis)
    return lax.ppermute(value, axis, [(i, (i + steps) % count) for i in range(count)])


def swapped(value, axis):
    count = lax.axis_size(axis)
    return lax.ppermute(value, axis, [(i, i ^ 1) for i in range(count)])


def local(positions, line_vectors, burgers, mobility, close_list, ghost_map):
    subs = ghost_map.shape[0]
    ghosts = ghost_map.shape[1] // 2
    domains = lax.axis_size("dom")
    reach = lax.axis_size("blk") // 4
    state = jnp.concatenate([positions, line_vectors, burgers], 0)
    others = [shifted(state, "blk", s * k) for k in range(1, reach + 1) for s in (1, -1)]
    closes = [close_list] + [shifted(close_list, "dom", -2 * j) for j in range(1, domains // 2)]
    closes += [swapped(c, "dom") for c in closes]
    pack = long_range(positions, line_vectors, burgers, mobility, ghost_map, others)
    packs = [pack] + [shifted(pack, "dom", -2 * j) for j in range(1, domains // 2)]
    packs += [swapped(p, "dom") for p in packs]
    core_of = lambda: lax.rem(lax.axis_index("dom"), 2)
    return tuple(step(packs, closes, subs, ghosts, core_of))


def solution(mesh):
    spread = P(None, ("blk", "dom"))
    return jax.shard_map(
        local,
        mesh=mesh,
        in_specs=(spread, spread, spread, P(("blk", "dom")), spread, spread),
        out_specs=(spread, spread),
        check_vma=False,
    )
```

time: 1030 us -> 96.4 us (0.09)
  local copies, waits for them, and re-layouts: 957 us -> 1.47 us
  Pallas kernels: 0 us -> 61.5 us
  starting transfers between devices: 32.7 us -> 14.9 us
  waiting for transfers between devices: 28 us -> 15.9 us
  other arithmetic: 11.7 us -> 0.77 us
    gather x24 -> x0, local copies, waits for them, and re-layouts: 954 us -> none  [the longest x16 946 us: short_force(): jnp.take(extended_rows, places, axis=1, mode='fill', fill_value=0.0)]
    pallas_call x0 -> x2, Pallas kernels: none -> 61.5 us  [the longest x1 47.6 us: step(): pl.pallas_call(kernel, out_shape=[jax.ShapeDtypeStruct((3, seg), jnp.floa...]
    ppermute x18 -> x16, starting transfers between devices: 32.7 us -> 14.9 us  [the longest x8 13.5 us: shifted(): lax.ppermute(value, axis, [(i, (i + steps) % count) for i in range(count)])]
    ppermute x18 -> x16, waiting for transfers between devices: 28 us -> 15.9 us  [the longest x8 14.8 us: shifted(): lax.ppermute(value, axis, [(i, (i + steps) % count) for i in range(count)])]
  transfers between devices with their start and end apart: 18 -> 16, of which waited for: 8 -> 7; matrix products, arithmetic and copies ran while one was open for 12% -> 0% of each run, Pallas kernels for 0% -> 0%
where the time goes in v1:
time: 96.4 us; the launch traced here: 95.3 us
  Pallas kernels  61.5 us (64%)
  waiting for transfers between devices  15.9 us (16%)
  starting transfers between devices  14.9 us (15%)
  local copies, waits for them, and re-layouts  1.47 us (2%)
    pallas_call x1, Pallas kernels, step(): pl.pallas_call(kernel, out_shape=[jax.ShapeDtypeStruct((3, seg), jnp.floa...  47.6 us
    ppermute x8, waiting for transfers between devices, shifted(): lax.ppermute(value, axis, [(i, (i + steps) % count) for i in range(count)])  14.8 us
    pallas_call x1, Pallas kernels, long_range(): pl.pallas_call(lambda *refs: long_kernel(len(others), seg, *refs), out_sh...  13.9 us
    ppermute x8, starting transfers between devices, shifted(): lax.ppermute(value, axis, [(i, (i + steps) % count) for i in range(count)])  13.5 us
  transfers between devices with their start and end apart: 16, of which 7 were waited for; matrix products, arithmetic and copies ran while one was open for 0% of the time, Pallas kernels for 0%

profile of v1, /device:TPU:0, one launch (start us, length us, event | category | flops | bytes accessed | tf_op | source)
XLA Modules:
  0.0 95.3 jit_solution(8462708574208390275)
XLA Ops:
  0.6 0.8 pad_maximum_fusion
  1.4 0.0 copy-start.1
  1.4 3.9 %collective-permute-start.1 = (f32[9,1024]{1,0:T(8,128)S(1)}, f32[9,1024]{1,0:T(8,128)S(1)}, u32[]{:S(2)}, u32[]{:S(2)}) collective-permute-start(f32[9,1024]{1,0:T(8,128)S(1)} %pad_maximum_fusion), channel_id=1, source_target_pairs={{0,24},{8,0},{16,8},{24,16},{1,25},{9,1},{17,9},{25,17},{2,26},{10... | collective-permute-start | bytes 110600 | tf_op jit(solution)/shard_map/ppermute | solution.py:319
  5.4 0.0 collective-permute-start
  5.4 2.0 %collective-permute-done.1.refs_6_ = f32[9,1024]{1,0:T(8,128)S(1)} collective-permute-done((f32[9,1024]{1,0:T(8,128)S(1)}, f32[9,1024]{1,0:T(8,128)S(1)}, u32[]{:S(2)}, u32[]{:S(2)}) %collective-permute-start.1) | collective-permute-done | bytes 36896 | tf_op jit(solution)/shard_map/ppermute | solution.py:319
  7.4 0.0 copy-start.4
  7.4 3.1 %collective-permute-done.refs_5_ = f32[9,1024]{1,0:T(8,128)S(1)} collective-permute-done((f32[9,1024]{1,0:T(8,128)S(1)}, f32[9,1024]{1,0:T(8,128)S(1)}, u32[]{:S(2)}, u32[]{:S(2)}) %collective-permute-start) | collective-permute-done | bytes 36896 | tf_op jit(solution)/shard_map/ppermute | solution.py:319
  10.5 0.0 copy-start.5
  10.5 0.0 copy-done.4
  10.5 0.6 copy-done.5
  11.2 0.0 copy-start.2
  11.2 0.0 copy-start.3
  11.2 13.9 %long_range.1.refs_0_ = f32[16,1024]{1,0:T(8,128)} custom-call(f32[3,1024]{1,0:T(4,128)} %refs_0_.1, f32[3,1024]{1,0:T(4,128)} %refs_1_.1, f32[3,1024]{1,0:T(4,128)} %refs_2_.1, f32[1,1024]{1,0:T(1,128)} %bitcast.1, s32[4,512]{1,0:T(4,128)} %refs_4_.1, f32[9,1024]{1,0:T(8,128)} %copy-done.5, f32[9,1024]{1,0:T(8,128)} %copy-done.4), custom_call_target="tpu_custom_call" | custom-call | tf_op jit(solution)/shard_map/long_range/pallas_call | solution.py:307
  25.0 0.0 collective-permute-start.5
  25.0 1.6 %collective-permute-start.4 = (f32[16,1024]{1,0:T(8,128)}, f32[16,1024]{1,0:T(8,128)S(1)}, u32[]{:S(2)}, u32[]{:S(2)}) collective-permute-start(f32[16,1024]{1,0:T(8,128)} %long_range.1.refs_0_), channel_id=1, source_target_pairs={{0,2},{1,3},{2,4},{3,5},{4,6},{5,7},{6,0},{7,1},{8,10},{9,11},{10,... | collective-permute-start | bytes 196616 | tf_op jit(solution)/shard_map/ppermute | solution.py:319
  26.6 2.6 %collective-permute-start.3 = (f32[16,1024]{1,0:T(8,128)}, f32[16,1024]{1,0:T(8,128)S(1)}, u32[]{:S(2)}, u32[]{:S(2)}) collective-permute-start(f32[16,1024]{1,0:T(8,128)} %long_range.1.refs_0_), channel_id=1, source_target_pairs={{0,4},{1,5},{2,6},{3,7},{4,0},{5,1},{6,2},{7,3},{8,12},{9,13},{10,... | collective-permute-start | bytes 196616 | tf_op jit(solution)/shard_map/ppermute | solution.py:319
  29.2 0.0 copy-done.1
  29.2 0.2 collective-permute-start.11
  29.4 1.7 %collective-permute-start.10 = (s32[32,1024]{1,0:T(8,128)S(1)}, s32[32,1024]{1,0:T(8,128)S(1)}, u32[]{:S(2)}, u32[]{:S(2)}) collective-permute-start(s32[32,1024]{1,0:T(8,128)S(1)} %copy-done.1), channel_id=1, source_target_pairs={{0,4},{1,5},{2,6},{3,7},{4,0},{5,1},{6,2},{7,3},{8,12},{9,13},{10,... | collective-permute-start | bytes 393224 | tf_op jit(solution)/shard_map/ppermute | solution.py:319
  31.1 0.0 collective-permute-done.5.refs_4_
  31.1 1.9 %collective-permute-start.9 = (s32[32,1024]{1,0:T(8,128)S(1)}, s32[32,1024]{1,0:T(8,128)S(1)}, u32[]{:S(2)}, u32[]{:S(2)}) collective-permute-start(s32[32,1024]{1,0:T(8,128)S(1)} %copy-done.1), channel_id=1, source_target_pairs={{0,6},{1,7},{2,0},{3,1},{4,2},{5,3},{6,4},{7,5},{8,14},{9,15},{10,... | collective-permute-start | bytes 393224 | tf_op jit(solution)/shard_map/ppermute | solution.py:319
  33.0 0.0 collective-permute-done.4.refs_3_
  33.0 1.6 %collective-permute-start.2 = (f32[16,1024]{1,0:T(8,128)}, f32[16,1024]{1,0:T(8,128)S(1)}, u32[]{:S(2)}, u32[]{:S(2)}) collective-permute-start(f32[16,1024]{1,0:T(8,128)} %long_range.1.refs_0_), channel_id=1, source_target_pairs={{0,6},{1,7},{2,0},{3,1},{4,2},{5,3},{6,4},{7,5},{8,14},{9,15},{10,... | collective-permute-start | bytes 196616 | tf_op jit(solution)/shard_map/ppermute | solution.py:319
  34.6 5.4 %collective-permute-done.3.refs_2_ = f32[16,1024]{1,0:T(8,128)S(1)} collective-permute-done((f32[16,1024]{1,0:T(8,128)}, f32[16,1024]{1,0:T(8,128)S(1)}, u32[]{:S(2)}, u32[]{:S(2)}) %collective-permute-start.3) | collective-permute-done | bytes 65568 | tf_op jit(solution)/shard_map/ppermute | solution.py:319
  40.0 0.0 collective-permute-start.12
  40.0 4.2 %collective-permute-done.2.refs_1_ = f32[16,1024]{1,0:T(8,128)S(1)} collective-permute-done((f32[16,1024]{1,0:T(8,128)}, f32[16,1024]{1,0:T(8,128)S(1)}, u32[]{:S(2)}, u32[]{:S(2)}) %collective-permute-start.2) | collective-permute-done | bytes 65568 | tf_op jit(solution)/shard_map/ppermute | solution.py:319
  44.2 0.0 collective-permute-start.8
  44.3 0.0 collective-permute-done.11.refs_11_
  44.3 0.5 collective-permute-start.15
  44.8 0.0 collective-permute-done.10.refs_10_
  44.8 0.1 collective-permute-start.14
  44.8 0.0 collective-permute-done.9.refs_9_
  44.8 0.4 collective-permute-start.13
  45.3 0.0 collective-permute-done.12.refs_12_
  45.3 0.1 collective-permute-start.7
  45.4 0.1 collective-permute-done.8.refs_7_
  45.5 0.3 collective-permute-start.6
  45.8 0.7 collective-permute-done.7.refs_6_
  46.5 0.2 collective-permute-done.6.refs_5_
  46.8 0.0 collective-permute-done.15.refs_15_
  46.8 0.0 collective-permute-done.14.refs_14_
  46.8 0.0 collective-permute-done.13.refs_13_
  46.8 0.0 copy-done.2
  46.8 0.0 copy-done.3
  46.8 0.0 copy-start
  46.8 0.8 copy-done
  47.6 47.6 %step.1 = (f32[3,1024]{1,0:T(4,128)}, f32[3,1024]{1,0:T(4,128)}) custom-call(f32[16,1024]{1,0:T(8,128)S(1)} %copy-done, f32[16,1024]{1,0:T(8,128)S(1)} %collective-permute-done.2.refs_1_, f32[16,1024]{1,0:T(8,128)S(1)} %collective-permute-done.3.refs_2_, f32[16,1024]{1,0:T(8,128)S(1)} %collective-permute-done.4.refs_3_, ...), custom_call_target="tpu_custom_call" | custom-call | tf_op jit(solution)/shard_map/step/pallas_call | solution.py:243
Async XLA Ops:
  1.4 27.8 %copy-start.1 = (s32[32,1024]{1,0:T(8,128)S(1)}, s32[32,1024]{1,0:T(8,128)}, u32[]{:S(2)}) copy-start(s32[32,1024]{1,0:T(8,128)} %refs_8_.1) | copy-start | bytes 393220
  1.4 6.0 %collective-permute-start.1 = (f32[9,1024]{1,0:T(8,128)S(1)}, f32[9,1024]{1,0:T(8,128)S(1)}, u32[]{:S(2)}, u32[]{:S(2)}) collective-permute-start(f32[9,1024]{1,0:T(8,128)S(1)} %pad_maximum_fusion), channel_id=1, source_target_pairs={{0,24},{8,0},{16,8},{24,16},{1,25},{9,1},{17,9},{25,17},{2,26},{10... | collective-permute-start | bytes 110600 | tf_op jit(solution)/shard_map/ppermute | solution.py:319
  5.4 5.2 %collective-permute-start = (f32[9,1024]{1,0:T(8,128)S(1)}, f32[9,1024]{1,0:T(8,128)S(1)}, u32[]{:S(2)}, u32[]{:S(2)}) collective-permute-start(f32[9,1024]{1,0:T(8,128)S(1)} %pad_maximum_fusion), channel_id=1, source_target_pairs={{0,8},{8,16},{16,24},{24,0},{1,9},{9,17},{17,25},{25,1},{2,10},{10... | collective-permute-start | bytes 110600 | tf_op jit(solution)/shard_map/ppermute | solution.py:319
  7.4 3.1 %copy-start.4 = (f32[9,1024]{1,0:T(8,128)}, f32[9,1024]{1,0:T(8,128)S(1)}, u32[]{:S(2)}) copy-start(f32[9,1024]{1,0:T(8,128)S(1)} %collective-permute-done.1.refs_6_) | copy-start | bytes 110596
  10.5 0.6 copy-start.5
  11.2 35.6 %copy-start.2 = (s32[132]{0:T(256)S(1)}, s32[132]{0:T(256)}, u32[]{:S(2)}) copy-start(s32[132]{0:T(256)} %constant.5.clone.refs_17_) | copy-start | bytes 1588
  11.2 35.6 %copy-start.3 = (s32[132]{0:T(256)S(1)}, s32[132]{0:T(256)}, u32[]{:S(2)}) copy-start(s32[132]{0:T(256)} %constant.4.clone.refs_16_) | copy-start | bytes 1588
  25.0 6.1 %collective-permute-start.5 = (f32[16,1024]{1,0:T(8,128)}, f32[16,1024]{1,0:T(8,128)S(1)}, u32[]{:S(2)}, u32[]{:S(2)}) collective-permute-start(f32[16,1024]{1,0:T(8,128)} %long_range.1.refs_0_), channel_id=1, source_target_pairs={{0,1},{1,0},{2,3},{3,2},{4,5},{5,4},{6,7},{7,6},{8,9},{9,8},{10,11... | collective-permute-start | bytes 196616 | tf_op jit(solution)/shard_map/ppermute | solution.py:324
  25.0 8.0 %collective-permute-start.4 = (f32[16,1024]{1,0:T(8,128)}, f32[16,1024]{1,0:T(8,128)S(1)}, u32[]{:S(2)}, u32[]{:S(2)}) collective-permute-start(f32[16,1024]{1,0:T(8,128)} %long_range.1.refs_0_), channel_id=1, source_target_pairs={{0,2},{1,3},{2,4},{3,5},{4,6},{5,7},{6,0},{7,1},{8,10},{9,11},{10,... | collective-permute-start | bytes 196616 | tf_op jit(solution)/shard_map/ppermute | solution.py:319
  26.6 13.4 %collective-permute-start.3 = (f32[16,1024]{1,0:T(8,128)}, f32[16,1024]{1,0:T(8,128)S(1)}, u32[]{:S(2)}, u32[]{:S(2)}) collective-permute-start(f32[16,1024]{1,0:T(8,128)} %long_range.1.refs_0_), channel_id=1, source_target_pairs={{0,4},{1,5},{2,6},{3,7},{4,0},{5,1},{6,2},{7,3},{8,12},{9,13},{10,... | collective-permute-start | bytes 196616 | tf_op jit(solution)/shard_map/ppermute | solution.py:319
  29.2 15.1 %collective-permute-start.11 = (s32[32,1024]{1,0:T(8,128)S(1)}, s32[32,1024]{1,0:T(8,128)S(1)}, u32[]{:S(2)}, u32[]{:S(2)}) collective-permute-start(s32[32,1024]{1,0:T(8,128)S(1)} %copy-done.1), channel_id=1, source_target_pairs={{0,2},{1,3},{2,4},{3,5},{4,6},{5,7},{6,0},{7,1},{8,10},{9,11},{10,... | collective-permute-start | bytes 393224 | tf_op jit(solution)/shard_map/ppermute | solution.py:319
  29.4 15.3 %collective-permute-start.10 = (s32[32,1024]{1,0:T(8,128)S(1)}, s32[32,1024]{1,0:T(8,128)S(1)}, u32[]{:S(2)}, u32[]{:S(2)}) collective-permute-start(s32[32,1024]{1,0:T(8,128)S(1)} %copy-done.1), channel_id=1, source_target_pairs={{0,4},{1,5},{2,6},{3,7},{4,0},{5,1},{6,2},{7,3},{8,12},{9,13},{10,... | collective-permute-start | bytes 393224 | tf_op jit(solution)/shard_map/ppermute | solution.py:319
  31.1 13.7 %collective-permute-start.9 = (s32[32,1024]{1,0:T(8,128)S(1)}, s32[32,1024]{1,0:T(8,128)S(1)}, u32[]{:S(2)}, u32[]{:S(2)}) collective-permute-start(s32[32,1024]{1,0:T(8,128)S(1)} %copy-done.1), channel_id=1, source_target_pairs={{0,6},{1,7},{2,0},{3,1},{4,2},{5,3},{6,4},{7,5},{8,14},{9,15},{10,... | collective-permute-start | bytes 393224 | tf_op jit(solution)/shard_map/ppermute | solution.py:319
  33.0 11.2 %collective-permute-start.2 = (f32[16,1024]{1,0:T(8,128)}, f32[16,1024]{1,0:T(8,128)S(1)}, u32[]{:S(2)}, u32[]{:S(2)}) collective-permute-start(f32[16,1024]{1,0:T(8,128)} %long_range.1.refs_0_), channel_id=1, source_target_pairs={{0,6},{1,7},{2,0},{3,1},{4,2},{5,3},{6,4},{7,5},{8,14},{9,15},{10,... | collective-permute-start | bytes 196616 | tf_op jit(solution)/shard_map/ppermute | solution.py:319
  40.0 5.3 %collective-permute-start.12 = (s32[32,1024]{1,0:T(8,128)S(1)}, s32[32,1024]{1,0:T(8,128)S(1)}, u32[]{:S(2)}, u32[]{:S(2)}) collective-permute-start(s32[32,1024]{1,0:T(8,128)S(1)} %copy-done.1), channel_id=1, source_target_pairs={{0,1},{1,0},{2,3},{3,2},{4,5},{5,4},{6,7},{7,6},{8,9},{9,8},{10,11... | collective-permute-start | bytes 393224 | tf_op jit(solution)/shard_map/ppermute | solution.py:324
  44.2 1.3 %collective-permute-start.8 = (f32[16,1024]{1,0:T(8,128)S(1)}, f32[16,1024]{1,0:T(8,128)S(1)}, u32[]{:S(2)}, u32[]{:S(2)}) collective-permute-start(f32[16,1024]{1,0:T(8,128)S(1)} %collective-permute-done.4.refs_3_), channel_id=1, source_target_pairs={{0,1},{1,0},{2,3},{3,2},{4,5},{5,4},{6,7},{7,6},{8,9},{9,8},{10,11... | collective-permute-start | bytes 196616 | tf_op jit(solution)/shard_map/ppermute | solution.py:324
  44.3 2.5 %collective-permute-start.15 = (s32[32,1024]{1,0:T(8,128)S(1)}, s32[32,1024]{1,0:T(8,128)S(1)}, u32[]{:S(2)}, u32[]{:S(2)}) collective-permute-start(s32[32,1024]{1,0:T(8,128)S(1)} %collective-permute-done.11.refs_11_), channel_id=1, source_target_pairs={{0,1},{1,0},{2,3},{3,2},{4,5},{5,4},{6,7},{7,6},{8,9},{9,8},{10,11... | collective-permute-start | bytes 393224 | tf_op jit(solution)/shard_map/ppermute | solution.py:324
  44.8 2.0 %collective-permute-start.14 = (s32[32,1024]{1,0:T(8,128)S(1)}, s32[32,1024]{1,0:T(8,128)S(1)}, u32[]{:S(2)}, u32[]{:S(2)}) collective-permute-start(s32[32,1024]{1,0:T(8,128)S(1)} %collective-permute-done.10.refs_10_), channel_id=1, source_target_pairs={{0,1},{1,0},{2,3},{3,2},{4,5},{5,4},{6,7},{7,6},{8,9},{9,8},{10,11... | collective-permute-start | bytes 393224 | tf_op jit(solution)/shard_map/ppermute | solution.py:324
  44.8 1.9 %collective-permute-start.13 = (s32[32,1024]{1,0:T(8,128)S(1)}, s32[32,1024]{1,0:T(8,128)S(1)}, u32[]{:S(2)}, u32[]{:S(2)}) collective-permute-start(s32[32,1024]{1,0:T(8,128)S(1)} %collective-permute-done.9.refs_9_), channel_id=1, source_target_pairs={{0,1},{1,0},{2,3},{3,2},{4,5},{5,4},{6,7},{7,6},{8,9},{9,8},{10,11... | collective-permute-start | bytes 393224 | tf_op jit(solution)/shard_map/ppermute | solution.py:324
  45.3 1.3 %collective-permute-start.7 = (f32[16,1024]{1,0:T(8,128)S(1)}, f32[16,1024]{1,0:T(8,128)S(1)}, u32[]{:S(2)}, u32[]{:S(2)}) collective-permute-start(f32[16,1024]{1,0:T(8,128)S(1)} %collective-permute-done.3.refs_2_), channel_id=1, source_target_pairs={{0,1},{1,0},{2,3},{3,2},{4,5},{5,4},{6,7},{7,6},{8,9},{9,8},{10,11... | collective-permute-start | bytes 196616 | tf_op jit(solution)/shard_map/ppermute | solution.py:324
  45.5 1.3 %collective-permute-start.6 = (f32[16,1024]{1,0:T(8,128)S(1)}, f32[16,1024]{1,0:T(8,128)S(1)}, u32[]{:S(2)}, u32[]{:S(2)}) collective-permute-start(f32[16,1024]{1,0:T(8,128)S(1)} %collective-permute-done.2.refs_1_), channel_id=1, source_target_pairs={{0,1},{1,0},{2,3},{3,2},{4,5},{5,4},{6,7},{7,6},{8,9},{9,8},{10,11... | collective-permute-start | bytes 196616 | tf_op jit(solution)/shard_map/ppermute | solution.py:324
  46.8 0.8 copy-start

commit v2 on v1

v2 whole, which is shorter than its diff:
```python
import math

import jax
import jax.numpy as jnp
from jax import lax
from jax.experimental import pallas as pl
from jax.experimental.pallas import tpu as pltpu
from jax.sharding import PartitionSpec as P

LANES = 128
ROWS = 8
long_core = 1.0
short_core = 0.25
time_step = 0.05


def lane_gather(row_block, places):
    return jnp.take_along_axis(row_block, places, axis=1, mode="promise_in_bounds")


def level_halves(domains, evals):
    levels = [{(0, 0), (0, 1)}]
    for _ in range(evals - 1):
        last = levels[-1]
        grown = set(last)
        for domain in {d for d, _ in last}:
            grown.add(((domain - 1) % domains, 1))
            grown.add(((domain + 1) % domains, 0))
        levels.append(grown)
    return [sorted(level) for level in levels[::-1]]


WEIGHT_VMEM = 24
STEP_VMEM = 24

def fetch(refs, held, me, sem):
    half = len(refs) // 2
    copies = []
    for j in range(half):
        for other in range(2):
            at = other * half + j
            copies.append(pltpu.make_async_copy(refs[at], held.at[me ^ (2 * j + other)], sem.at[at]))
    for copy in copies:
        copy.start()
    for copy in copies:
        copy.wait()


def weights_kernel(domains, slots, subs, plan, own_index, *refs):
    block_refs = refs[:domains]
    dom_table, half_table = refs[domains : domains + 2]
    weight, close, gplaces, pack, still_rows, still, sem = refs[domains + 2 :]
    seg = pack.shape[2]
    cells = seg // LANES
    groups = slots // ROWS
    half_cells = cells // 2
    half_lanes = half_cells * LANES
    ghosts = seg // (2 * (subs // 2))
    me = own_index()
    scale = 1.0 / math.sqrt(slots)
    LINE, BURG, GHOST = slots, slots + 3, slots + 6
    fetch(block_refs, pack, me, sem)

    row = lax.broadcasted_iota(jnp.int32, (ROWS, LANES), 0)
    x_rows = row < 2
    y_rows = row < 4

    even_row = lax.rem(row, 2) == 0

    def bcast(ref, index, at, lane):
        return jnp.broadcast_to(ref[*index, at : at + 1, pl.ds(lane, LANES)], (ROWS, LANES))

    def spread(ref, d, at, lane):
        x, y, z = (bcast(ref, (d,), at + c, lane) for c in range(3))
        return jnp.where(x_rows, x, jnp.where(y_rows, y, z))

    def expand(d, carry):
        for q in range(cells):
            here = pl.ds(q * LANES, LANES)
            for at, slot in ((LINE, 0), (BURG, 1)):
                still_rows[slot, d, :, here] = spread(pack, d, at, q * LANES)
        for sub in range(subs):
            for side in range(2):
                lane = (sub % 2) * 2 * ghosts + side * ghosts
                at = GHOST + sub // 2
                place = jnp.where(even_row, bcast(pack, (d,), at, lane), bcast(pack, (d,), at, lane + LANES))
                gplaces[d, :, pl.ds((2 * sub + side) * LANES, LANES)] = place.astype(jnp.int32)
        return carry

    lax.fori_loop(0, domains, expand, 0)

    def domain_at(i):
        return lax.rem(dom_table[i] + me, domains)

    def owner_picks(i, count, sub, sources):
        made = []
        for u in range(count):
            d = domain_at(i + u)
            for side in range(2):
                place = gplaces[d, :, pl.ds(pl.multiple_of((2 * sub + side) * LANES, LANES), LANES)]
                lane = place & (LANES - 1)
                cell = place >> 7
                to = lax.rem(d + (1 if side else domains - 1), domains)
                for source, ref, slot in sources:
                    out = None
                    for k in range(half_cells):
                        got = lane_gather(source[d, :, pl.ds(side * half_lanes + k * LANES, LANES)], lane)
                        out = got if out is None else jnp.where(cell == side * half_cells + k, got, out)
                    made.append((ref, slot, to, 1 - side, out))
        for ref, slot, to, at, out in made:
            ref[*slot, to, at] = out

    def over(span, body):
        start, steps, count = span
        if steps == 1:
            body(start, count)
            return
        def one(i, carry):
            body(start + i * count, count)
            return carry
        lax.fori_loop(0, steps, one, 0)

    def items(i, count):
        for u in range(count):
            d = domain_at(i + u)
            for k in range(half_cells):
                yield d, pl.multiple_of(half_table[i + u] * half_lanes + k * LANES, LANES), k

    def dots(mine, theirs):
        return mine[0] * theirs[0] + mine[1] * theirs[1] + mine[2] * theirs[2]

    def pair_weight(mine, source, places):
        theirs = [lane_gather(m, places) for m in source]
        return dots(mine[:3], theirs[:3]) * dots(mine[3:], theirs[3:]) * scale

    def ghost_rows(ref, slot, d, k):
        side, pair = divmod(k, 2)
        return [bcast(ref, (*slot, d, side), 2 * c + pair, 0) for c in range(3)]

    def blocks(d, lane):
        for g in range(groups):
            yield (d, slice(g * ROWS, (g + 1) * ROWS), pl.ds(lane, LANES))

    def weights(i, count, upto):
        made = []
        for d, lane, k in items(i, count):
            mine = [bcast(pack, (d,), LINE + c, lane) for c in range(6)]
            far = [ghost_rows(still, (sub, 0), d, k) + ghost_rows(still, (sub, 1), d, k) for sub in range(upto)]
            for at in blocks(d, lane):
                entry = pack[at].astype(jnp.int32)
                places = entry & (LANES - 1)
                near, held = entry < LANES, entry < 2 * LANES
                near_w = pair_weight(mine, mine, places)
                made.append((close.at[at], entry))
                for sub in range(upto):
                    made.append((weight.at[(sub, *at)], jnp.where(near, near_w, jnp.where(held, pair_weight(mine, far[sub], places), 0.0))))
        for ref, value in made:
            ref[...] = value

    for sub in range(subs):
        over(plan["still"][sub], lambda i, count: owner_picks(i, count, sub, ((still_rows.at[0], still, (sub, 0)), (still_rows.at[1], still, (sub, 1)))))
    for upto, span in plan["weights"]:
        over(span, lambda i, count: weights(i, count, upto))


def step_kernel(domains, slots, subs, plan, own_index, *refs):
    now_refs = refs[:domains]
    weight, close, gplaces, dom_table, half_table = refs[domains : domains + 5]
    out_pos, out_vel = refs[domains + 5 : domains + 7]
    now, state, vels, long_, ghost, sem = refs[domains + 7 :]
    seg = now.shape[2]
    evals = vels.shape[0]
    cells = seg // LANES
    groups = slots // ROWS
    half_cells = cells // 2
    half_lanes = half_cells * LANES
    me = own_index()
    POS, MOB, FAR = 0, 3, 4
    fetch(now_refs, now, me, sem)

    row = lax.broadcasted_iota(jnp.int32, (ROWS, LANES), 0)
    x_rows = row < 2
    y_rows = row < 4

    def bcast(ref, index, at, lane):
        return jnp.broadcast_to(ref[*index, at : at + 1, pl.ds(lane, LANES)], (ROWS, LANES))

    def spread(d, at, lane):
        x, y, z = (bcast(now, (d,), at + c, lane) for c in range(3))
        return jnp.where(x_rows, x, jnp.where(y_rows, y, z))

    def expand(d, carry):
        for q in range(cells):
            here = pl.ds(q * LANES, LANES)
            state[0, d, :, here] = spread(d, POS, q * LANES)
            long_[d, :, here] = spread(d, FAR, q * LANES)
        return carry

    lax.fori_loop(0, domains, expand, 0)

    def domain_at(i):
        return lax.rem(dom_table[i] + me, domains)

    def owner_picks(i, count, sub, sources):
        made = []
        for u in range(count):
            d = domain_at(i + u)
            for side in range(2):
                place = gplaces[d, :, pl.ds(pl.multiple_of((2 * sub + side) * LANES, LANES), LANES)]
                lane = place & (LANES - 1)
                cell = place >> 7
                to = lax.rem(d + (1 if side else domains - 1), domains)
                for source, ref, slot in sources:
                    out = None
                    for k in range(half_cells):
                        got = lane_gather(source[d, :, pl.ds(side * half_lanes + k * LANES, LANES)], lane)
                        out = got if out is None else jnp.where(cell == side * half_cells + k, got, out)
                    made.append((ref, slot, to, 1 - side, out))
        for ref, slot, to, at, out in made:
            ref[*slot, to, at] = out

    def over(span, body):
        start, steps, count = span
        if steps == 1:
            body(start, count)
            return
        def one(i, carry):
            body(start + i * count, count)
            return carry
        lax.fori_loop(0, steps, one, 0)

    def items(i, count):
        for u in range(count):
            d = domain_at(i + u)
            for k in range(half_cells):
                yield d, pl.multiple_of(half_table[i + u] * half_lanes + k * LANES, LANES), k

    def ghost_rows(ref, slot, d, k):
        side, pair = divmod(k, 2)
        return [bcast(ref, (*slot, d, side), 2 * c + pair, 0) for c in range(3)]

    def blocks(d, lane):
        for g in range(groups):
            yield (d, slice(g * ROWS, (g + 1) * ROWS), pl.ds(lane, LANES))

    def total(block):
        for shift in (4, 2, 1):
            block = block + pltpu.roll(block, shift, 0)
        return block

    def force(level, sub, d, lane, k):
        mine = [bcast(state, (level, d), 2 * c, lane) for c in range(3)]
        far = ghost_rows(ghost, (), d, k)
        sums = [None] * 3
        for at in blocks(d, lane):
            entry = close[at]
            places = entry & (LANES - 1)
            near = entry < LANES
            delta = [m - jnp.where(near, lane_gather(m, places), lane_gather(f, places)) for m, f in zip(mine, far)]
            radius = delta[0] * delta[0] + delta[1] * delta[1] + delta[2] * delta[2] + short_core * short_core
            inverse = lax.rsqrt(radius)
            w = weight[(sub, *at)] * (inverse * inverse * inverse)
            for c in range(3):
                term = w * delta[c]
                sums[c] = term if sums[c] is None else sums[c] + term
        sums = [total(s) for s in sums]
        return jnp.where(x_rows, sums[0], jnp.where(y_rows, sums[1], sums[2]))

    def evaluate(level, owners, halves):
        sub = level // 2
        stage = lax.rem(level, 2)
        base = level - stage
        over(owners, lambda i, count: owner_picks(i, count, sub, ((state.at[level], ghost, ()),)))

        def one(i, count):
            made = []
            for d, lane, k in items(i, count):
                here = pl.ds(lane, LANES)
                vel = bcast(now, (d,), MOB, lane) * (long_[d, :, here] + force(level, sub, d, lane, k))
                vel = jnp.where(stage == 1, 0.5 * (vels[base, d, :, here] + vel), vel)
                made.append((d, here, vel, state[base, d, :, here] + time_step * vel))
            for d, here, vel, moved in made:
                vels[level, d, :, here] = vel
                state[level + 1, d, :, here] = moved

        over(halves, one)

    for first, last, owners, halves in plan["levels"]:
        if last - first == 1:
            evaluate(jnp.int32(first), owners, halves)
        else:
            lax.fori_loop(first, last, lambda level, carry: (evaluate(level, owners, halves), carry)[1], 0)

    for c in range(3):
        out_pos[c : c + 1, :] = state[evals, me, 2 * c : 2 * c + 1, :]
        out_vel[c : c + 1, :] = vels[evals - 1, me, 2 * c : 2 * c + 1, :]


class Plan:
    def __init__(self):
        self.domains, self.halves = [], []

    def span(self, entries, limit):
        count = min(range(1, limit + 1), key=lambda c: (-(-len(entries) // c) * (c + 0.5), c))
        start, steps = len(self.domains), -(-len(entries) // count)
        entries = entries + [entries[-1]] * (steps * count - len(entries))
        self.domains.extend(d for d, _ in entries)
        self.halves.extend(h for _, h in entries)
        return start, steps, count

    def tables(self):
        return jnp.array(self.domains, jnp.int32), jnp.array(self.halves, jnp.int32)


def owners_of(level, domains):
    return sorted({((d + s) % domains, 0) for d, _ in level for s in (1, -1)})


TABLE = pl.BlockSpec(memory_space=pltpu.SMEM)
ANYWHERE = pl.BlockSpec(memory_space=pl.ANY)
VMEM = pl.BlockSpec(memory_space=pltpu.VMEM)


def pair_weights(blocks, slots, subs, own_index, most=2, most_owners=4):
    domains = len(blocks)
    rows, seg = blocks[0].shape
    levels = level_halves(domains, 2 * subs)
    table = Plan()
    plan = {"still": [table.span(owners_of(levels[2 * t], domains), most_owners) for t in range(subs)], "weights": []}
    for upto in range(1, subs + 1):
        after = levels[2 * upto] if upto < subs else []
        only = [h for h in levels[2 * upto - 2] if h not in after]
        if only:
            plan["weights"].append((upto, table.span(only, most)))

    def kernel(*refs):
        weights_kernel(domains, slots, subs, plan, own_index, *refs)

    return pl.pallas_call(
        kernel,
        out_shape=[
            jax.ShapeDtypeStruct((subs, domains, slots, seg), jnp.float32),
            jax.ShapeDtypeStruct((domains, slots, seg), jnp.int32),
            jax.ShapeDtypeStruct((domains, ROWS, seg), jnp.int32),
        ],
        in_specs=[ANYWHERE] * domains + [TABLE] * 2,
        out_specs=[VMEM] * 3,
        scratch_shapes=[
            pltpu.VMEM((domains, rows, seg), jnp.float32),
            pltpu.VMEM((2, domains, ROWS, seg), jnp.float32),
            pltpu.VMEM((subs, 2, domains, 2, ROWS, LANES), jnp.float32),
            pltpu.SemaphoreType.DMA((domains,)),
        ],
        compiler_params=pltpu.CompilerParams(vmem_limit_bytes=WEIGHT_VMEM * 2**20),
        cost_estimate=pl.CostEstimate(flops=10**7, bytes_accessed=4 * 10**7, transcendentals=0),
        name="weights",
    )(*blocks, *table.tables())


def step(now, weights, subs, own_index, most=8, most_owners=8):
    domains = len(now)
    rows, seg = now[0].shape
    slots = weights[0].shape[2]
    levels = level_halves(domains, 2 * subs)
    table = Plan()
    plan = {"levels": []}
    first = 0
    while first < len(levels):
        last = first + 1
        while last < len(levels) and levels[last] == levels[first]:
            last += 1
        plan["levels"].append((first, last, table.span(owners_of(levels[first], domains), most_owners), table.span(levels[first], most)))
        first = last

    def kernel(*refs):
        step_kernel(domains, slots, subs, plan, own_index, *refs)

    return pl.pallas_call(
        kernel,
        out_shape=[jax.ShapeDtypeStruct((3, seg), jnp.float32)] * 2,
        in_specs=[ANYWHERE] * domains + [VMEM] * 3 + [TABLE] * 2,
        out_specs=[VMEM] * 2,
        scratch_shapes=[
            pltpu.VMEM((domains, rows, seg), jnp.float32),
            pltpu.VMEM((2 * subs + 1, domains, ROWS, seg), jnp.float32),
            pltpu.VMEM((2 * subs, domains, ROWS, seg), jnp.float32),
            pltpu.VMEM((domains, ROWS, seg), jnp.float32),
            pltpu.VMEM((domains, 2, ROWS, LANES), jnp.float32),
            pltpu.SemaphoreType.DMA((domains,)),
        ],
        compiler_params=pltpu.CompilerParams(vmem_limit_bytes=STEP_VMEM * 2**20),
        cost_estimate=pl.CostEstimate(flops=10**7, bytes_accessed=6 * 10**7, transcendentals=10**6),
        name="step",
    )(*now, *weights, *table.tables())


def long_kernel(sources, seg, *refs):
    own, mob = refs[:3], refs[3]
    others = refs[4 : 4 + sources]
    out, tiles = refs[4 + sources :]
    cells = seg // LANES
    unroll = 16
    scale = 1.0 / math.sqrt((sources + 1) * LANES)
    for s in range(sources + 1):
        for c in range(9):
            for q in range(cells):
                src = own[c // 3][c % 3 : c % 3 + 1, q * LANES : (q + 1) * LANES] if s == 0 else others[s - 1][c : c + 1, q * LANES : (q + 1) * LANES]
                tiles[s * 9 + c, q : q + 1, :] = src
    mine = [tiles[c] for c in range(9)]

    def one(i, forces):
        forces = list(forces)
        for s in range(sources + 1):
            for u in range(unroll):
                other = [pltpu.roll(tiles[s * 9 + c], i * unroll + u, 1) for c in range(9)]
                delta = [mine[c] - other[c] for c in range(3)]
                radius = delta[0] * delta[0] + delta[1] * delta[1] + delta[2] * delta[2] + long_core * long_core
                inverse = lax.rsqrt(radius)
                line = mine[3] * other[3] + mine[4] * other[4] + mine[5] * other[5]
                burg = mine[6] * other[6] + mine[7] * other[7] + mine[8] * other[8]
                w = burg * line * (inverse * inverse * inverse)
                for c in range(3):
                    forces[c] = forces[c] + w * delta[c]
        return tuple(forces)

    out[0:3, :] = own[0][...]
    out[3:4, :] = mob[...]
    zero = jnp.zeros_like(mine[0])
    forces = lax.fori_loop(0, LANES // unroll, one, (zero,) * 3)
    for c in range(3):
        for q in range(cells):
            out[4 + c : 5 + c, q * LANES : (q + 1) * LANES] = forces[c][q : q + 1, :] * scale


def long_range(positions, line_vectors, burgers, mobility, others):
    seg = positions.shape[1]
    return pl.pallas_call(
        lambda *refs: long_kernel(len(others), seg, *refs),
        out_shape=jax.ShapeDtypeStruct((ROWS, seg), jnp.float32),
        in_specs=[pl.BlockSpec(memory_space=pltpu.VMEM)] * (4 + len(others)),
        out_specs=pl.BlockSpec(memory_space=pltpu.VMEM),
        scratch_shapes=[pltpu.VMEM((9 * (len(others) + 1), seg // LANES, LANES), jnp.float32)],
        cost_estimate=pl.CostEstimate(flops=10**7, bytes_accessed=2 * 10**7, transcendentals=10**6),
        name="long_range",
    )(positions, line_vectors, burgers, mobility[None], *others)


def shifted(value, axis, steps):
    count = lax.axis_size(axis)
    return lax.ppermute(value, axis, [(i, (i + steps) % count) for i in range(count)])


def matched(value, axis, step):
    count = lax.axis_size(axis)
    return lax.ppermute(value, axis, [(i, i ^ step) for i in range(count)])


def cycle_neighbours(value, axis):
    count = lax.axis_size(axis)
    got = [matched(value, axis, 1), lax.ppermute(value, axis, [(i, (((i - 1) % count) ^ 1) + 1 if ((i - 1) % count) ^ 1 != count - 1 else 0) for i in range(count)])]
    for k in range(2, count // 4 + 1):
        got += [shifted(value, axis, k), shifted(value, axis, -k)]
    return got


def along_chips(value):
    return [value] + [matched(value, "dom", 2 * j) for j in range(1, lax.axis_size("dom") // 2)]


def local(positions, line_vectors, burgers, mobility, close_list, ghost_map):
    slots, seg = close_list.shape
    subs = ghost_map.shape[0]
    own_index = lambda: lax.axis_index("dom")
    state = jnp.concatenate([positions, line_vectors, burgers], 0)
    others = cycle_neighbours(state, "blk")
    block = jnp.concatenate([close_list.astype(jnp.float32), line_vectors, burgers, ghost_map.astype(jnp.float32).reshape(-1, seg)], 0)
    blocks = along_chips(block)
    now = long_range(positions, line_vectors, burgers, mobility, others)
    blocks, now = lax.optimization_barrier((blocks, now))
    nows = along_chips(now)
    blocks = blocks + [matched(b, "dom", 1) for b in blocks]
    weights = pair_weights(blocks, slots, subs, own_index)
    nows, weights = lax.optimization_barrier((nows, weights))
    nows = nows + [matched(n, "dom", 1) for n in nows]
    return tuple(step(nows, weights, subs, own_index))


def solution(mesh):
    spread = P(None, ("blk", "dom"))
    return jax.shard_map(
        local,
        mesh=mesh,
        in_specs=(spread, spread, spread, P(("blk", "dom")), spread, spread),
        out_specs=(spread, spread),
        check_vma=False,
    )
```

time: 96.4 us -> 63.9 us (0.66)
  Pallas kernels: 61.5 us -> 35.3 us
  waiting for transfers between devices: 15.9 us -> 4.56 us
  local copies, waits for them, and re-layouts: 1.47 us -> 4.01 us
  other arithmetic: 0.77 us -> 3.14 us
    pallas_call x1, Pallas kernels: 47.6 us -> 17.9 us  [step(): pl.pallas_call(kernel, out_shape=[jax.ShapeDtypeStruct((3, seg), jnp.floa...]
    pallas_call x0 -> x1, Pallas kernels: none -> 11.5 us  [pair_weights(): pl.pallas_call(kernel, out_shape=[jax.ShapeDtypeStruct((subs, domains, sl...]
    ppermute x16, waiting for transfers between devices: 15.9 us -> 4.56 us  [the longest x1 2.3 us: cycle_neighbours(): lax.ppermute(value, axis, [(i, ((i - 1) % count ^ 1) + 1 if (i - 1) % cou...]
    pallas_call x1, Pallas kernels: 13.9 us -> 5.88 us  [long_range(): pl.pallas_call(lambda *refs: long_kernel(len(others), seg, *refs), out_sh...]
    unnamed x12 -> x14, local copies, waits for them, and re-layouts: 1.47 us -> 3.99 us
    convert_element_type x0 -> x2, other arithmetic: none -> 1.62 us  [the longest x1 0.92 us: local(): close_list.astype(jnp.float32)]
  transfers between devices with their start and end apart: 16 -> 16, of which waited for: 7 -> 5; matrix products, arithmetic and copies ran while one was open for 0% -> 1% of each run, Pallas kernels for 0% -> 28%
where the time goes in v2:
time: 63.9 us; the launch traced here: 63.2 us
  Pallas kernels  35.3 us (55%)
  starting transfers between devices  15.5 us (24%)
  waiting for transfers between devices  4.56 us (7%)
  local copies, waits for them, and re-layouts  4.01 us (6%)
  other arithmetic  3.14 us (5%)
  between operations  0.72 us (1%)
    pallas_call x1, Pallas kernels, step(): pl.pallas_call(kernel, out_shape=[jax.ShapeDtypeStruct((3, seg), jnp.floa...  17.9 us
    ppermute x15, starting transfers between devices, matched(): return lax.ppermute(value, axis, [(i, i ^ step) for i in range(count)])  14 us
    pallas_call x1, Pallas kernels, pair_weights(): pl.pallas_call(kernel, out_shape=[jax.ShapeDtypeStruct((subs, domains, sl...  11.5 us
    pallas_call x1, Pallas kernels, long_range(): pl.pallas_call(lambda *refs: long_kernel(len(others), seg, *refs), out_sh...  5.88 us
    unnamed x14, local copies, waits for them, and re-layouts  3.99 us
    ppermute x1, waiting for transfers between devices, cycle_neighbours(): lax.ppermute(value, axis, [(i, ((i - 1) % count ^ 1) + 1 if (i - 1) % cou...  2.3 us
    ppermute x15, waiting for transfers between devices, matched(): return lax.ppermute(value, axis, [(i, i ^ step) for i in range(count)])  2.25 us
    ppermute x1, starting transfers between devices, cycle_neighbours(): lax.ppermute(value, axis, [(i, ((i - 1) % count ^ 1) + 1 if (i - 1) % cou...  1.49 us
  transfers between devices with their start and end apart: 16, of which 5 were waited for; matrix products, arithmetic and copies ran while one was open for 1% of the time, Pallas kernels for 28%

profile of v2, /device:TPU:0, one launch (start us, length us, event | category | flops | bytes accessed | tf_op | source)
XLA Modules:
  0.0 63.2 jit_solution(17255097778601217051)
XLA Ops:
  0.6 0.9 %convert_element_type.6 = f32[32,1024]{1,0:T(8,128)S(1)} convert(s32[32,1024]{1,0:T(8,128)} %param.14) | non-fusion elementwise | flops 32768 | bytes 262144 | tf_op jit(solution)/shard_map/convert_element_type | solution.py:476
  1.5 0.7 %convert_element_type.7 = f32[4,512]{1,0:T(4,128)S(1)} convert(s32[4,512]{1,0:T(4,128)} %param.15) | non-fusion elementwise | flops 2048 | bytes 16384 | tf_op jit(solution)/shard_map/convert_element_type | solution.py:476
  2.3 0.8 %pad_maximum_fusion.refs_0_ = f32[40,1024]{1,0:T(8,128)S(1)} fusion(f32[2,1024]{1,0:T(2,128)S(1)} %reshape.7, f32[3,1024]{1,0:T(4,128)} %refs_2_.1, f32[3,1024]{1,0:T(4,128)} %refs_1_.1, f32[32,1024]{1,0:T(8,128)S(1)} %convert_element_type.6), kind=kLoop, calls=%fused_computation | loop fusion | flops 122880 | bytes 327680 | tf_op jit(solution)/shard_map/concatenate | solution.py:476
  3.0 3.1 %collective-permute-start = (f32[40,1024]{1,0:T(8,128)S(1)}, f32[40,1024]{1,0:T(8,128)S(1)}, u32[]{:S(2)}, u32[]{:S(2)}) collective-permute-start(f32[40,1024]{1,0:T(8,128)S(1)} %pad_maximum_fusion.refs_0_), channel_id=1, source_target_pairs={{0,2},{1,3},{2,0},{3,1},{4,6},{5,7},{6,4},{7,5},{8,10},{9,11},{10,... | collective-permute-start | bytes 491528 | tf_op jit(solution)/shard_map/ppermute | solution.py:455
  6.1 2.6 %collective-permute-start.1 = (f32[40,1024]{1,0:T(8,128)S(1)}, f32[40,1024]{1,0:T(8,128)S(1)}, u32[]{:S(2)}, u32[]{:S(2)}) collective-permute-start(f32[40,1024]{1,0:T(8,128)S(1)} %pad_maximum_fusion.refs_0_), channel_id=1, source_target_pairs={{0,4},{1,5},{2,6},{3,7},{4,0},{5,1},{6,2},{7,3},{8,12},{9,13},{10,... | collective-permute-start | bytes 491528 | tf_op jit(solution)/shard_map/ppermute | solution.py:455
  8.7 0.0 collective-permute-start.2
  8.7 0.8 %pad_maximum_fusion.1 = f32[9,1024]{1,0:T(8,128)S(1)} fusion(f32[3,1024]{1,0:T(4,128)} %refs_2_.1, f32[3,1024]{1,0:T(4,128)} %refs_1_.1, f32[3,1024]{1,0:T(4,128)} %refs_0_.1), kind=kLoop, calls=%fused_computation.1 | loop fusion | flops 18432 | bytes 73728 | tf_op jit(solution)/shard_map/concatenate | solution.py:474
  9.5 1.8 %collective-permute-start.3 = (f32[9,1024]{1,0:T(8,128)S(1)}, f32[9,1024]{1,0:T(8,128)S(1)}, u32[]{:S(2)}, u32[]{:S(2)}) collective-permute-start(f32[9,1024]{1,0:T(8,128)S(1)} %pad_maximum_fusion.1), channel_id=1, source_target_pairs={{0,8},{8,0},{16,24},{24,16},{1,9},{9,1},{17,25},{25,17},{2,10},{10... | collective-permute-start | bytes 110600 | tf_op jit(solution)/shard_map/ppermute | solution.py:455
  11.3 1.5 %collective-permute-start.4 = (f32[9,1024]{1,0:T(8,128)S(1)}, f32[9,1024]{1,0:T(8,128)S(1)}, u32[]{:S(2)}, u32[]{:S(2)}) collective-permute-start(f32[9,1024]{1,0:T(8,128)S(1)} %pad_maximum_fusion.1), channel_id=1, source_target_pairs={{0,24},{8,16},{16,8},{24,0},{1,25},{9,17},{17,9},{25,1},{2,26},{10... | collective-permute-start | bytes 110600 | tf_op jit(solution)/shard_map/ppermute | solution.py:460
  12.8 1.4 %collective-permute-done.3.refs_4_ = f32[9,1024]{1,0:T(8,128)S(1)} collective-permute-done((f32[9,1024]{1,0:T(8,128)S(1)}, f32[9,1024]{1,0:T(8,128)S(1)}, u32[]{:S(2)}, u32[]{:S(2)}) %collective-permute-start.3) | collective-permute-done | bytes 36896 | tf_op jit(solution)/shard_map/ppermute | solution.py:455
  14.1 0.0 copy-start.5
  14.1 2.3 %collective-permute-done.4.refs_5_ = f32[9,1024]{1,0:T(8,128)S(1)} collective-permute-done((f32[9,1024]{1,0:T(8,128)S(1)}, f32[9,1024]{1,0:T(8,128)S(1)}, u32[]{:S(2)}, u32[]{:S(2)}) %collective-permute-start.4) | collective-permute-done | bytes 36896 | tf_op jit(solution)/shard_map/ppermute | solution.py:460
  16.4 0.0 copy-start.6
  16.4 0.0 copy-done.5
  16.4 0.6 copy-done.6
  17.0 5.9 %long_range.1.refs_0_ = f32[8,1024]{1,0:T(8,128)} custom-call(f32[3,1024]{1,0:T(4,128)} %refs_0_.1, f32[3,1024]{1,0:T(4,128)} %refs_1_.1, f32[3,1024]{1,0:T(4,128)} %refs_2_.1, f32[1,1024]{1,0:T(1,128)} %bitcast.1, f32[9,1024]{1,0:T(8,128)} %copy-done.5, f32[9,1024]{1,0:T(8,128)} %copy-done.6), custom_call_target="tpu_custom_call" | custom-call | flops 10000000 | bytes 20000000 | tf_op jit(solution)/shard_map/long_range/pallas_call | solution.py:437
  22.9 0.0 collective-permute-done.refs_1_
  22.9 0.0 collective-permute-done.1.refs_2_
  22.9 0.0 collective-permute-done.2.refs_3_
  22.9 0.1 collective-permute-start.10
  23.0 0.5 collective-permute-start.11
  23.5 0.1 collective-permute-start.8
  23.6 0.4 collective-permute-start.9
  24.0 0.8 %collective-permute-start.5 = (f32[8,1024]{1,0:T(8,128)}, f32[8,1024]{1,0:T(8,128)S(1)}, u32[]{:S(2)}, u32[]{:S(2)}) collective-permute-start(f32[8,1024]{1,0:T(8,128)} %long_range.1.refs_0_), channel_id=1, source_target_pairs={{0,2},{1,3},{2,0},{3,1},{4,6},{5,7},{6,4},{7,5},{8,10},{9,11},{10,... | collective-permute-start | bytes 98312 | tf_op jit(solution)/shard_map/ppermute | solution.py:455
  24.8 0.0 collective-permute-done.10.refs_6_
  24.8 3.3 %collective-permute-start.6 = (f32[8,1024]{1,0:T(8,128)}, f32[8,1024]{1,0:T(8,128)S(1)}, u32[]{:S(2)}, u32[]{:S(2)}) collective-permute-start(f32[8,1024]{1,0:T(8,128)} %long_range.1.refs_0_), channel_id=1, source_target_pairs={{0,4},{1,5},{2,6},{3,7},{4,0},{5,1},{6,2},{7,3},{8,12},{9,13},{10,... | collective-permute-start | bytes 98312 | tf_op jit(solution)/shard_map/ppermute | solution.py:455
  28.2 0.0 collective-permute-done.11.refs_7_
  28.2 0.2 collective-permute-start.7
  28.4 0.0 collective-permute-done.8.refs_4_
  28.4 0.0 collective-permute-done.9.refs_5_
  28.4 0.7 %copy-done.3 = s32[46]{0:T(128)S(1)} copy-done((s32[46]{0:T(128)S(1)}, s32[46]{0:T(128)}, u32[]{:S(2)}) %copy-start.3) | copy-done | bytes 208
  29.1 0.7 %copy-done.4 = s32[46]{0:T(128)S(1)} copy-done((s32[46]{0:T(128)S(1)}, s32[46]{0:T(128)}, u32[]{:S(2)}) %copy-start.4) | copy-done | bytes 208
  29.7 11.5 %weights.1 = (f32[4,8,32,1024]{3,2,1,0:T(8,128)S(1)}, s32[8,32,1024]{2,1,0:T(8,128)S(1)}, s32[8,8,1024]{2,1,0:T(8,128)S(1)}) custom-call(f32[40,1024]{1,0:T(8,128)S(1)} %pad_maximum_fusion.refs_0_, f32[40,1024]{1,0:T(8,128)S(1)} %collective-permute-done.refs_1_, f32[40,1024]{1,0:T(8,128)S(1)} %collective-permute-done.1.refs_2_, ...), custom_call_target="tpu_custom_call" | custom-call | flops 10000000 | bytes 40000000 | tf_op jit(solution)/shard_map/weights/pallas_call | solution.py:339
  41.3 0.0 collective-permute-done.5.refs_1_
  41.3 0.0 collective-permute-done.6.refs_2_
  41.3 0.0 collective-permute-done.7.refs_3_
  41.3 0.1 collective-permute-start.12
  41.4 0.5 collective-permute-start.13
  41.9 0.1 collective-permute-start.14
  41.9 0.4 collective-permute-start.15
  42.4 0.4 collective-permute-done.12.refs_4_
  42.8 0.0 collective-permute-done.13.refs_5_
  42.8 0.3 collective-permute-done.14.refs_6_
  43.1 0.2 collective-permute-done.15.refs_7_
  43.2 0.8 %copy-done = f32[8,1024]{1,0:T(8,128)S(1)} copy-done((f32[8,1024]{1,0:T(8,128)S(1)}, f32[8,1024]{1,0:T(8,128)}, u32[]{:S(2)}) %copy-start) | copy-done | bytes 32792
  44.0 0.7 %copy-done.1 = s32[90]{0:T(128)S(1)} copy-done((s32[90]{0:T(128)S(1)}, s32[90]{0:T(128)}, u32[]{:S(2)}) %copy-start.1) | copy-done | bytes 384
  44.7 0.7 %copy-done.2 = s32[90]{0:T(128)S(1)} copy-done((s32[90]{0:T(128)S(1)}, s32[90]{0:T(128)}, u32[]{:S(2)}) %copy-start.2) | copy-done | bytes 384
  45.3 17.9 %step.1 = (f32[3,1024]{1,0:T(4,128)}, f32[3,1024]{1,0:T(4,128)}) custom-call(f32[8,1024]{1,0:T(8,128)S(1)} %copy-done, f32[8,1024]{1,0:T(8,128)S(1)} %collective-permute-done.5.refs_1_, f32[8,1024]{1,0:T(8,128)S(1)} %collective-permute-done.6.refs_2_, f32[8,1024]{1,0:T(8,128)S(1)} %collective-permute-done.7.refs_3_, ...), custom_call_target="tpu_custom_call" | custom-call | flops 10000000 | bytes 60000000 | tf_op jit(solution)/shard_map/step/pallas_call | solution.py:378
  (6 shorter events, 0.0 us)
Async XLA Ops:
  3.0 19.9 %collective-permute-start = (f32[40,1024]{1,0:T(8,128)S(1)}, f32[40,1024]{1,0:T(8,128)S(1)}, u32[]{:S(2)}, u32[]{:S(2)}) collective-permute-start(f32[40,1024]{1,0:T(8,128)S(1)} %pad_maximum_fusion.refs_0_), channel_id=1, source_target_pairs={{0,2},{1,3},{2,0},{3,1},{4,6},{5,7},{6,4},{7,5},{8,10},{9,11},{10,... | collective-permute-start | bytes 491528 | tf_op jit(solution)/shard_map/ppermute | solution.py:455
  6.1 16.8 %collective-permute-start.1 = (f32[40,1024]{1,0:T(8,128)S(1)}, f32[40,1024]{1,0:T(8,128)S(1)}, u32[]{:S(2)}, u32[]{:S(2)}) collective-permute-start(f32[40,1024]{1,0:T(8,128)S(1)} %pad_maximum_fusion.refs_0_), channel_id=1, source_target_pairs={{0,4},{1,5},{2,6},{3,7},{4,0},{5,1},{6,2},{7,3},{8,12},{9,13},{10,... | collective-permute-start | bytes 491528 | tf_op jit(solution)/shard_map/ppermute | solution.py:455
  8.7 14.2 %collective-permute-start.2 = (f32[40,1024]{1,0:T(8,128)S(1)}, f32[40,1024]{1,0:T(8,128)S(1)}, u32[]{:S(2)}, u32[]{:S(2)}) collective-permute-start(f32[40,1024]{1,0:T(8,128)S(1)} %pad_maximum_fusion.refs_0_), channel_id=1, source_target_pairs={{0,6},{1,7},{2,4},{3,5},{4,2},{5,3},{6,0},{7,1},{8,14},{9,15},{10,... | collective-permute-start | bytes 491528 | tf_op jit(solution)/shard_map/ppermute | solution.py:455
  9.5 4.6 %collective-permute-start.3 = (f32[9,1024]{1,0:T(8,128)S(1)}, f32[9,1024]{1,0:T(8,128)S(1)}, u32[]{:S(2)}, u32[]{:S(2)}) collective-permute-start(f32[9,1024]{1,0:T(8,128)S(1)} %pad_maximum_fusion.1), channel_id=1, source_target_pairs={{0,8},{8,0},{16,24},{24,16},{1,9},{9,1},{17,25},{25,17},{2,10},{10... | collective-permute-start | bytes 110600 | tf_op jit(solution)/shard_map/ppermute | solution.py:455
  11.3 5.2 %collective-permute-start.4 = (f32[9,1024]{1,0:T(8,128)S(1)}, f32[9,1024]{1,0:T(8,128)S(1)}, u32[]{:S(2)}, u32[]{:S(2)}) collective-permute-start(f32[9,1024]{1,0:T(8,128)S(1)} %pad_maximum_fusion.1), channel_id=1, source_target_pairs={{0,24},{8,16},{16,8},{24,0},{1,25},{9,17},{17,9},{25,1},{2,26},{10... | collective-permute-start | bytes 110600 | tf_op jit(solution)/shard_map/ppermute | solution.py:460
  14.1 2.3 %copy-start.5 = (f32[9,1024]{1,0:T(8,128)}, f32[9,1024]{1,0:T(8,128)S(1)}, u32[]{:S(2)}) copy-start(f32[9,1024]{1,0:T(8,128)S(1)} %collective-permute-done.3.refs_4_) | copy-start | bytes 110596
  16.4 0.6 copy-start.6
  22.9 1.9 %collective-permute-start.10 = (f32[40,1024]{1,0:T(8,128)S(1)}, f32[40,1024]{1,0:T(8,128)S(1)}, u32[]{:S(2)}, u32[]{:S(2)}) collective-permute-start(f32[40,1024]{1,0:T(8,128)S(1)} %collective-permute-done.1.refs_2_), channel_id=1, source_target_pairs={{0,1},{1,0},{2,3},{3,2},{4,5},{5,4},{6,7},{7,6},{8,9},{9,8},{10,11... | collective-permute-start | bytes 491528 | tf_op jit(solution)/shard_map/ppermute | solution.py:455
  23.0 5.2 %collective-permute-start.11 = (f32[40,1024]{1,0:T(8,128)S(1)}, f32[40,1024]{1,0:T(8,128)S(1)}, u32[]{:S(2)}, u32[]{:S(2)}) collective-permute-start(f32[40,1024]{1,0:T(8,128)S(1)} %collective-permute-done.2.refs_3_), channel_id=1, source_target_pairs={{0,1},{1,0},{2,3},{3,2},{4,5},{5,4},{6,7},{7,6},{8,9},{9,8},{10,11... | collective-permute-start | bytes 491528 | tf_op jit(solution)/shard_map/ppermute | solution.py:455
  23.5 4.9 %collective-permute-start.8 = (f32[40,1024]{1,0:T(8,128)S(1)}, f32[40,1024]{1,0:T(8,128)S(1)}, u32[]{:S(2)}, u32[]{:S(2)}) collective-permute-start(f32[40,1024]{1,0:T(8,128)S(1)} %pad_maximum_fusion.refs_0_), channel_id=1, source_target_pairs={{0,1},{1,0},{2,3},{3,2},{4,5},{5,4},{6,7},{7,6},{8,9},{9,8},{10,11... | collective-permute-start | bytes 491528 | tf_op jit(solution)/shard_map/ppermute | solution.py:455
  23.6 4.8 %collective-permute-start.9 = (f32[40,1024]{1,0:T(8,128)S(1)}, f32[40,1024]{1,0:T(8,128)S(1)}, u32[]{:S(2)}, u32[]{:S(2)}) collective-permute-start(f32[40,1024]{1,0:T(8,128)S(1)} %collective-permute-done.refs_1_), channel_id=1, source_target_pairs={{0,1},{1,0},{2,3},{3,2},{4,5},{5,4},{6,7},{7,6},{8,9},{9,8},{10,11... | collective-permute-start | bytes 491528 | tf_op jit(solution)/shard_map/ppermute | solution.py:455
  24.0 17.2 %collective-permute-start.5 = (f32[8,1024]{1,0:T(8,128)}, f32[8,1024]{1,0:T(8,128)S(1)}, u32[]{:S(2)}, u32[]{:S(2)}) collective-permute-start(f32[8,1024]{1,0:T(8,128)} %long_range.1.refs_0_), channel_id=1, source_target_pairs={{0,2},{1,3},{2,0},{3,1},{4,6},{5,7},{6,4},{7,5},{8,10},{9,11},{10,... | collective-permute-start | bytes 98312 | tf_op jit(solution)/shard_map/ppermute | solution.py:455
  24.8 16.4 %collective-permute-start.6 = (f32[8,1024]{1,0:T(8,128)}, f32[8,1024]{1,0:T(8,128)S(1)}, u32[]{:S(2)}, u32[]{:S(2)}) collective-permute-start(f32[8,1024]{1,0:T(8,128)} %long_range.1.refs_0_), channel_id=1, source_target_pairs={{0,4},{1,5},{2,6},{3,7},{4,0},{5,1},{6,2},{7,3},{8,12},{9,13},{10,... | collective-permute-start | bytes 98312 | tf_op jit(solution)/shard_map/ppermute | solution.py:455
  28.2 13.1 %collective-permute-start.7 = (f32[8,1024]{1,0:T(8,128)}, f32[8,1024]{1,0:T(8,128)S(1)}, u32[]{:S(2)}, u32[]{:S(2)}) collective-permute-start(f32[8,1024]{1,0:T(8,128)} %long_range.1.refs_0_), channel_id=1, source_target_pairs={{0,6},{1,7},{2,4},{3,5},{4,2},{5,3},{6,0},{7,1},{8,14},{9,15},{10,... | collective-permute-start | bytes 98312 | tf_op jit(solution)/shard_map/ppermute | solution.py:455
  28.4 0.7 %copy-start.3 = (s32[46]{0:T(128)S(1)}, s32[46]{0:T(128)}, u32[]{:S(2)}) copy-start(s32[46]{0:T(128)} %constant.8.clone.refs_8_) | copy-start | bytes 556
  29.1 0.7 %copy-start.4 = (s32[46]{0:T(128)S(1)}, s32[46]{0:T(128)}, u32[]{:S(2)}) copy-start(s32[46]{0:T(128)} %constant.9.clone.refs_9_) | copy-start | bytes 556
  41.3 1.5 %collective-permute-start.12 = (f32[8,1024]{1,0:T(8,128)}, f32[8,1024]{1,0:T(8,128)S(1)}, u32[]{:S(2)}, u32[]{:S(2)}) collective-permute-start(f32[8,1024]{1,0:T(8,128)} %long_range.1.refs_0_), channel_id=1, source_target_pairs={{0,1},{1,0},{2,3},{3,2},{4,5},{5,4},{6,7},{7,6},{8,9},{9,8},{10,11... | collective-permute-start | bytes 98312 | tf_op jit(solution)/shard_map/ppermute | solution.py:455
  41.4 1.4 %collective-permute-start.13 = (f32[8,1024]{1,0:T(8,128)S(1)}, f32[8,1024]{1,0:T(8,128)S(1)}, u32[]{:S(2)}, u32[]{:S(2)}) collective-permute-start(f32[8,1024]{1,0:T(8,128)S(1)} %collective-permute-done.5.refs_1_), channel_id=1, source_target_pairs={{0,1},{1,0},{2,3},{3,2},{4,5},{5,4},{6,7},{7,6},{8,9},{9,8},{10,11... | collective-permute-start | bytes 98312 | tf_op jit(solution)/shard_map/ppermute | solution.py:455
  41.9 1.2 %collective-permute-start.14 = (f32[8,1024]{1,0:T(8,128)S(1)}, f32[8,1024]{1,0:T(8,128)S(1)}, u32[]{:S(2)}, u32[]{:S(2)}) collective-permute-start(f32[8,1024]{1,0:T(8,128)S(1)} %collective-permute-done.6.refs_2_), channel_id=1, source_target_pairs={{0,1},{1,0},{2,3},{3,2},{4,5},{5,4},{6,7},{7,6},{8,9},{9,8},{10,11... | collective-permute-start | bytes 98312 | tf_op jit(solution)/shard_map/ppermute | solution.py:455
  41.9 1.3 %collective-permute-start.15 = (f32[8,1024]{1,0:T(8,128)S(1)}, f32[8,1024]{1,0:T(8,128)S(1)}, u32[]{:S(2)}, u32[]{:S(2)}) collective-permute-start(f32[8,1024]{1,0:T(8,128)S(1)} %collective-permute-done.7.refs_3_), channel_id=1, source_target_pairs={{0,1},{1,0},{2,3},{3,2},{4,5},{5,4},{6,7},{7,6},{8,9},{9,8},{10,11... | collective-permute-start | bytes 98312 | tf_op jit(solution)/shard_map/ppermute | solution.py:455
  43.2 0.8 %copy-start = (f32[8,1024]{1,0:T(8,128)S(1)}, f32[8,1024]{1,0:T(8,128)}, u32[]{:S(2)}) copy-start(f32[8,1024]{1,0:T(8,128)} %long_range.1.refs_0_) | copy-start | bytes 98308
  44.0 0.7 %copy-start.1 = (s32[90]{0:T(128)S(1)}, s32[90]{0:T(128)}, u32[]{:S(2)}) copy-start(s32[90]{0:T(128)} %constant.10.clone.refs_11_) | copy-start | bytes 1084
  44.7 0.7 %copy-start.2 = (s32[90]{0:T(128)S(1)}, s32[90]{0:T(128)}, u32[]{:S(2)}) copy-start(s32[90]{0:T(128)} %constant.11.clone.refs_12_) | copy-start | bytes 1084

commit v3 on v2

--- a/solution.py
+++ b/solution.py
@@ -30,16 +30,18 @@
     return [sorted(level) for level in levels[::-1]]
 
 
+SMALL_VMEM = 8
+PACK_VMEM = 60
 WEIGHT_VMEM = 24
 STEP_VMEM = 24
 
-def fetch(refs, held, me, sem):
+def fetch(refs, held, me, sem, order):
     half = len(refs) // 2
     copies = []
     for j in range(half):
         for other in range(2):
             at = other * half + j
-            copies.append(pltpu.make_async_copy(refs[at], held.at[me ^ (2 * j + other)], sem.at[at]))
+            copies.append(pltpu.make_async_copy(refs[at], held.at[me ^ (2 * order[j] + other)], sem.at[at]))
     for copy in copies:
         copy.start()
     for copy in copies:
@@ -48,8 +50,7 @@
 
 def weights_kernel(domains, slots, subs, plan, own_index, *refs):
     block_refs = refs[:domains]
-    dom_table, half_table = refs[domains : domains + 2]
-    weight, close, gplaces, pack, still_rows, still, sem = refs[domains + 2 :]
+    weight, close, gplaces, pack, still_rows, still, sem = refs[domains:]
     seg = pack.shape[2]
     cells = seg // LANES
     groups = slots // ROWS
@@ -59,7 +60,7 @@
     me = own_index()
     scale = 1.0 / math.sqrt(slots)
     LINE, BURG, GHOST = slots, slots + 3, slots + 6
-    fetch(block_refs, pack, me, sem)
+    fetch(block_refs, pack, me, sem, [0, *range(domains // 2 - 1, 0, -1)])
 
     row = lax.broadcasted_iota(jnp.int32, (ROWS, LANES), 0)
     x_rows = row < 2
@@ -89,13 +90,13 @@
 
     lax.fori_loop(0, domains, expand, 0)
 
-    def domain_at(i):
-        return lax.rem(dom_table[i] + me, domains)
-
-    def owner_picks(i, count, sub, sources):
+    def domain_of(offset):
+        return lax.rem(offset + me, domains)
+
+    def owner_picks(owners, sub, sources):
         made = []
-        for u in range(count):
-            d = domain_at(i + u)
+        for offset, _ in owners:
+            d = domain_of(offset)
             for side in range(2):
                 place = gplaces[d, :, pl.ds(pl.multiple_of((2 * sub + side) * LANES, LANES), LANES)]
                 lane = place & (LANES - 1)
@@ -111,20 +112,21 @@
             ref[*slot, to, at] = out
 
     def over(span, body):
-        start, steps, count = span
+        steps, count, entries = span
         if steps == 1:
-            body(start, count)
+            body(entries)
             return
         def one(i, carry):
-            body(start + i * count, count)
+            body([tuple(chosen(i, [entries[n * count + u][at] for n in range(steps)]) for at in (0, 1)) for u in range(count)])
             return carry
         lax.fori_loop(0, steps, one, 0)
 
-    def items(i, count):
-        for u in range(count):
-            d = domain_at(i + u)
+    def items(entries):
+        for offset, side in entries:
+            d = domain_of(offset)
             for k in range(half_cells):
-                yield d, pl.multiple_of(half_table[i + u] * half_lanes + k * LANES, LANES), k
+                lane = side * half_lanes + k * LANES
+                yield d, lane if isinstance(lane, int) else pl.multiple_of(lane, LANES), k
 
     def dots(mine, theirs):
         return mine[0] * theirs[0] + mine[1] * theirs[1] + mine[2] * theirs[2]
@@ -141,9 +143,9 @@
         for g in range(groups):
             yield (d, slice(g * ROWS, (g + 1) * ROWS), pl.ds(lane, LANES))
 
-    def weights(i, count, upto):
+    def weights(entries, upto):
         made = []
-        for d, lane, k in items(i, count):
+        for d, lane, k in items(entries):
             mine = [bcast(pack, (d,), LINE + c, lane) for c in range(6)]
             far = [ghost_rows(still, (sub, 0), d, k) + ghost_rows(still, (sub, 1), d, k) for sub in range(upto)]
             for at in blocks(d, lane):
@@ -158,16 +160,16 @@
             ref[...] = value
 
     for sub in range(subs):
-        over(plan["still"][sub], lambda i, count: owner_picks(i, count, sub, ((still_rows.at[0], still, (sub, 0)), (still_rows.at[1], still, (sub, 1)))))
+        over(plan["still"][sub], lambda owners: owner_picks(owners, sub, ((still_rows.at[0], still, (sub, 0)), (still_rows.at[1], still, (sub, 1)))))
     for upto, span in plan["weights"]:
-        over(span, lambda i, count: weights(i, count, upto))
+        over(span, lambda entries: weights(entries, upto))
 
 
 def step_kernel(domains, slots, subs, plan, own_index, *refs):
     now_refs = refs[:domains]
-    weight, close, gplaces, dom_table, half_table = refs[domains : domains + 5]
-    out_pos, out_vel = refs[domains + 5 : domains + 7]
-    now, state, vels, long_, ghost, sem = refs[domains + 7 :]
+    weight, close, gplaces = refs[domains : domains + 3]
+    out_pos, out_vel = refs[domains + 3 : domains + 5]
+    now, state, vels, long_, ghost, sem = refs[domains + 5 :]
     seg = now.shape[2]
     evals = vels.shape[0]
     cells = seg // LANES
@@ -176,7 +178,7 @@
     half_lanes = half_cells * LANES
     me = own_index()
     POS, MOB, FAR = 0, 3, 4
-    fetch(now_refs, now, me, sem)
+    fetch(now_refs, now, me, sem, range(domains // 2))
 
     row = lax.broadcasted_iota(jnp.int32, (ROWS, LANES), 0)
     x_rows = row < 2
@@ -198,13 +200,13 @@
 
     lax.fori_loop(0, domains, expand, 0)
 
-    def domain_at(i):
-        return lax.rem(dom_table[i] + me, domains)
-
-    def owner_picks(i, count, sub, sources):
+    def domain_of(offset):
+        return lax.rem(offset + me, domains)
+
+    def owner_picks(owners, sub, sources):
         made = []
-        for u in range(count):
-            d = domain_at(i + u)
+        for offset, _ in owners:
+            d = domain_of(offset)
             for side in range(2):
                 place = gplaces[d, :, pl.ds(pl.multiple_of((2 * sub + side) * LANES, LANES), LANES)]
                 lane = place & (LANES - 1)
@@ -220,20 +222,21 @@
             ref[*slot, to, at] = out
 
     def over(span, body):
-        start, steps, count = span
+        steps, count, entries = span
         if steps == 1:
-            body(start, count)
+            body(entries)
             return
         def one(i, carry):
-            body(start + i * count, count)
+            body([tuple(chosen(i, [entries[n * count + u][at] for n in range(steps)]) for at in (0, 1)) for u in range(count)])
             return carry
         lax.fori_loop(0, steps, one, 0)
 
-    def items(i, count):
-        for u in range(count):
-            d = domain_at(i + u)
+    def items(entries):
+        for offset, side in entries:
+            d = domain_of(offset)
             for k in range(half_cells):
-                yield d, pl.multiple_of(half_table[i + u] * half_lanes + k * LANES, LANES), k
+                lane = side * half_lanes + k * LANES
+                yield d, lane if isinstance(lane, int) else pl.multiple_of(lane, LANES), k
 
     def ghost_rows(ref, slot, d, k):
         side, pair = divmod(k, 2)
@@ -270,11 +273,11 @@
         sub = level // 2
         stage = lax.rem(level, 2)
         base = level - stage
-        over(owners, lambda i, count: owner_picks(i, count, sub, ((state.at[level], ghost, ()),)))
-
-        def one(i, count):
+        over(owners, lambda owners: owner_picks(owners, sub, ((state.at[level], ghost, ()),)))
+
+        def one(entries):
             made = []
-            for d, lane, k in items(i, count):
+            for d, lane, k in items(entries):
                 here = pl.ds(lane, LANES)
                 vel = bcast(now, (d,), MOB, lane) * (long_[d, :, here] + force(level, sub, d, lane, k))
                 vel = jnp.where(stage == 1, 0.5 * (vels[base, d, :, here] + vel), vel)
@@ -296,27 +299,27 @@
         out_vel[c : c + 1, :] = vels[evals - 1, me, 2 * c : 2 * c + 1, :]
 
 
-class Plan:
-    def __init__(self):
-        self.domains, self.halves = [], []
-
-    def span(self, entries, limit):
-        count = min(range(1, limit + 1), key=lambda c: (-(-len(entries) // c) * (c + 0.5), c))
-        start, steps = len(self.domains), -(-len(entries) // count)
-        entries = entries + [entries[-1]] * (steps * count - len(entries))
-        self.domains.extend(d for d, _ in entries)
-        self.halves.extend(h for _, h in entries)
-        return start, steps, count
-
-    def tables(self):
-        return jnp.array(self.domains, jnp.int32), jnp.array(self.halves, jnp.int32)
+def span(entries, limit):
+    count = min(range(1, limit + 1), key=lambda c: (-(-len(entries) // c) * (c + 0.5), c))
+    steps = -(-len(entries) // count)
+    return steps, count, entries + [entries[-1]] * (steps * count - len(entries))
+
+
+def chosen(step, values):
+    if len(set(values)) == 1:
+        return values[0]
+    if [v - values[0] for v in values] == [n * (values[1] - values[0]) for n in range(len(values))]:
+        return values[0] + step * (values[1] - values[0])
+    out = values[-1]
+    for n in range(len(values) - 2, -1, -1):
+        out = jnp.where(step == n, values[n], out)
+    return out
 
 
 def owners_of(level, domains):
     return sorted({((d + s) % domains, 0) for d, _ in level for s in (1, -1)})
 
 
-TABLE = pl.BlockSpec(memory_space=pltpu.SMEM)
 ANYWHERE = pl.BlockSpec(memory_space=pl.ANY)
 VMEM = pl.BlockSpec(memory_space=pltpu.VMEM)
 
@@ -325,13 +328,12 @@
     domains = len(blocks)
     rows, seg = blocks[0].shape
     levels = level_halves(domains, 2 * subs)
-    table = Plan()
-    plan = {"still": [table.span(owners_of(levels[2 * t], domains), most_owners) for t in range(subs)], "weights": []}
+    plan = {"still": [span(owners_of(levels[2 * t], domains), most_owners) for t in range(subs)], "weights": []}
     for upto in range(1, subs + 1):
         after = levels[2 * upto] if upto < subs else []
         only = [h for h in levels[2 * upto - 2] if h not in after]
         if only:
-            plan["weights"].append((upto, table.span(only, most)))
+            plan["weights"].append((upto, span(only, most)))
 
     def kernel(*refs):
         weights_kernel(domains, slots, subs, plan, own_index, *refs)
@@ -343,7 +345,7 @@
             jax.ShapeDtypeStruct((domains, slots, seg), jnp.int32),
             jax.ShapeDtypeStruct((domains, ROWS, seg), jnp.int32),
         ],
-        in_specs=[ANYWHERE] * domains + [TABLE] * 2,
+        in_specs=[ANYWHERE] * domains,
         out_specs=[VMEM] * 3,
         scratch_shapes=[
             pltpu.VMEM((domains, rows, seg), jnp.float32),
@@ -354,7 +356,7 @@
         compiler_params=pltpu.CompilerParams(vmem_limit_bytes=WEIGHT_VMEM * 2**20),
         cost_estimate=pl.CostEstimate(flops=10**7, bytes_accessed=4 * 10**7, transcendentals=0),
         name="weights",
-    )(*blocks, *table.tables())
+    )(*blocks)
 
 
 def step(now, weights, subs, own_index, most=8, most_owners=8):
@@ -362,14 +364,13 @@
     rows, seg = now[0].shape
     slots = weights[0].shape[2]
     levels = level_halves(domains, 2 * subs)
-    table = Plan()
     plan = {"levels": []}
     first = 0
     while first < len(levels):
         last = first + 1
         while last < len(levels) and levels[last] == levels[first]:
             last += 1
-        plan["levels"].append((first, last, table.span(owners_of(levels[first], domains), most_owners), table.span(levels[first], most)))
+        plan["levels"].append((first, last, span(owners_of(levels[first], domains), most_owners), span(levels[first], most)))
         first = last
 
     def kernel(*refs):
@@ -378,7 +379,7 @@
     return pl.pallas_call(
         kernel,
         out_shape=[jax.ShapeDtypeStruct((3, seg), jnp.float32)] * 2,
-        in_specs=[ANYWHERE] * domains + [VMEM] * 3 + [TABLE] * 2,
+        in_specs=[ANYWHERE] * domains + [VMEM] * 3,
         out_specs=[VMEM] * 2,
         scratch_shapes=[
             pltpu.VMEM((domains, rows, seg), jnp.float32),
@@ -391,58 +392,125 @@
         compiler_params=pltpu.CompilerParams(vmem_limit_bytes=STEP_VMEM * 2**20),
         cost_estimate=pl.CostEstimate(flops=10**7, bytes_accessed=6 * 10**7, transcendentals=10**6),
         name="step",
-    )(*now, *weights, *table.tables())
-
-
-def long_kernel(sources, seg, *refs):
-    own, mob = refs[:3], refs[3]
-    others = refs[4 : 4 + sources]
-    out, tiles = refs[4 + sources :]
+    )(*now, *weights)
+
+
+def pack_kernel(*refs):
+    here, (block, state), held, sem = refs[:6], refs[6:8], refs[8:14], refs[14]
+    copies = [pltpu.make_async_copy(src, dst, sem.at[n]) for n, (src, dst) in enumerate(zip(here, held))]
+    for copy in copies:
+        copy.start()
+    for copy in copies:
+        copy.wait()
+    positions, line_vectors, burgers, mobility, close_list, ghost_map = held
+    slots, seg = close_list.shape
+    block[:slots, :] = close_list[...].astype(jnp.float32)
+    state[0:3, :] = positions[...]
+    for at, ref in ((0, line_vectors), (3, burgers)):
+        block[slots + at : slots + at + 3, :] = ref[...]
+        state[3 + at : 6 + at, :] = ref[...]
+    state[9:10, :] = mobility[...]
+    subs, wide = ghost_map.shape
+    per = seg // wide
+    for t in range(subs):
+        at = slots + 6 + t // per
+        block[at : at + 1, (t % per) * wide : (t % per + 1) * wide] = ghost_map[t : t + 1, :].astype(jnp.float32)
+
+
+def packed(*arrays):
+    slots, seg = arrays[4].shape
+    return pl.pallas_call(
+        pack_kernel,
+        out_shape=[jax.ShapeDtypeStruct((slots + 6 + arrays[5].size // seg, seg), jnp.float32), jax.ShapeDtypeStruct((10, seg), jnp.float32)],
+        in_specs=[pl.BlockSpec(memory_space=pltpu.HBM)] * 6,
+        out_specs=[VMEM] * 2,
+        scratch_shapes=[pltpu.VMEM(a.shape, a.dtype) for a in arrays] + [pltpu.SemaphoreType.DMA((6,))],
+        compiler_params=pltpu.CompilerParams(vmem_limit_bytes=PACK_VMEM * 2**20),
+        name="pack",
+    )(*arrays)
+
+
+def split(rows):
+    parts = []
+    for _ in range(3):
+        parts.append(rows.astype(jnp.bfloat16).astype(jnp.float32))
+        rows = rows - parts[-1]
+    return parts
+
+
+SOURCE_PARTS = (0, 0, 1, 0, 2, 1)
+TARGET_PARTS = (0, 1, 0, 2, 0, 1)
+FEATURES = 48
+
+
+def long_kernel(sources, seg, unroll, *refs):
+    states, block = refs[: sources + 1], refs[sources + 1]
+    out, held, features, aims, sem = refs[sources + 2 :]
+    copy = pltpu.make_async_copy(block, held, sem)
+    copy.start()
     cells = seg // LANES
-    unroll = 16
     scale = 1.0 / math.sqrt((sources + 1) * LANES)
+    zero = jnp.zeros((3, seg), jnp.float32)
     for s in range(sources + 1):
-        for c in range(9):
-            for q in range(cells):
-                src = own[c // 3][c % 3 : c % 3 + 1, q * LANES : (q + 1) * LANES] if s == 0 else others[s - 1][c : c + 1, q * LANES : (q + 1) * LANES]
-                tiles[s * 9 + c, q : q + 1, :] = src
-    mine = [tiles[c] for c in range(9)]
-
-    def one(i, forces):
-        forces = list(forces)
+        vectors = (states[s][3:6, :], states[s][6:9, :])
+        for n, vector in enumerate(vectors):
+            parts = split(vector)
+            for k, part in enumerate(SOURCE_PARTS):
+                features[s, 18 * n + 3 * k : 18 * n + 3 * k + 3, :] = parts[part]
+            if s == 0:
+                for k, part in enumerate(TARGET_PARTS):
+                    aims[18 * n + 3 * k : 18 * n + 3 * k + 3, :] = parts[part]
+        for k, part in enumerate(split(states[s][0:3, :])):
+            features[s, 36 + 3 * k : 39 + 3 * k, :] = part
+        features[s, 45:48, :] = zero
+    out[0:3, :] = states[0][0:3, :]
+    out[3:4, :] = states[0][9:10, :]
+    row = lax.broadcasted_iota(jnp.int32, (FEATURES, LANES), 0)
+    column_of = [jnp.where((row >= 36) & (row < 45) & (row % 3 == c), 1.0, 0.0) for c in range(3)]
+
+    def cell_at(lane):
+        here = pl.ds(lane, LANES)
+        aim = aims[:, here]
+        right = jnp.concatenate([jnp.where(row < 18, aim, 0.0), jnp.where((row >= 18) & (row < 36), aim, 0.0), *column_of], 1).astype(jnp.bfloat16)
+        mine = [states[0][c : c + 1, here] for c in range(3)]
+        forces = [jnp.zeros((ROWS, LANES), jnp.float32)] * 3
         for s in range(sources + 1):
-            for u in range(unroll):
-                other = [pltpu.roll(tiles[s * 9 + c], i * unroll + u, 1) for c in range(9)]
-                delta = [mine[c] - other[c] for c in range(3)]
-                radius = delta[0] * delta[0] + delta[1] * delta[1] + delta[2] * delta[2] + long_core * long_core
-                inverse = lax.rsqrt(radius)
-                line = mine[3] * other[3] + mine[4] * other[4] + mine[5] * other[5]
-                burg = mine[6] * other[6] + mine[7] * other[7] + mine[8] * other[8]
-                w = burg * line * (inverse * inverse * inverse)
-                for c in range(3):
-                    forces[c] = forces[c] + w * delta[c]
-        return tuple(forces)
-
-    out[0:3, :] = own[0][...]
-    out[3:4, :] = mob[...]
-    zero = jnp.zeros_like(mine[0])
-    forces = lax.fori_loop(0, LANES // unroll, one, (zero,) * 3)
-    for c in range(3):
-        for q in range(cells):
-            out[4 + c : 5 + c, q * LANES : (q + 1) * LANES] = forces[c][q : q + 1, :] * scale
-
-
-def long_range(positions, line_vectors, burgers, mobility, others):
-    seg = positions.shape[1]
+            left = jnp.transpose(features[s, :, here]).astype(jnp.bfloat16)
+            made = jnp.dot(left, right, preferred_element_type=jnp.float32)
+            line, burg, *at = [made[:, n * LANES : (n + 1) * LANES] for n in range(5)]
+            delta = [m - a for m, a in zip(mine, at)]
+            radius = delta[0] * delta[0] + delta[1] * delta[1] + delta[2] * delta[2] + long_core * long_core
+            inverse = lax.rsqrt(radius)
+            w = burg * line * (inverse * inverse * inverse)
+            for c in range(3):
+                forces[c] = forces[c] + jnp.sum((w * delta[c]).reshape(-1, ROWS, LANES), 0)
+        return [jnp.sum(f, 0, keepdims=True) * scale for f in forces]
+
+    def one(i, carry):
+        lanes = [pl.multiple_of((i * unroll + u) * LANES, LANES) for u in range(unroll)]
+        made = [cell_at(lane) for lane in lanes]
+        for lane, forces in zip(lanes, made):
+            for c in range(3):
+                out[4 + c : 5 + c, pl.ds(lane, LANES)] = forces[c]
+        return carry
+
+    aims[36:48, :] = jnp.zeros((12, seg), jnp.float32)
+    lax.fori_loop(0, cells // unroll, one, 0)
+    copy.wait()
+
+
+def long_range(state, others, block, unroll=8):
+    seg = state.shape[1]
     return pl.pallas_call(
-        lambda *refs: long_kernel(len(others), seg, *refs),
-        out_shape=jax.ShapeDtypeStruct((ROWS, seg), jnp.float32),
-        in_specs=[pl.BlockSpec(memory_space=pltpu.VMEM)] * (4 + len(others)),
-        out_specs=pl.BlockSpec(memory_space=pltpu.VMEM),
-        scratch_shapes=[pltpu.VMEM((9 * (len(others) + 1), seg // LANES, LANES), jnp.float32)],
+        lambda *refs: long_kernel(len(others), seg, unroll, *refs),
+        out_shape=[jax.ShapeDtypeStruct((ROWS, seg), jnp.float32), jax.ShapeDtypeStruct(block.shape, block.dtype)],
+        in_specs=[VMEM] * (1 + len(others)) + [pl.BlockSpec(memory_space=pl.ANY)],
+        out_specs=[VMEM] * 2,
+        scratch_shapes=[pltpu.VMEM((len(others) + 1, FEATURES, seg), jnp.float32), pltpu.VMEM((FEATURES, seg), jnp.float32), pltpu.SemaphoreType.DMA(())],
+        compiler_params=pltpu.CompilerParams(vmem_limit_bytes=SMALL_VMEM * 2**20),
         cost_estimate=pl.CostEstimate(flops=10**7, bytes_accessed=2 * 10**7, transcendentals=10**6),
         name="long_range",
-    )(positions, line_vectors, burgers, mobility[None], *others)
+    )(state, *others, block)
 
 
 def shifted(value, axis, steps):
@@ -463,21 +531,19 @@
     return got
 
 
-def along_chips(value):
-    return [value] + [matched(value, "dom", 2 * j) for j in range(1, lax.axis_size("dom") // 2)]
-
-
 def local(positions, line_vectors, burgers, mobility, close_list, ghost_map):
     slots, seg = close_list.shape
     subs = ghost_map.shape[0]
+    half = lax.axis_size("dom") // 2
     own_index = lambda: lax.axis_index("dom")
-    state = jnp.concatenate([positions, line_vectors, burgers], 0)
+    block, state = packed(positions, line_vectors, burgers, mobility[None], close_list, ghost_map)
     others = cycle_neighbours(state, "blk")
-    block = jnp.concatenate([close_list.astype(jnp.float32), line_vectors, burgers, ghost_map.astype(jnp.float32).reshape(-1, seg)], 0)
-    blocks = along_chips(block)
-    now = long_range(positions, line_vectors, burgers, mobility, others)
+    far_first = range(half - 1, 0, -1)
+    blocks = [matched(block, "dom", 2 * j) for j in far_first[:3]]
+    now, block = long_range(state, others, block)
     blocks, now = lax.optimization_barrier((blocks, now))
-    nows = along_chips(now)
+    nows = [now] + [matched(now, "dom", 2 * j) for j in range(1, half)]
+    blocks = [block] + blocks
     blocks = blocks + [matched(b, "dom", 1) for b in blocks]
     weights = pair_weights(blocks, slots, subs, own_index)
     nows, weights = lax.optimization_barrier((nows, weights))

time: 63.9 us -> 56.5 us (0.88)
  Pallas kernels: 35.3 us -> 31.5 us
  other arithmetic: 3.14 us -> 0 us
  waiting for transfers between devices: 4.56 us -> 7.38 us
  local copies, waits for them, and re-layouts: 4.01 us -> 1.75 us
    ppermute x15, waiting for transfers between devices: 2.25 us -> 5.14 us  [matched(): return lax.ppermute(value, axis, [(i, i ^ step) for i in range(count)])]
    unnamed x14 -> x4, local copies, waits for them, and re-layouts: 3.99 us -> 1.75 us
    pallas_call x1 -> x2, Pallas kernels: 5.88 us -> 3.72 us  [the longest x1 1.98 us: long_range(): pl.pallas_call(lambda *refs: long_kernel(len(others), seg, unroll, *refs)...]
    convert_element_type x2 -> x0, other arithmetic: 1.62 us -> none  [the longest x1 0.92 us: local(): close_list.astype(jnp.float32)]
    concatenate x2 -> x0, other arithmetic: 1.53 us -> none  [the longest x1 0.77 us: local(): state = jnp.concatenate([positions, line_vectors, burgers], 0)]
    pallas_call x1, Pallas kernels: 17.9 us -> 16.8 us  [step(): pl.pallas_call(kernel, out_shape=[jax.ShapeDtypeStruct((3, seg), jnp.floa...]
  transfers between devices with their start and end apart: 16 -> 16, of which waited for: 5 -> 7; matrix products, arithmetic and copies ran while one was open for 1% -> 0% of each run, Pallas kernels for 28% -> 23%
where the time goes in v3:
time: 56.5 us; the launch traced here: 56.3 us
  Pallas kernels  31.5 us (56%)
  starting transfers between devices  14.9 us (26%)
  waiting for transfers between devices  7.38 us (13%)
  local copies, waits for them, and re-layouts  1.75 us (3%)
  between operations  0.72 us (1%)
    pallas_call x1, Pallas kernels, step(): pl.pallas_call(kernel, out_shape=[jax.ShapeDtypeStruct((3, seg), jnp.floa...  16.8 us
    ppermute x15, starting transfers between devices, matched(): return lax.ppermute(value, axis, [(i, i ^ step) for i in range(count)])  13.4 us
    pallas_call x1, Pallas kernels, pair_weights(): pl.pallas_call(kernel, out_shape=[jax.ShapeDtypeStruct((subs, domains, sl...  10.9 us
    ppermute x15, waiting for transfers between devices, matched(): return lax.ppermute(value, axis, [(i, i ^ step) for i in range(count)])  5.14 us
    ppermute x1, waiting for transfers between devices, cycle_neighbours(): lax.ppermute(value, axis, [(i, ((i - 1) % count ^ 1) + 1 if (i - 1) % cou...  2.23 us
    pallas_call x1, Pallas kernels, long_range(): pl.pallas_call(lambda *refs: long_kernel(len(others), seg, unroll, *refs)...  1.98 us
    unnamed x4, local copies, waits for them, and re-layouts  1.75 us
    pallas_call x1, Pallas kernels, packed(): pl.pallas_call(pack_kernel, out_shape=[jax.ShapeDtypeStruct((slots + 6 +...  1.74 us
  transfers between devices with their start and end apart: 16, of which 7 were waited for; matrix products, arithmetic and copies ran while one was open for 0% of the time, Pallas kernels for 23%

profile of v3, /device:TPU:0, one launch (start us, length us, event | category | flops | bytes accessed | tf_op | source)
XLA Modules:
  0.0 56.3 jit_solution(2620081552434073287)
XLA Ops:
  0.6 1.7 %pack.1 = (f32[40,1024]{1,0:T(8,128)}, f32[10,1024]{1,0:T(8,128)}) custom-call(f32[3,1024]{1,0:T(4,128)} %refs_0_.1, f32[3,1024]{1,0:T(4,128)} %refs_1_.1, f32[3,1024]{1,0:T(4,128)} %refs_2_.1, f32[1,1024]{1,0:T(1,128)} %bitcast.1, s32[32,1024]{1,0:T(8,128)} %refs_4_.1, s32[4,512]{1,0:T(4,128)} %refs_5_.1), custom_call_target="tpu_custom_call" | custom-call | tf_op jit(solution)/shard_map/pack/pallas_call | solution.py:422
  2.4 5.1 %collective-permute-start = (f32[40,1024]{1,0:T(8,128)}, f32[40,1024]{1,0:T(8,128)S(1)}, u32[]{:S(2)}, u32[]{:S(2)}) collective-permute-start(f32[40,1024]{1,0:T(8,128)} %get-tuple-element.20.refs_3_), channel_id=1, source_target_pairs={{0,6},{1,7},{2,4},{3,5},{4,2},{5,3},{6,0},{7,1},{8,14},{9,15},{10,... | collective-permute-start | bytes 491528 | tf_op jit(solution)/shard_map/ppermute | solution.py:523
  7.5 0.0 collective-permute-start.1
  7.5 0.6 %collective-permute-start.2 = (f32[40,1024]{1,0:T(8,128)}, f32[40,1024]{1,0:T(8,128)S(1)}, u32[]{:S(2)}, u32[]{:S(2)}) collective-permute-start(f32[40,1024]{1,0:T(8,128)} %get-tuple-element.20.refs_3_), channel_id=1, source_target_pairs={{0,2},{1,3},{2,0},{3,1},{4,6},{5,7},{6,4},{7,5},{8,10},{9,11},{10,... | collective-permute-start | bytes 491528 | tf_op jit(solution)/shard_map/ppermute | solution.py:523
  8.1 1.6 %collective-permute-start.3 = (f32[10,1024]{1,0:T(8,128)}, f32[10,1024]{1,0:T(8,128)S(1)}, u32[]{:S(2)}, u32[]{:S(2)}) collective-permute-start(f32[10,1024]{1,0:T(8,128)} %get-tuple-element.21.refs_0_), channel_id=1, source_target_pairs={{0,8},{8,0},{16,24},{24,16},{1,9},{9,1},{17,25},{25,17},{2,10},{10... | collective-permute-start | bytes 122888 | tf_op jit(solution)/shard_map/ppermute | solution.py:523
  9.8 1.5 %collective-permute-start.4 = (f32[10,1024]{1,0:T(8,128)}, f32[10,1024]{1,0:T(8,128)S(1)}, u32[]{:S(2)}, u32[]{:S(2)}) collective-permute-start(f32[10,1024]{1,0:T(8,128)} %get-tuple-element.21.refs_0_), channel_id=1, source_target_pairs={{0,24},{8,16},{16,8},{24,0},{1,25},{9,17},{17,9},{25,1},{2,26},{10... | collective-permute-start | bytes 122888 | tf_op jit(solution)/shard_map/ppermute | solution.py:528
  11.3 1.7 %collective-permute-done.3.refs_1_ = f32[10,1024]{1,0:T(8,128)S(1)} collective-permute-done((f32[10,1024]{1,0:T(8,128)}, f32[10,1024]{1,0:T(8,128)S(1)}, u32[]{:S(2)}, u32[]{:S(2)}) %collective-permute-start.3) | collective-permute-done | bytes 40992 | tf_op jit(solution)/shard_map/ppermute | solution.py:523
  12.9 2.2 %collective-permute-done.4.refs_2_ = f32[10,1024]{1,0:T(8,128)S(1)} collective-permute-done((f32[10,1024]{1,0:T(8,128)}, f32[10,1024]{1,0:T(8,128)S(1)}, u32[]{:S(2)}, u32[]{:S(2)}) %collective-permute-start.4) | collective-permute-done | bytes 40992 | tf_op jit(solution)/shard_map/ppermute | solution.py:528
  15.1 0.0 copy-start
  15.2 0.9 %copy-done = f32[40,1024]{1,0:T(8,128)S(1)} copy-done((f32[40,1024]{1,0:T(8,128)S(1)}, f32[40,1024]{1,0:T(8,128)}, u32[]{:S(2)}) %copy-start) | copy-done | bytes 163864
  16.1 0.0 copy-start.1
  16.1 0.8 %copy-done.1 = f32[10,1024]{1,0:T(8,128)S(1)} copy-done((f32[10,1024]{1,0:T(8,128)S(1)}, f32[10,1024]{1,0:T(8,128)}, u32[]{:S(2)}) %copy-start.1) | copy-done | bytes 40984
  16.9 2.0 %long_range.1 = (f32[8,1024]{1,0:T(8,128)S(1)}, f32[40,1024]{1,0:T(8,128)S(1)}) custom-call(f32[10,1024]{1,0:T(8,128)S(1)} %copy-done.1, f32[10,1024]{1,0:T(8,128)S(1)} %collective-permute-done.3.refs_1_, f32[10,1024]{1,0:T(8,128)S(1)} %collective-permute-done.4.refs_2_, f32[40,1024]{1,0:T(8,128)S(1)} %copy-done), custom_call_target="tpu_custom_call" | custom-call | flops 10000000 | bytes 20000000 | tf_op jit(solution)/shard_map/long_range/pallas_call | solution.py:504
  18.9 0.1 collective-permute-start.8
  19.0 0.0 collective-permute-done.refs_1_
  19.0 2.6 %collective-permute-done.1.refs_2_ = f32[40,1024]{1,0:T(8,128)S(1)} collective-permute-done((f32[40,1024]{1,0:T(8,128)}, f32[40,1024]{1,0:T(8,128)S(1)}, u32[]{:S(2)}, u32[]{:S(2)}) %collective-permute-start.1) | collective-permute-done | bytes 163872 | tf_op jit(solution)/shard_map/ppermute | solution.py:523
  21.6 0.0 collective-permute-done.2.refs_3_
  21.6 0.0 collective-permute-start.10
  21.6 0.5 collective-permute-start.11
  22.1 0.0 collective-permute-start.9
  22.1 0.0 collective-permute-start.5
  22.1 0.0 collective-permute-done.8.refs_4_
  22.1 3.0 %collective-permute-start.6 = (f32[8,1024]{1,0:T(8,128)S(1)}, f32[8,1024]{1,0:T(8,128)S(1)}, u32[]{:S(2)}, u32[]{:S(2)}) collective-permute-start(f32[8,1024]{1,0:T(8,128)S(1)} %get-tuple-element.31.refs_0_), channel_id=1, source_target_pairs={{0,4},{1,5},{2,6},{3,7},{4,0},{5,1},{6,2},{7,3},{8,12},{9,13},{10,... | collective-permute-start | bytes 98312 | tf_op jit(solution)/shard_map/ppermute | solution.py:523
  25.2 0.0 collective-permute-done.10.refs_6_
  25.2 1.3 %collective-permute-start.7 = (f32[8,1024]{1,0:T(8,128)S(1)}, f32[8,1024]{1,0:T(8,128)S(1)}, u32[]{:S(2)}, u32[]{:S(2)}) collective-permute-start(f32[8,1024]{1,0:T(8,128)S(1)} %get-tuple-element.31.refs_0_), channel_id=1, source_target_pairs={{0,6},{1,7},{2,4},{3,5},{4,2},{5,3},{6,0},{7,1},{8,14},{9,15},{10,... | collective-permute-start | bytes 98312 | tf_op jit(solution)/shard_map/ppermute | solution.py:523
  26.5 0.0 collective-permute-done.11.refs_7_
  26.5 0.0 collective-permute-done.9.refs_5_
  26.5 10.9 %weights.1 = (f32[4,8,32,1024]{3,2,1,0:T(8,128)S(1)}, s32[8,32,1024]{2,1,0:T(8,128)S(1)}, s32[8,8,1024]{2,1,0:T(8,128)S(1)}) custom-call(f32[40,1024]{1,0:T(8,128)S(1)} %get-tuple-element.24.refs_0_, f32[40,1024]{1,0:T(8,128)S(1)} %collective-permute-done.refs_1_, f32[40,1024]{1,0:T(8,128)S(1)} %collective-permute-done.1.refs_2_, ...), custom_call_target="tpu_custom_call" | custom-call | flops 10000000 | bytes 40000000 | tf_op jit(solution)/shard_map/weights/pallas_call | solution.py:341
  37.4 0.0 collective-permute-done.5.refs_1_
  37.5 0.0 collective-permute-done.6.refs_2_
  37.5 0.0 collective-permute-done.7.refs_3_
  37.5 0.1 collective-permute-start.12
  37.6 0.5 collective-permute-start.13
  38.1 0.1 collective-permute-start.14
  38.1 0.4 collective-permute-start.15
  38.6 0.2 collective-permute-done.12.refs_4_
  38.8 0.2 collective-permute-done.13.refs_5_
  38.9 0.3 collective-permute-done.14.refs_6_
  39.3 0.2 collective-permute-done.15.refs_7_
  39.4 16.8 %step.1 = (f32[3,1024]{1,0:T(4,128)}, f32[3,1024]{1,0:T(4,128)}) custom-call(f32[8,1024]{1,0:T(8,128)S(1)} %get-tuple-element.31.refs_0_, f32[8,1024]{1,0:T(8,128)S(1)} %collective-permute-done.5.refs_1_, f32[8,1024]{1,0:T(8,128)S(1)} %collective-permute-done.6.refs_2_, f32[8,1024]{1,0:T(8,128)S(1)} %collective-permute-done.7.refs_3_, ...), custom_call_target="tpu_custom_call" | custom-call | flops 10000000 | bytes 60000000 | tf_op jit(solution)/shard_map/step/pallas_call | solution.py:379
Async XLA Ops:
  2.4 16.6 %collective-permute-start = (f32[40,1024]{1,0:T(8,128)}, f32[40,1024]{1,0:T(8,128)S(1)}, u32[]{:S(2)}, u32[]{:S(2)}) collective-permute-start(f32[40,1024]{1,0:T(8,128)} %get-tuple-element.20.refs_3_), channel_id=1, source_target_pairs={{0,6},{1,7},{2,4},{3,5},{4,2},{5,3},{6,0},{7,1},{8,14},{9,15},{10,... | collective-permute-start | bytes 491528 | tf_op jit(solution)/shard_map/ppermute | solution.py:523
  7.5 14.1 %collective-permute-start.1 = (f32[40,1024]{1,0:T(8,128)}, f32[40,1024]{1,0:T(8,128)S(1)}, u32[]{:S(2)}, u32[]{:S(2)}) collective-permute-start(f32[40,1024]{1,0:T(8,128)} %get-tuple-element.20.refs_3_), channel_id=1, source_target_pairs={{0,4},{1,5},{2,6},{3,7},{4,0},{5,1},{6,2},{7,3},{8,12},{9,13},{10,... | collective-permute-start | bytes 491528 | tf_op jit(solution)/shard_map/ppermute | solution.py:523
  7.5 14.1 %collective-permute-start.2 = (f32[40,1024]{1,0:T(8,128)}, f32[40,1024]{1,0:T(8,128)S(1)}, u32[]{:S(2)}, u32[]{:S(2)}) collective-permute-start(f32[40,1024]{1,0:T(8,128)} %get-tuple-element.20.refs_3_), channel_id=1, source_target_pairs={{0,2},{1,3},{2,0},{3,1},{4,6},{5,7},{6,4},{7,5},{8,10},{9,11},{10,... | collective-permute-start | bytes 491528 | tf_op jit(solution)/shard_map/ppermute | solution.py:523
  8.1 4.8 %collective-permute-start.3 = (f32[10,1024]{1,0:T(8,128)}, f32[10,1024]{1,0:T(8,128)S(1)}, u32[]{:S(2)}, u32[]{:S(2)}) collective-permute-start(f32[10,1024]{1,0:T(8,128)} %get-tuple-element.21.refs_0_), channel_id=1, source_target_pairs={{0,8},{8,0},{16,24},{24,16},{1,9},{9,1},{17,25},{25,17},{2,10},{10... | collective-permute-start | bytes 122888 | tf_op jit(solution)/shard_map/ppermute | solution.py:523
  9.8 5.4 %collective-permute-start.4 = (f32[10,1024]{1,0:T(8,128)}, f32[10,1024]{1,0:T(8,128)S(1)}, u32[]{:S(2)}, u32[]{:S(2)}) collective-permute-start(f32[10,1024]{1,0:T(8,128)} %get-tuple-element.21.refs_0_), channel_id=1, source_target_pairs={{0,24},{8,16},{16,8},{24,0},{1,25},{9,17},{17,9},{25,1},{2,26},{10... | collective-permute-start | bytes 122888 | tf_op jit(solution)/shard_map/ppermute | solution.py:528
  15.1 0.9 %copy-start = (f32[40,1024]{1,0:T(8,128)S(1)}, f32[40,1024]{1,0:T(8,128)}, u32[]{:S(2)}) copy-start(f32[40,1024]{1,0:T(8,128)} %get-tuple-element.20.refs_3_) | copy-start | bytes 491524
  16.1 0.8 %copy-start.1 = (f32[10,1024]{1,0:T(8,128)S(1)}, f32[10,1024]{1,0:T(8,128)}, u32[]{:S(2)}) copy-start(f32[10,1024]{1,0:T(8,128)} %get-tuple-element.21.refs_0_) | copy-start | bytes 122884
  18.9 3.2 %collective-permute-start.8 = (f32[40,1024]{1,0:T(8,128)S(1)}, f32[40,1024]{1,0:T(8,128)S(1)}, u32[]{:S(2)}, u32[]{:S(2)}) collective-permute-start(f32[40,1024]{1,0:T(8,128)S(1)} %get-tuple-element.24.refs_0_), channel_id=1, source_target_pairs={{0,1},{1,0},{2,3},{3,2},{4,5},{5,4},{6,7},{7,6},{8,9},{9,8},{10,11... | collective-permute-start | bytes 491528 | tf_op jit(solution)/shard_map/ppermute | solution.py:523
  21.6 3.6 %collective-permute-start.10 = (f32[40,1024]{1,0:T(8,128)S(1)}, f32[40,1024]{1,0:T(8,128)S(1)}, u32[]{:S(2)}, u32[]{:S(2)}) collective-permute-start(f32[40,1024]{1,0:T(8,128)S(1)} %collective-permute-done.1.refs_2_), channel_id=1, source_target_pairs={{0,1},{1,0},{2,3},{3,2},{4,5},{5,4},{6,7},{7,6},{8,9},{9,8},{10,11... | collective-permute-start | bytes 491528 | tf_op jit(solution)/shard_map/ppermute | solution.py:523
  21.6 4.9 %collective-permute-start.11 = (f32[40,1024]{1,0:T(8,128)S(1)}, f32[40,1024]{1,0:T(8,128)S(1)}, u32[]{:S(2)}, u32[]{:S(2)}) collective-permute-start(f32[40,1024]{1,0:T(8,128)S(1)} %collective-permute-done.2.refs_3_), channel_id=1, source_target_pairs={{0,1},{1,0},{2,3},{3,2},{4,5},{5,4},{6,7},{7,6},{8,9},{9,8},{10,11... | collective-permute-start | bytes 491528 | tf_op jit(solution)/shard_map/ppermute | solution.py:523
  22.1 4.4 %collective-permute-start.9 = (f32[40,1024]{1,0:T(8,128)S(1)}, f32[40,1024]{1,0:T(8,128)S(1)}, u32[]{:S(2)}, u32[]{:S(2)}) collective-permute-start(f32[40,1024]{1,0:T(8,128)S(1)} %collective-permute-done.refs_1_), channel_id=1, source_target_pairs={{0,1},{1,0},{2,3},{3,2},{4,5},{5,4},{6,7},{7,6},{8,9},{9,8},{10,11... | collective-permute-start | bytes 491528 | tf_op jit(solution)/shard_map/ppermute | solution.py:523
  22.1 15.3 %collective-permute-start.5 = (f32[8,1024]{1,0:T(8,128)S(1)}, f32[8,1024]{1,0:T(8,128)S(1)}, u32[]{:S(2)}, u32[]{:S(2)}) collective-permute-start(f32[8,1024]{1,0:T(8,128)S(1)} %get-tuple-element.31.refs_0_), channel_id=1, source_target_pairs={{0,2},{1,3},{2,0},{3,1},{4,6},{5,7},{6,4},{7,5},{8,10},{9,11},{10,... | collective-permute-start | bytes 98312 | tf_op jit(solution)/shard_map/ppermute | solution.py:523
  22.1 15.3 %collective-permute-start.6 = (f32[8,1024]{1,0:T(8,128)S(1)}, f32[8,1024]{1,0:T(8,128)S(1)}, u32[]{:S(2)}, u32[]{:S(2)}) collective-permute-start(f32[8,1024]{1,0:T(8,128)S(1)} %get-tuple-element.31.refs_0_), channel_id=1, source_target_pairs={{0,4},{1,5},{2,6},{3,7},{4,0},{5,1},{6,2},{7,3},{8,12},{9,13},{10,... | collective-permute-start | bytes 98312 | tf_op jit(solution)/shard_map/ppermute | solution.py:523
  25.2 12.3 %collective-permute-start.7 = (f32[8,1024]{1,0:T(8,128)S(1)}, f32[8,1024]{1,0:T(8,128)S(1)}, u32[]{:S(2)}, u32[]{:S(2)}) collective-permute-start(f32[8,1024]{1,0:T(8,128)S(1)} %get-tuple-element.31.refs_0_), channel_id=1, source_target_pairs={{0,6},{1,7},{2,4},{3,5},{4,2},{5,3},{6,0},{7,1},{8,14},{9,15},{10,... | collective-permute-start | bytes 98312 | tf_op jit(solution)/shard_map/ppermute | solution.py:523
  37.5 1.3 %collective-permute-start.12 = (f32[8,1024]{1,0:T(8,128)S(1)}, f32[8,1024]{1,0:T(8,128)S(1)}, u32[]{:S(2)}, u32[]{:S(2)}) collective-permute-start(f32[8,1024]{1,0:T(8,128)S(1)} %get-tuple-element.31.refs_0_), channel_id=1, source_target_pairs={{0,1},{1,0},{2,3},{3,2},{4,5},{5,4},{6,7},{7,6},{8,9},{9,8},{10,11... | collective-permute-start | bytes 98312 | tf_op jit(solution)/shard_map/ppermute | solution.py:523
  37.6 1.4 %collective-permute-start.13 = (f32[8,1024]{1,0:T(8,128)S(1)}, f32[8,1024]{1,0:T(8,128)S(1)}, u32[]{:S(2)}, u32[]{:S(2)}) collective-permute-start(f32[8,1024]{1,0:T(8,128)S(1)} %collective-permute-done.5.refs_1_), channel_id=1, source_target_pairs={{0,1},{1,0},{2,3},{3,2},{4,5},{5,4},{6,7},{7,6},{8,9},{9,8},{10,11... | collective-permute-start | bytes 98312 | tf_op jit(solution)/shard_map/ppermute | solution.py:523
  38.1 1.2 %collective-permute-start.14 = (f32[8,1024]{1,0:T(8,128)S(1)}, f32[8,1024]{1,0:T(8,128)S(1)}, u32[]{:S(2)}, u32[]{:S(2)}) collective-permute-start(f32[8,1024]{1,0:T(8,128)S(1)} %collective-permute-done.6.refs_2_), channel_id=1, source_target_pairs={{0,1},{1,0},{2,3},{3,2},{4,5},{5,4},{6,7},{7,6},{8,9},{9,8},{10,11... | collective-permute-start | bytes 98312 | tf_op jit(solution)/shard_map/ppermute | solution.py:523
  38.1 1.3 %collective-permute-start.15 = (f32[8,1024]{1,0:T(8,128)S(1)}, f32[8,1024]{1,0:T(8,128)S(1)}, u32[]{:S(2)}, u32[]{:S(2)}) collective-permute-start(f32[8,1024]{1,0:T(8,128)S(1)} %collective-permute-done.7.refs_3_), channel_id=1, source_target_pairs={{0,1},{1,0},{2,3},{3,2},{4,5},{5,4},{6,7},{7,6},{8,9},{9,8},{10,11... | collective-permute-start | bytes 98312 | tf_op jit(solution)/shard_map/ppermute | solution.py:523

commit v4 on v3

--- a/solution.py
+++ b/solution.py
@@ -30,18 +30,20 @@
     return [sorted(level) for level in levels[::-1]]
 
 
+EXPAND = 4
 SMALL_VMEM = 8
 PACK_VMEM = 60
 WEIGHT_VMEM = 24
 STEP_VMEM = 24
 
 def fetch(refs, held, me, sem, order):
-    half = len(refs) // 2
+    half = held.shape[0] // 2
     copies = []
     for j in range(half):
         for other in range(2):
             at = other * half + j
-            copies.append(pltpu.make_async_copy(refs[at], held.at[me ^ (2 * order[j] + other)], sem.at[at]))
+            src = refs[at] if len(refs) > half else refs[j].at[pl.ds(other * held.shape[1], held.shape[1])]
+            copies.append(pltpu.make_async_copy(src, held.at[me ^ (2 * order[j] + other)], sem.at[at]))
     for copy in copies:
         copy.start()
     for copy in copies:
@@ -88,7 +90,7 @@
                 gplaces[d, :, pl.ds((2 * sub + side) * LANES, LANES)] = place.astype(jnp.int32)
         return carry
 
-    lax.fori_loop(0, domains, expand, 0)
+    lax.fori_loop(0, domains, expand, 0, unroll=EXPAND)
 
     def domain_of(offset):
         return lax.rem(offset + me, domains)
@@ -166,10 +168,11 @@
 
 
 def step_kernel(domains, slots, subs, plan, own_index, *refs):
-    now_refs = refs[:domains]
-    weight, close, gplaces = refs[domains : domains + 3]
-    out_pos, out_vel = refs[domains + 3 : domains + 5]
-    now, state, vels, long_, ghost, sem = refs[domains + 5 :]
+    half = domains // 2
+    now_refs = refs[:half]
+    weight, close, gplaces = refs[half : half + 3]
+    out_pos, out_vel = refs[half + 3 : half + 5]
+    now, state, vels, long_, ghost, sem = refs[half + 5 :]
     seg = now.shape[2]
     evals = vels.shape[0]
     cells = seg // LANES
@@ -198,7 +201,7 @@
             long_[d, :, here] = spread(d, FAR, q * LANES)
         return carry
 
-    lax.fori_loop(0, domains, expand, 0)
+    lax.fori_loop(0, domains, expand, 0, unroll=EXPAND)
 
     def domain_of(offset):
         return lax.rem(offset + me, domains)
@@ -324,7 +327,7 @@
 VMEM = pl.BlockSpec(memory_space=pltpu.VMEM)
 
 
-def pair_weights(blocks, slots, subs, own_index, most=2, most_owners=4):
+def pair_weights(blocks, slots, subs, own_index, most=4, most_owners=8):
     domains = len(blocks)
     rows, seg = blocks[0].shape
     levels = level_halves(domains, 2 * subs)
@@ -359,9 +362,9 @@
     )(*blocks)
 
 
-def step(now, weights, subs, own_index, most=8, most_owners=8):
-    domains = len(now)
-    rows, seg = now[0].shape
+def step(now, weights, subs, own_index, most=16, most_owners=8):
+    domains = 2 * len(now)
+    rows, seg = now[0].shape[0] // 2, now[0].shape[1]
     slots = weights[0].shape[2]
     levels = level_halves(domains, 2 * subs)
     plan = {"levels": []}
@@ -379,7 +382,7 @@
     return pl.pallas_call(
         kernel,
         out_shape=[jax.ShapeDtypeStruct((3, seg), jnp.float32)] * 2,
-        in_specs=[ANYWHERE] * domains + [VMEM] * 3,
+        in_specs=[ANYWHERE] * len(now) + [VMEM] * 3,
         out_specs=[VMEM] * 2,
         scratch_shapes=[
             pltpu.VMEM((domains, rows, seg), jnp.float32),
@@ -396,20 +399,17 @@
 
 
 def pack_kernel(*refs):
-    here, (block, state), held, sem = refs[:6], refs[6:8], refs[8:14], refs[14]
+    here, block, held, sem = refs[:4], refs[4], refs[5:9], refs[9]
     copies = [pltpu.make_async_copy(src, dst, sem.at[n]) for n, (src, dst) in enumerate(zip(here, held))]
     for copy in copies:
         copy.start()
     for copy in copies:
         copy.wait()
-    positions, line_vectors, burgers, mobility, close_list, ghost_map = held
+    line_vectors, burgers, close_list, ghost_map = held
     slots, seg = close_list.shape
     block[:slots, :] = close_list[...].astype(jnp.float32)
-    state[0:3, :] = positions[...]
-    for at, ref in ((0, line_vectors), (3, burgers)):
-        block[slots + at : slots + at + 3, :] = ref[...]
-        state[3 + at : 6 + at, :] = ref[...]
-    state[9:10, :] = mobility[...]
+    block[slots : slots + 3, :] = line_vectors[...]
+    block[slots + 3 : slots + 6, :] = burgers[...]
     subs, wide = ghost_map.shape
     per = seg // wide
     for t in range(subs):
@@ -418,13 +418,13 @@
 
 
 def packed(*arrays):
-    slots, seg = arrays[4].shape
+    slots, seg = arrays[2].shape
     return pl.pallas_call(
         pack_kernel,
-        out_shape=[jax.ShapeDtypeStruct((slots + 6 + arrays[5].size // seg, seg), jnp.float32), jax.ShapeDtypeStruct((10, seg), jnp.float32)],
-        in_specs=[pl.BlockSpec(memory_space=pltpu.HBM)] * 6,
-        out_specs=[VMEM] * 2,
-        scratch_shapes=[pltpu.VMEM(a.shape, a.dtype) for a in arrays] + [pltpu.SemaphoreType.DMA((6,))],
+        out_shape=jax.ShapeDtypeStruct((slots + 6 + arrays[3].size // seg, seg), jnp.float32),
+        in_specs=[pl.BlockSpec(memory_space=pl.ANY)] * len(arrays),
+        out_specs=VMEM,
+        scratch_shapes=[pltpu.VMEM(a.shape, a.dtype) for a in arrays] + [pltpu.SemaphoreType.DMA((len(arrays),))],
         compiler_params=pltpu.CompilerParams(vmem_limit_bytes=PACK_VMEM * 2**20),
         name="pack",
     )(*arrays)
@@ -536,18 +536,20 @@
     subs = ghost_map.shape[0]
     half = lax.axis_size("dom") // 2
     own_index = lambda: lax.axis_index("dom")
-    block, state = packed(positions, line_vectors, burgers, mobility[None], close_list, ghost_map)
+    block = packed(line_vectors, burgers, close_list, ghost_map)
+    state = jnp.concatenate([positions, line_vectors, burgers, mobility[None]], 0)
     others = cycle_neighbours(state, "blk")
     far_first = range(half - 1, 0, -1)
     blocks = [matched(block, "dom", 2 * j) for j in far_first[:3]]
     now, block = long_range(state, others, block)
-    blocks, now = lax.optimization_barrier((blocks, now))
+    pair = jnp.concatenate([now, matched(now, "dom", 1)], 0)
+    blocks, _ = lax.optimization_barrier((blocks, now))
+    now = pair
     nows = [now] + [matched(now, "dom", 2 * j) for j in range(1, half)]
     blocks = [block] + blocks
     blocks = blocks + [matched(b, "dom", 1) for b in blocks]
     weights = pair_weights(blocks, slots, subs, own_index)
     nows, weights = lax.optimization_barrier((nows, weights))
-    nows = nows + [matched(n, "dom", 1) for n in nows]
     return tuple(step(nows, weights, subs, own_index))
 
 

time: 56.5 us -> 53.8 us (0.952)
  waiting for transfers between devices: 7.38 us -> 6 us
  Pallas kernels: 31.5 us -> 30.3 us
  local copies, waits for them, and re-layouts: 1.75 us -> 0.92 us
  other arithmetic: 0 us -> 0.79 us
    ppermute x15 -> x12, waiting for transfers between devices: 5.14 us -> 3.77 us  [matched(): return lax.ppermute(value, axis, [(i, i ^ step) for i in range(count)])]
    pallas_call x1, Pallas kernels: 10.9 us -> 10.1 us  [pair_weights(): pl.pallas_call(kernel, out_shape=[jax.ShapeDtypeStruct((subs, domains, sl...]
    unnamed x4 -> x3, local copies, waits for them, and re-layouts: 1.75 us -> 0.92 us
    concatenate x0 -> x1, other arithmetic: none -> 0.79 us  [local(): jnp.concatenate([positions, line_vectors, burgers, mobility[None]], 0)]
    ppermute x15 -> x12, starting transfers between devices: 13.4 us -> 13 us  [matched(): return lax.ppermute(value, axis, [(i, i ^ step) for i in range(count)])]
  transfers between devices with their start and end apart: 16 -> 13, of which waited for: 7 -> 3; matrix products, arithmetic and copies ran while one was open for 0% -> 1% of each run, Pallas kernels for 23% -> 23%
where the time goes in v4:
time: 53.8 us; the launch traced here: 53.4 us
  Pallas kernels  30.3 us (56%)
  starting transfers between devices  14.5 us (27%)
  waiting for transfers between devices  6 us (11%)
  local copies, waits for them, and re-layouts  0.92 us (2%)
  between operations  0.88 us (2%)
  other arithmetic  0.79 us (1%)
    pallas_call x1, Pallas kernels, step(): pl.pallas_call(kernel, out_shape=[jax.ShapeDtypeStruct((3, seg), jnp.floa...  16.5 us
    ppermute x12, starting transfers between devices, matched(): return lax.ppermute(value, axis, [(i, i ^ step) for i in range(count)])  13 us
    pallas_call x1, Pallas kernels, pair_weights(): pl.pallas_call(kernel, out_shape=[jax.ShapeDtypeStruct((subs, domains, sl...  10.1 us
    ppermute x12, waiting for transfers between devices, matched(): return lax.ppermute(value, axis, [(i, i ^ step) for i in range(count)])  3.77 us
    ppermute x1, waiting for transfers between devices, cycle_neighbours(): lax.ppermute(value, axis, [(i, ((i - 1) % count ^ 1) + 1 if (i - 1) % cou...  2.23 us
    pallas_call x1, Pallas kernels, long_range(): pl.pallas_call(lambda *refs: long_kernel(len(others), seg, unroll, *refs)...  1.98 us
    pallas_call x1, Pallas kernels, packed(): pl.pallas_call(pack_kernel, out_shape=jax.ShapeDtypeStruct((slots + 6 + a...  1.66 us
    ppermute x1, starting transfers between devices, cycle_neighbours(): lax.ppermute(value, axis, [(i, ((i - 1) % count ^ 1) + 1 if (i - 1) % cou...  1.49 us
  transfers between devices with their start and end apart: 13, of which 3 were waited for; matrix products, arithmetic and copies ran while one was open for 1% of the time, Pallas kernels for 23%

profile of v4, /device:TPU:0, one launch (start us, length us, event | category | flops | bytes accessed | tf_op | source)
XLA Modules:
  0.0 53.4 jit_solution(13704132973681004165)
XLA Ops:
  0.6 1.7 %pack.1.refs_3_ = f32[40,1024]{1,0:T(8,128)} custom-call(f32[3,1024]{1,0:T(4,128)} %refs_0_.1, f32[3,1024]{1,0:T(4,128)} %refs_1_.1, s32[32,1024]{1,0:T(8,128)} %refs_2_.1, s32[4,512]{1,0:T(4,128)} %refs_3_.1), custom_call_target="tpu_custom_call" | custom-call | tf_op jit(solution)/shard_map/pack/pallas_call | solution.py:422
  2.3 5.1 %collective-permute-start.6 = (f32[40,1024]{1,0:T(8,128)}, f32[40,1024]{1,0:T(8,128)S(1)}, u32[]{:S(2)}, u32[]{:S(2)}) collective-permute-start(f32[40,1024]{1,0:T(8,128)} %pack.1.refs_3_), channel_id=1, source_target_pairs={{0,6},{1,7},{2,4},{3,5},{4,2},{5,3},{6,0},{7,1},{8,14},{9,15},{10,... | collective-permute-start | bytes 491528 | tf_op jit(solution)/shard_map/ppermute | solution.py:523
  7.4 0.0 collective-permute-start.7
  7.4 0.6 %collective-permute-start.8 = (f32[40,1024]{1,0:T(8,128)}, f32[40,1024]{1,0:T(8,128)S(1)}, u32[]{:S(2)}, u32[]{:S(2)}) collective-permute-start(f32[40,1024]{1,0:T(8,128)} %pack.1.refs_3_), channel_id=1, source_target_pairs={{0,2},{1,3},{2,0},{3,1},{4,6},{5,7},{6,4},{7,5},{8,10},{9,11},{10,... | collective-permute-start | bytes 491528 | tf_op jit(solution)/shard_map/ppermute | solution.py:523
  8.1 0.8 %pad_maximum_fusion.refs_0_ = f32[10,1024]{1,0:T(8,128)S(1)} fusion(f32[1,1024]{1,0:T(1,128)} %bitcast.1, f32[3,1024]{1,0:T(4,128)} %refs_1_.1, f32[3,1024]{1,0:T(4,128)} %refs_0_.1, f32[3,1024]{1,0:T(4,128)} %param.6), kind=kLoop, calls=%fused_computation | loop fusion | flops 30720 | bytes 81920 | tf_op jit(solution)/shard_map/concatenate | solution.py:540
  8.8 1.7 %collective-permute-start = (f32[10,1024]{1,0:T(8,128)S(1)}, f32[10,1024]{1,0:T(8,128)S(1)}, u32[]{:S(2)}, u32[]{:S(2)}) collective-permute-start(f32[10,1024]{1,0:T(8,128)S(1)} %pad_maximum_fusion.refs_0_), channel_id=1, source_target_pairs={{0,8},{8,0},{16,24},{24,16},{1,9},{9,1},{17,25},{25,17},{2,10},{10... | collective-permute-start | bytes 122888 | tf_op jit(solution)/shard_map/ppermute | solution.py:523
  10.5 1.5 %collective-permute-start.1 = (f32[10,1024]{1,0:T(8,128)S(1)}, f32[10,1024]{1,0:T(8,128)S(1)}, u32[]{:S(2)}, u32[]{:S(2)}) collective-permute-start(f32[10,1024]{1,0:T(8,128)S(1)} %pad_maximum_fusion.refs_0_), channel_id=1, source_target_pairs={{0,24},{8,16},{16,8},{24,0},{1,25},{9,17},{17,9},{25,1},{2,26},{10... | collective-permute-start | bytes 122888 | tf_op jit(solution)/shard_map/ppermute | solution.py:528
  12.0 1.4 %collective-permute-done.refs_1_ = f32[10,1024]{1,0:T(8,128)S(1)} collective-permute-done((f32[10,1024]{1,0:T(8,128)S(1)}, f32[10,1024]{1,0:T(8,128)S(1)}, u32[]{:S(2)}, u32[]{:S(2)}) %collective-permute-start) | collective-permute-done | bytes 40992 | tf_op jit(solution)/shard_map/ppermute | solution.py:523
  13.5 2.2 %collective-permute-done.1.refs_2_ = f32[10,1024]{1,0:T(8,128)S(1)} collective-permute-done((f32[10,1024]{1,0:T(8,128)S(1)}, f32[10,1024]{1,0:T(8,128)S(1)}, u32[]{:S(2)}, u32[]{:S(2)}) %collective-permute-start.1) | collective-permute-done | bytes 40992 | tf_op jit(solution)/shard_map/ppermute | solution.py:528
  15.7 0.0 copy-start
  15.7 0.9 %copy-done = f32[40,1024]{1,0:T(8,128)S(1)} copy-done((f32[40,1024]{1,0:T(8,128)S(1)}, f32[40,1024]{1,0:T(8,128)}, u32[]{:S(2)}) %copy-start) | copy-done | bytes 163864
  16.6 2.0 %long_range.1 = (f32[8,1024]{1,0:T(8,128)S(1)}, f32[40,1024]{1,0:T(8,128)S(1)}) custom-call(f32[10,1024]{1,0:T(8,128)S(1)} %pad_maximum_fusion.refs_0_, f32[10,1024]{1,0:T(8,128)S(1)} %collective-permute-done.refs_1_, f32[10,1024]{1,0:T(8,128)S(1)} %collective-permute-done.1.refs_2_, f32[40,1024]{1,0:T(8,128)S(1)} %copy-done), custom_call_target="tpu_custom_call" | custom-call | flops 10000000 | bytes 20000000 | tf_op jit(solution)/shard_map/long_range/pallas_call | solution.py:504
  18.6 0.1 collective-permute-start.9
  18.7 0.5 collective-permute-start.2
  19.2 0.0 collective-permute-done.6.refs_1_
  19.2 2.3 %collective-permute-done.7.refs_2_ = f32[40,1024]{1,0:T(8,128)S(1)} collective-permute-done((f32[40,1024]{1,0:T(8,128)}, f32[40,1024]{1,0:T(8,128)S(1)}, u32[]{:S(2)}, u32[]{:S(2)}) %collective-permute-start.7) | collective-permute-done | bytes 163872 | tf_op jit(solution)/shard_map/ppermute | solution.py:523
  21.5 0.0 collective-permute-done.8.refs_3_
  21.5 0.0 collective-permute-start.10
  21.5 0.5 collective-permute-start.11
  22.0 0.1 collective-permute-start.12
  22.1 0.0 collective-permute-done.2
  22.1 0.0 collective-permute-start.3
  22.2 0.0 collective-permute-done.9.refs_4_
  22.2 3.0 %collective-permute-start.4 = (f32[16,1024]{1,0:T(8,128)S(1)}, f32[16,1024]{1,0:T(8,128)S(1)}, u32[]{:S(2)}, u32[]{:S(2)}) collective-permute-start(f32[16,1024]{1,0:T(8,128)S(1)} %constant_dynamic-update-slice_fusion.refs_0_), channel_id=1, source_target_pairs={{0,4},{1,5},{2,6},{3,7},{4,0},{5,1},{6,2},{7,3},{8,12},{9,13},{10,... | collective-permute-start | bytes 196616 | tf_op jit(solution)/shard_map/ppermute | solution.py:523
  25.2 0.0 collective-permute-done.10.refs_5_
  25.2 1.3 %collective-permute-start.5 = (f32[16,1024]{1,0:T(8,128)S(1)}, f32[16,1024]{1,0:T(8,128)S(1)}, u32[]{:S(2)}, u32[]{:S(2)}) collective-permute-start(f32[16,1024]{1,0:T(8,128)S(1)} %constant_dynamic-update-slice_fusion.refs_0_), channel_id=1, source_target_pairs={{0,6},{1,7},{2,4},{3,5},{4,2},{5,3},{6,0},{7,1},{8,14},{9,15},{10,... | collective-permute-start | bytes 196616 | tf_op jit(solution)/shard_map/ppermute | solution.py:523
  26.5 0.0 collective-permute-done.11.refs_6_
  26.5 0.0 collective-permute-done.12.refs_7_
  26.5 10.1 %weights.1 = (f32[4,8,32,1024]{3,2,1,0:T(8,128)S(1)}, s32[8,32,1024]{2,1,0:T(8,128)S(1)}, s32[8,8,1024]{2,1,0:T(8,128)S(1)}) custom-call(f32[40,1024]{1,0:T(8,128)S(1)} %get-tuple-element.18.refs_0_, f32[40,1024]{1,0:T(8,128)S(1)} %collective-permute-done.6.refs_1_, f32[40,1024]{1,0:T(8,128)S(1)} %collective-permute-done.7.refs_2_, ...), custom_call_target="tpu_custom_call" | custom-call | flops 10000000 | bytes 40000000 | tf_op jit(solution)/shard_map/weights/pallas_call | solution.py:344
  36.6 0.0 collective-permute-done.3.refs_1_
  36.6 0.0 collective-permute-done.4.refs_2_
  36.7 0.0 collective-permute-done.5.refs_3_
  36.7 16.5 %step.1 = (f32[3,1024]{1,0:T(4,128)}, f32[3,1024]{1,0:T(4,128)}) custom-call(f32[16,1024]{1,0:T(8,128)S(1)} %constant_dynamic-update-slice_fusion.refs_0_, f32[16,1024]{1,0:T(8,128)S(1)} %collective-permute-done.3.refs_1_, f32[16,1024]{1,0:T(8,128)S(1)} %collective-permute-done.4.refs_2_, f32[16,1024]{1,0:T(8,128)S(1)} %collective-permute-done.5.refs_3_, ...), custom_call_target="tpu_custom_call" | custom-call | flops 10000000 | bytes 60000000 | tf_op jit(solution)/shard_map/step/pallas_call | solution.py:382
  (2 shorter events, 0.0 us)
Async XLA Ops:
  2.3 16.9 %collective-permute-start.6 = (f32[40,1024]{1,0:T(8,128)}, f32[40,1024]{1,0:T(8,128)S(1)}, u32[]{:S(2)}, u32[]{:S(2)}) collective-permute-start(f32[40,1024]{1,0:T(8,128)} %pack.1.refs_3_), channel_id=1, source_target_pairs={{0,6},{1,7},{2,4},{3,5},{4,2},{5,3},{6,0},{7,1},{8,14},{9,15},{10,... | collective-permute-start | bytes 491528 | tf_op jit(solution)/shard_map/ppermute | solution.py:523
  7.4 14.1 %collective-permute-start.7 = (f32[40,1024]{1,0:T(8,128)}, f32[40,1024]{1,0:T(8,128)S(1)}, u32[]{:S(2)}, u32[]{:S(2)}) collective-permute-start(f32[40,1024]{1,0:T(8,128)} %pack.1.refs_3_), channel_id=1, source_target_pairs={{0,4},{1,5},{2,6},{3,7},{4,0},{5,1},{6,2},{7,3},{8,12},{9,13},{10,... | collective-permute-start | bytes 491528 | tf_op jit(solution)/shard_map/ppermute | solution.py:523
  7.4 14.1 %collective-permute-start.8 = (f32[40,1024]{1,0:T(8,128)}, f32[40,1024]{1,0:T(8,128)S(1)}, u32[]{:S(2)}, u32[]{:S(2)}) collective-permute-start(f32[40,1024]{1,0:T(8,128)} %pack.1.refs_3_), channel_id=1, source_target_pairs={{0,2},{1,3},{2,0},{3,1},{4,6},{5,7},{6,4},{7,5},{8,10},{9,11},{10,... | collective-permute-start | bytes 491528 | tf_op jit(solution)/shard_map/ppermute | solution.py:523
  8.8 4.6 %collective-permute-start = (f32[10,1024]{1,0:T(8,128)S(1)}, f32[10,1024]{1,0:T(8,128)S(1)}, u32[]{:S(2)}, u32[]{:S(2)}) collective-permute-start(f32[10,1024]{1,0:T(8,128)S(1)} %pad_maximum_fusion.refs_0_), channel_id=1, source_target_pairs={{0,8},{8,0},{16,24},{24,16},{1,9},{9,1},{17,25},{25,17},{2,10},{10... | collective-permute-start | bytes 122888 | tf_op jit(solution)/shard_map/ppermute | solution.py:523
  10.5 5.2 %collective-permute-start.1 = (f32[10,1024]{1,0:T(8,128)S(1)}, f32[10,1024]{1,0:T(8,128)S(1)}, u32[]{:S(2)}, u32[]{:S(2)}) collective-permute-start(f32[10,1024]{1,0:T(8,128)S(1)} %pad_maximum_fusion.refs_0_), channel_id=1, source_target_pairs={{0,24},{8,16},{16,8},{24,0},{1,25},{9,17},{17,9},{25,1},{2,26},{10... | collective-permute-start | bytes 122888 | tf_op jit(solution)/shard_map/ppermute | solution.py:528
  15.7 0.9 %copy-start = (f32[40,1024]{1,0:T(8,128)S(1)}, f32[40,1024]{1,0:T(8,128)}, u32[]{:S(2)}) copy-start(f32[40,1024]{1,0:T(8,128)} %pack.1.refs_3_) | copy-start | bytes 491524
  18.6 3.5 %collective-permute-start.9 = (f32[40,1024]{1,0:T(8,128)S(1)}, f32[40,1024]{1,0:T(8,128)S(1)}, u32[]{:S(2)}, u32[]{:S(2)}) collective-permute-start(f32[40,1024]{1,0:T(8,128)S(1)} %get-tuple-element.18.refs_0_), channel_id=1, source_target_pairs={{0,1},{1,0},{2,3},{3,2},{4,5},{5,4},{6,7},{7,6},{8,9},{9,8},{10,11... | collective-permute-start | bytes 491528 | tf_op jit(solution)/shard_map/ppermute | solution.py:523
  18.7 3.4 %collective-permute-start.2 = (f32[8,1024]{1,0:T(8,128)S(1)}, f32[8,1024]{1,0:T(8,128)S(1)}, u32[]{:S(2)}, u32[]{:S(2)}) collective-permute-start(f32[8,1024]{1,0:T(8,128)S(1)} %get-tuple-element.17), channel_id=1, source_target_pairs={{0,1},{1,0},{2,3},{3,2},{4,5},{5,4},{6,7},{7,6},{8,9},{9,8},{10,11... | collective-permute-start | bytes 98312 | tf_op jit(solution)/shard_map/ppermute | solution.py:523
  21.5 3.7 %collective-permute-start.10 = (f32[40,1024]{1,0:T(8,128)S(1)}, f32[40,1024]{1,0:T(8,128)S(1)}, u32[]{:S(2)}, u32[]{:S(2)}) collective-permute-start(f32[40,1024]{1,0:T(8,128)S(1)} %collective-permute-done.6.refs_1_), channel_id=1, source_target_pairs={{0,1},{1,0},{2,3},{3,2},{4,5},{5,4},{6,7},{7,6},{8,9},{9,8},{10,11... | collective-permute-start | bytes 491528 | tf_op jit(solution)/shard_map/ppermute | solution.py:523
  21.5 5.0 %collective-permute-start.11 = (f32[40,1024]{1,0:T(8,128)S(1)}, f32[40,1024]{1,0:T(8,128)S(1)}, u32[]{:S(2)}, u32[]{:S(2)}) collective-permute-start(f32[40,1024]{1,0:T(8,128)S(1)} %collective-permute-done.7.refs_2_), channel_id=1, source_target_pairs={{0,1},{1,0},{2,3},{3,2},{4,5},{5,4},{6,7},{7,6},{8,9},{9,8},{10,11... | collective-permute-start | bytes 491528 | tf_op jit(solution)/shard_map/ppermute | solution.py:523
  22.0 4.5 %collective-permute-start.12 = (f32[40,1024]{1,0:T(8,128)S(1)}, f32[40,1024]{1,0:T(8,128)S(1)}, u32[]{:S(2)}, u32[]{:S(2)}) collective-permute-start(f32[40,1024]{1,0:T(8,128)S(1)} %collective-permute-done.8.refs_3_), channel_id=1, source_target_pairs={{0,1},{1,0},{2,3},{3,2},{4,5},{5,4},{6,7},{7,6},{8,9},{9,8},{10,11... | collective-permute-start | bytes 491528 | tf_op jit(solution)/shard_map/ppermute | solution.py:523
  22.1 14.5 %collective-permute-start.3 = (f32[16,1024]{1,0:T(8,128)S(1)}, f32[16,1024]{1,0:T(8,128)S(1)}, u32[]{:S(2)}, u32[]{:S(2)}) collective-permute-start(f32[16,1024]{1,0:T(8,128)S(1)} %constant_dynamic-update-slice_fusion.refs_0_), channel_id=1, source_target_pairs={{0,2},{1,3},{2,0},{3,1},{4,6},{5,7},{6,4},{7,5},{8,10},{9,11},{10,... | collective-permute-start | bytes 196616 | tf_op jit(solution)/shard_map/ppermute | solution.py:523
  22.2 14.5 %collective-permute-start.4 = (f32[16,1024]{1,0:T(8,128)S(1)}, f32[16,1024]{1,0:T(8,128)S(1)}, u32[]{:S(2)}, u32[]{:S(2)}) collective-permute-start(f32[16,1024]{1,0:T(8,128)S(1)} %constant_dynamic-update-slice_fusion.refs_0_), channel_id=1, source_target_pairs={{0,4},{1,5},{2,6},{3,7},{4,0},{5,1},{6,2},{7,3},{8,12},{9,13},{10,... | collective-permute-start | bytes 196616 | tf_op jit(solution)/shard_map/ppermute | solution.py:523
  25.2 11.5 %collective-permute-start.5 = (f32[16,1024]{1,0:T(8,128)S(1)}, f32[16,1024]{1,0:T(8,128)S(1)}, u32[]{:S(2)}, u32[]{:S(2)}) collective-permute-start(f32[16,1024]{1,0:T(8,128)S(1)} %constant_dynamic-update-slice_fusion.refs_0_), channel_id=1, source_target_pairs={{0,6},{1,7},{2,4},{3,5},{4,2},{5,3},{6,0},{7,1},{8,14},{9,15},{10,... | collective-permute-start | bytes 196616 | tf_op jit(solution)/shard_map/ppermute | solution.py:523

commit v5 on v4

--- a/solution.py
+++ b/solution.py
@@ -43,7 +43,8 @@
         for other in range(2):
             at = other * half + j
             src = refs[at] if len(refs) > half else refs[j].at[pl.ds(other * held.shape[1], held.shape[1])]
-            copies.append(pltpu.make_async_copy(src, held.at[me ^ (2 * order[j] + other)], sem.at[at]))
+            place = lax.rem((me ^ (2 * order[j] + other)) - me + 2 * half, 2 * half)
+            copies.append(pltpu.make_async_copy(src, held.at[place], sem.at[at]))
     for copy in copies:
         copy.start()
     for copy in copies:
@@ -92,18 +93,15 @@
 
     lax.fori_loop(0, domains, expand, 0, unroll=EXPAND)
 
-    def domain_of(offset):
-        return lax.rem(offset + me, domains)
-
     def owner_picks(owners, sub, sources):
         made = []
         for offset, _ in owners:
-            d = domain_of(offset)
+            d = offset
             for side in range(2):
                 place = gplaces[d, :, pl.ds(pl.multiple_of((2 * sub + side) * LANES, LANES), LANES)]
                 lane = place & (LANES - 1)
                 cell = place >> 7
-                to = lax.rem(d + (1 if side else domains - 1), domains)
+                to = (d + (1 if side else domains - 1)) % domains
                 for source, ref, slot in sources:
                     out = None
                     for k in range(half_cells):
@@ -125,7 +123,7 @@
 
     def items(entries):
         for offset, side in entries:
-            d = domain_of(offset)
+            d = offset
             for k in range(half_cells):
                 lane = side * half_lanes + k * LANES
                 yield d, lane if isinstance(lane, int) else pl.multiple_of(lane, LANES), k
@@ -203,18 +201,15 @@
 
     lax.fori_loop(0, domains, expand, 0, unroll=EXPAND)
 
-    def domain_of(offset):
-        return lax.rem(offset + me, domains)
-
     def owner_picks(owners, sub, sources):
         made = []
         for offset, _ in owners:
-            d = domain_of(offset)
+            d = offset
             for side in range(2):
                 place = gplaces[d, :, pl.ds(pl.multiple_of((2 * sub + side) * LANES, LANES), LANES)]
                 lane = place & (LANES - 1)
                 cell = place >> 7
-                to = lax.rem(d + (1 if side else domains - 1), domains)
+                to = (d + (1 if side else domains - 1)) % domains
                 for source, ref, slot in sources:
                     out = None
                     for k in range(half_cells):
@@ -236,7 +231,7 @@
 
     def items(entries):
         for offset, side in entries:
-            d = domain_of(offset)
+            d = offset
             for k in range(half_cells):
                 lane = side * half_lanes + k * LANES
                 yield d, lane if isinstance(lane, int) else pl.multiple_of(lane, LANES), k
@@ -274,7 +269,7 @@
 
     def evaluate(level, owners, halves):
         sub = level // 2
-        stage = lax.rem(level, 2)
+        stage = level % 2
         base = level - stage
         over(owners, lambda owners: owner_picks(owners, sub, ((state.at[level], ghost, ()),)))
 
@@ -283,7 +278,8 @@
             for d, lane, k in items(entries):
                 here = pl.ds(lane, LANES)
                 vel = bcast(now, (d,), MOB, lane) * (long_[d, :, here] + force(level, sub, d, lane, k))
-                vel = jnp.where(stage == 1, 0.5 * (vels[base, d, :, here] + vel), vel)
+                if stage == 1:
+                    vel = 0.5 * (vels[base, d, :, here] + vel)
                 made.append((d, here, vel, state[base, d, :, here] + time_step * vel))
             for d, here, vel, moved in made:
                 vels[level, d, :, here] = vel
@@ -293,13 +289,13 @@
 
     for first, last, owners, halves in plan["levels"]:
         if last - first == 1:
-            evaluate(jnp.int32(first), owners, halves)
+            evaluate(first, owners, halves)
         else:
             lax.fori_loop(first, last, lambda level, carry: (evaluate(level, owners, halves), carry)[1], 0)
 
     for c in range(3):
-        out_pos[c : c + 1, :] = state[evals, me, 2 * c : 2 * c + 1, :]
-        out_vel[c : c + 1, :] = vels[evals - 1, me, 2 * c : 2 * c + 1, :]
+        out_pos[c : c + 1, :] = state[evals, 0, 2 * c : 2 * c + 1, :]
+        out_vel[c : c + 1, :] = vels[evals - 1, 0, 2 * c : 2 * c + 1, :]
 
 
 def span(entries, limit):
@@ -371,8 +367,6 @@
     first = 0
     while first < len(levels):
         last = first + 1
-        while last < len(levels) and levels[last] == levels[first]:
-            last += 1
         plan["levels"].append((first, last, span(owners_of(levels[first], domains), most_owners), span(levels[first], most)))
         first = last
 

time: 53.8 us -> 52.8 us (0.981)
  Pallas kernels: 30.3 us -> 29.3 us
    pallas_call x1, Pallas kernels: 16.5 us -> 15.6 us  [step(): pl.pallas_call(kernel, out_shape=[jax.ShapeDtypeStruct((3, seg), jnp.floa...]
  transfers between devices with their start and end apart: 13 -> 13, of which waited for: 3 -> 3; matrix products, arithmetic and copies ran while one was open for 1% -> 2% of each run, Pallas kernels for 23% -> 23%
where the time goes in v5:
time: 52.8 us; the launch traced here: 52.4 us
  Pallas kernels  29.3 us (55%)
  starting transfers between devices  14.5 us (27%)
  waiting for transfers between devices  6 us (11%)
  local copies, waits for them, and re-layouts  0.92 us (2%)
  between operations  0.88 us (2%)
  other arithmetic  0.79 us (1%)
    pallas_call x1, Pallas kernels, step(): pl.pallas_call(kernel, out_shape=[jax.ShapeDtypeStruct((3, seg), jnp.floa...  15.6 us
    ppermute x12, starting transfers between devices, matched(): return lax.ppermute(value, axis, [(i, i ^ step) for i in range(count)])  13 us
    pallas_call x1, Pallas kernels, pair_weights(): pl.pallas_call(kernel, out_shape=[jax.ShapeDtypeStruct((subs, domains, sl...  10.1 us
    ppermute x12, waiting for transfers between devices, matched(): return lax.ppermute(value, axis, [(i, i ^ step) for i in range(count)])  3.77 us
    ppermute x1, waiting for transfers between devices, cycle_neighbours(): lax.ppermute(value, axis, [(i, ((i - 1) % count ^ 1) + 1 if (i - 1) % cou...  2.23 us
    pallas_call x1, Pallas kernels, long_range(): pl.pallas_call(lambda *refs: long_kernel(len(others), seg, unroll, *refs)...  1.98 us
    pallas_call x1, Pallas kernels, packed(): pl.pallas_call(pack_kernel, out_shape=jax.ShapeDtypeStruct((slots + 6 + a...  1.66 us
    ppermute x1, starting transfers between devices, cycle_neighbours(): lax.ppermute(value, axis, [(i, ((i - 1) % count ^ 1) + 1 if (i - 1) % cou...  1.49 us
  transfers between devices with their start and end apart: 13, of which 3 were waited for; matrix products, arithmetic and copies ran while one was open for 2% of the time, Pallas kernels for 23%

profile of v5, /device:TPU:0, one launch (start us, length us, event | category | flops | bytes accessed | tf_op | source)
XLA Modules:
  0.0 52.4 jit_solution(7368314973145583538)
XLA Ops:
  0.6 1.7 %pack.1.refs_3_ = f32[40,1024]{1,0:T(8,128)} custom-call(f32[3,1024]{1,0:T(4,128)} %refs_0_.1, f32[3,1024]{1,0:T(4,128)} %refs_1_.1, s32[32,1024]{1,0:T(8,128)} %refs_2_.1, s32[4,512]{1,0:T(4,128)} %refs_3_.1), custom_call_target="tpu_custom_call" | custom-call | tf_op jit(solution)/shard_map/pack/pallas_call | solution.py:416
  2.3 5.1 %collective-permute-start.6 = (f32[40,1024]{1,0:T(8,128)}, f32[40,1024]{1,0:T(8,128)S(1)}, u32[]{:S(2)}, u32[]{:S(2)}) collective-permute-start(f32[40,1024]{1,0:T(8,128)} %pack.1.refs_3_), channel_id=1, source_target_pairs={{0,6},{1,7},{2,4},{3,5},{4,2},{5,3},{6,0},{7,1},{8,14},{9,15},{10,... | collective-permute-start | bytes 491528 | tf_op jit(solution)/shard_map/ppermute | solution.py:517
  7.4 0.0 collective-permute-start.7
  7.4 0.6 %collective-permute-start.8 = (f32[40,1024]{1,0:T(8,128)}, f32[40,1024]{1,0:T(8,128)S(1)}, u32[]{:S(2)}, u32[]{:S(2)}) collective-permute-start(f32[40,1024]{1,0:T(8,128)} %pack.1.refs_3_), channel_id=1, source_target_pairs={{0,2},{1,3},{2,0},{3,1},{4,6},{5,7},{6,4},{7,5},{8,10},{9,11},{10,... | collective-permute-start | bytes 491528 | tf_op jit(solution)/shard_map/ppermute | solution.py:517
  8.1 0.8 %pad_maximum_fusion.refs_0_ = f32[10,1024]{1,0:T(8,128)S(1)} fusion(f32[1,1024]{1,0:T(1,128)} %bitcast.1, f32[3,1024]{1,0:T(4,128)} %refs_1_.1, f32[3,1024]{1,0:T(4,128)} %refs_0_.1, f32[3,1024]{1,0:T(4,128)} %param.6), kind=kLoop, calls=%fused_computation | loop fusion | flops 30720 | bytes 81920 | tf_op jit(solution)/shard_map/concatenate | solution.py:534
  8.8 1.7 %collective-permute-start = (f32[10,1024]{1,0:T(8,128)S(1)}, f32[10,1024]{1,0:T(8,128)S(1)}, u32[]{:S(2)}, u32[]{:S(2)}) collective-permute-start(f32[10,1024]{1,0:T(8,128)S(1)} %pad_maximum_fusion.refs_0_), channel_id=1, source_target_pairs={{0,8},{8,0},{16,24},{24,16},{1,9},{9,1},{17,25},{25,17},{2,10},{10... | collective-permute-start | bytes 122888 | tf_op jit(solution)/shard_map/ppermute | solution.py:517
  10.5 1.5 %collective-permute-start.1 = (f32[10,1024]{1,0:T(8,128)S(1)}, f32[10,1024]{1,0:T(8,128)S(1)}, u32[]{:S(2)}, u32[]{:S(2)}) collective-permute-start(f32[10,1024]{1,0:T(8,128)S(1)} %pad_maximum_fusion.refs_0_), channel_id=1, source_target_pairs={{0,24},{8,16},{16,8},{24,0},{1,25},{9,17},{17,9},{25,1},{2,26},{10... | collective-permute-start | bytes 122888 | tf_op jit(solution)/shard_map/ppermute | solution.py:522
  12.0 1.4 %collective-permute-done.refs_1_ = f32[10,1024]{1,0:T(8,128)S(1)} collective-permute-done((f32[10,1024]{1,0:T(8,128)S(1)}, f32[10,1024]{1,0:T(8,128)S(1)}, u32[]{:S(2)}, u32[]{:S(2)}) %collective-permute-start) | collective-permute-done | bytes 40992 | tf_op jit(solution)/shard_map/ppermute | solution.py:517
  13.5 2.2 %collective-permute-done.1.refs_2_ = f32[10,1024]{1,0:T(8,128)S(1)} collective-permute-done((f32[10,1024]{1,0:T(8,128)S(1)}, f32[10,1024]{1,0:T(8,128)S(1)}, u32[]{:S(2)}, u32[]{:S(2)}) %collective-permute-start.1) | collective-permute-done | bytes 40992 | tf_op jit(solution)/shard_map/ppermute | solution.py:522
  15.7 0.0 copy-start
  15.7 0.9 %copy-done = f32[40,1024]{1,0:T(8,128)S(1)} copy-done((f32[40,1024]{1,0:T(8,128)S(1)}, f32[40,1024]{1,0:T(8,128)}, u32[]{:S(2)}) %copy-start) | copy-done | bytes 163864
  16.6 2.0 %long_range.1 = (f32[8,1024]{1,0:T(8,128)S(1)}, f32[40,1024]{1,0:T(8,128)S(1)}) custom-call(f32[10,1024]{1,0:T(8,128)S(1)} %pad_maximum_fusion.refs_0_, f32[10,1024]{1,0:T(8,128)S(1)} %collective-permute-done.refs_1_, f32[10,1024]{1,0:T(8,128)S(1)} %collective-permute-done.1.refs_2_, f32[40,1024]{1,0:T(8,128)S(1)} %copy-done), custom_call_target="tpu_custom_call" | custom-call | flops 10000000 | bytes 20000000 | tf_op jit(solution)/shard_map/long_range/pallas_call | solution.py:498
  18.6 0.1 collective-permute-start.9
  18.7 0.5 collective-permute-start.2
  19.2 0.0 collective-permute-done.6.refs_1_
  19.2 2.3 %collective-permute-done.7.refs_2_ = f32[40,1024]{1,0:T(8,128)S(1)} collective-permute-done((f32[40,1024]{1,0:T(8,128)}, f32[40,1024]{1,0:T(8,128)S(1)}, u32[]{:S(2)}, u32[]{:S(2)}) %collective-permute-start.7) | collective-permute-done | bytes 163872 | tf_op jit(solution)/shard_map/ppermute | solution.py:517
  21.5 0.0 collective-permute-done.8.refs_3_
  21.5 0.0 collective-permute-start.10
  21.5 0.5 collective-permute-start.11
  22.0 0.1 collective-permute-start.12
  22.1 0.0 collective-permute-done.2
  22.1 0.0 collective-permute-start.3
  22.2 0.0 collective-permute-done.9.refs_4_
  22.2 3.0 %collective-permute-start.4 = (f32[16,1024]{1,0:T(8,128)S(1)}, f32[16,1024]{1,0:T(8,128)S(1)}, u32[]{:S(2)}, u32[]{:S(2)}) collective-permute-start(f32[16,1024]{1,0:T(8,128)S(1)} %constant_dynamic-update-slice_fusion.refs_0_), channel_id=1, source_target_pairs={{0,4},{1,5},{2,6},{3,7},{4,0},{5,1},{6,2},{7,3},{8,12},{9,13},{10,... | collective-permute-start | bytes 196616 | tf_op jit(solution)/shard_map/ppermute | solution.py:517
  25.2 0.0 collective-permute-done.10.refs_5_
  25.2 1.3 %collective-permute-start.5 = (f32[16,1024]{1,0:T(8,128)S(1)}, f32[16,1024]{1,0:T(8,128)S(1)}, u32[]{:S(2)}, u32[]{:S(2)}) collective-permute-start(f32[16,1024]{1,0:T(8,128)S(1)} %constant_dynamic-update-slice_fusion.refs_0_), channel_id=1, source_target_pairs={{0,6},{1,7},{2,4},{3,5},{4,2},{5,3},{6,0},{7,1},{8,14},{9,15},{10,... | collective-permute-start | bytes 196616 | tf_op jit(solution)/shard_map/ppermute | solution.py:517
  26.5 0.0 collective-permute-done.11.refs_6_
  26.5 0.0 collective-permute-done.12.refs_7_
  26.5 10.1 %weights.1 = (f32[4,8,32,1024]{3,2,1,0:T(8,128)S(1)}, s32[8,32,1024]{2,1,0:T(8,128)S(1)}, s32[8,8,1024]{2,1,0:T(8,128)S(1)}) custom-call(f32[40,1024]{1,0:T(8,128)S(1)} %get-tuple-element.18.refs_0_, f32[40,1024]{1,0:T(8,128)S(1)} %collective-permute-done.6.refs_1_, f32[40,1024]{1,0:T(8,128)S(1)} %collective-permute-done.7.refs_2_, ...), custom_call_target="tpu_custom_call" | custom-call | flops 10000000 | bytes 40000000 | tf_op jit(solution)/shard_map/weights/pallas_call | solution.py:340
  36.6 0.0 collective-permute-done.3.refs_1_
  36.6 0.0 collective-permute-done.4.refs_2_
  36.7 0.0 collective-permute-done.5.refs_3_
  36.7 15.6 %step.1 = (f32[3,1024]{1,0:T(4,128)}, f32[3,1024]{1,0:T(4,128)}) custom-call(f32[16,1024]{1,0:T(8,128)S(1)} %constant_dynamic-update-slice_fusion.refs_0_, f32[16,1024]{1,0:T(8,128)S(1)} %collective-permute-done.3.refs_1_, f32[16,1024]{1,0:T(8,128)S(1)} %collective-permute-done.4.refs_2_, f32[16,1024]{1,0:T(8,128)S(1)} %collective-permute-done.5.refs_3_, ...), custom_call_target="tpu_custom_call" | custom-call | flops 10000000 | bytes 60000000 | tf_op jit(solution)/shard_map/step/pallas_call | solution.py:376
  (2 shorter events, 0.0 us)
Async XLA Ops:
  2.3 16.9 %collective-permute-start.6 = (f32[40,1024]{1,0:T(8,128)}, f32[40,1024]{1,0:T(8,128)S(1)}, u32[]{:S(2)}, u32[]{:S(2)}) collective-permute-start(f32[40,1024]{1,0:T(8,128)} %pack.1.refs_3_), channel_id=1, source_target_pairs={{0,6},{1,7},{2,4},{3,5},{4,2},{5,3},{6,0},{7,1},{8,14},{9,15},{10,... | collective-permute-start | bytes 491528 | tf_op jit(solution)/shard_map/ppermute | solution.py:517
  7.4 14.1 %collective-permute-start.7 = (f32[40,1024]{1,0:T(8,128)}, f32[40,1024]{1,0:T(8,128)S(1)}, u32[]{:S(2)}, u32[]{:S(2)}) collective-permute-start(f32[40,1024]{1,0:T(8,128)} %pack.1.refs_3_), channel_id=1, source_target_pairs={{0,4},{1,5},{2,6},{3,7},{4,0},{5,1},{6,2},{7,3},{8,12},{9,13},{10,... | collective-permute-start | bytes 491528 | tf_op jit(solution)/shard_map/ppermute | solution.py:517
  7.4 14.1 %collective-permute-start.8 = (f32[40,1024]{1,0:T(8,128)}, f32[40,1024]{1,0:T(8,128)S(1)}, u32[]{:S(2)}, u32[]{:S(2)}) collective-permute-start(f32[40,1024]{1,0:T(8,128)} %pack.1.refs_3_), channel_id=1, source_target_pairs={{0,2},{1,3},{2,0},{3,1},{4,6},{5,7},{6,4},{7,5},{8,10},{9,11},{10,... | collective-permute-start | bytes 491528 | tf_op jit(solution)/shard_map/ppermute | solution.py:517
  8.8 4.6 %collective-permute-start = (f32[10,1024]{1,0:T(8,128)S(1)}, f32[10,1024]{1,0:T(8,128)S(1)}, u32[]{:S(2)}, u32[]{:S(2)}) collective-permute-start(f32[10,1024]{1,0:T(8,128)S(1)} %pad_maximum_fusion.refs_0_), channel_id=1, source_target_pairs={{0,8},{8,0},{16,24},{24,16},{1,9},{9,1},{17,25},{25,17},{2,10},{10... | collective-permute-start | bytes 122888 | tf_op jit(solution)/shard_map/ppermute | solution.py:517
  10.5 5.2 %collective-permute-start.1 = (f32[10,1024]{1,0:T(8,128)S(1)}, f32[10,1024]{1,0:T(8,128)S(1)}, u32[]{:S(2)}, u32[]{:S(2)}) collective-permute-start(f32[10,1024]{1,0:T(8,128)S(1)} %pad_maximum_fusion.refs_0_), channel_id=1, source_target_pairs={{0,24},{8,16},{16,8},{24,0},{1,25},{9,17},{17,9},{25,1},{2,26},{10... | collective-permute-start | bytes 122888 | tf_op jit(solution)/shard_map/ppermute | solution.py:522
  15.7 0.9 %copy-start = (f32[40,1024]{1,0:T(8,128)S(1)}, f32[40,1024]{1,0:T(8,128)}, u32[]{:S(2)}) copy-start(f32[40,1024]{1,0:T(8,128)} %pack.1.refs_3_) | copy-start | bytes 491524
  18.6 3.5 %collective-permute-start.9 = (f32[40,1024]{1,0:T(8,128)S(1)}, f32[40,1024]{1,0:T(8,128)S(1)}, u32[]{:S(2)}, u32[]{:S(2)}) collective-permute-start(f32[40,1024]{1,0:T(8,128)S(1)} %get-tuple-element.18.refs_0_), channel_id=1, source_target_pairs={{0,1},{1,0},{2,3},{3,2},{4,5},{5,4},{6,7},{7,6},{8,9},{9,8},{10,11... | collective-permute-start | bytes 491528 | tf_op jit(solution)/shard_map/ppermute | solution.py:517
  18.7 3.4 %collective-permute-start.2 = (f32[8,1024]{1,0:T(8,128)S(1)}, f32[8,1024]{1,0:T(8,128)S(1)}, u32[]{:S(2)}, u32[]{:S(2)}) collective-permute-start(f32[8,1024]{1,0:T(8,128)S(1)} %get-tuple-element.17), channel_id=1, source_target_pairs={{0,1},{1,0},{2,3},{3,2},{4,5},{5,4},{6,7},{7,6},{8,9},{9,8},{10,11... | collective-permute-start | bytes 98312 | tf_op jit(solution)/shard_map/ppermute | solution.py:517
  21.5 3.7 %collective-permute-start.10 = (f32[40,1024]{1,0:T(8,128)S(1)}, f32[40,1024]{1,0:T(8,128)S(1)}, u32[]{:S(2)}, u32[]{:S(2)}) collective-permute-start(f32[40,1024]{1,0:T(8,128)S(1)} %collective-permute-done.6.refs_1_), channel_id=1, source_target_pairs={{0,1},{1,0},{2,3},{3,2},{4,5},{5,4},{6,7},{7,6},{8,9},{9,8},{10,11... | collective-permute-start | bytes 491528 | tf_op jit(solution)/shard_map/ppermute | solution.py:517
  21.5 5.0 %collective-permute-start.11 = (f32[40,1024]{1,0:T(8,128)S(1)}, f32[40,1024]{1,0:T(8,128)S(1)}, u32[]{:S(2)}, u32[]{:S(2)}) collective-permute-start(f32[40,1024]{1,0:T(8,128)S(1)} %collective-permute-done.7.refs_2_), channel_id=1, source_target_pairs={{0,1},{1,0},{2,3},{3,2},{4,5},{5,4},{6,7},{7,6},{8,9},{9,8},{10,11... | collective-permute-start | bytes 491528 | tf_op jit(solution)/shard_map/ppermute | solution.py:517
  22.0 4.5 %collective-permute-start.12 = (f32[40,1024]{1,0:T(8,128)S(1)}, f32[40,1024]{1,0:T(8,128)S(1)}, u32[]{:S(2)}, u32[]{:S(2)}) collective-permute-start(f32[40,1024]{1,0:T(8,128)S(1)} %collective-permute-done.8.refs_3_), channel_id=1, source_target_pairs={{0,1},{1,0},{2,3},{3,2},{4,5},{5,4},{6,7},{7,6},{8,9},{9,8},{10,11... | collective-permute-start | bytes 491528 | tf_op jit(solution)/shard_map/ppermute | solution.py:517
  22.1 14.5 %collective-permute-start.3 = (f32[16,1024]{1,0:T(8,128)S(1)}, f32[16,1024]{1,0:T(8,128)S(1)}, u32[]{:S(2)}, u32[]{:S(2)}) collective-permute-start(f32[16,1024]{1,0:T(8,128)S(1)} %constant_dynamic-update-slice_fusion.refs_0_), channel_id=1, source_target_pairs={{0,2},{1,3},{2,0},{3,1},{4,6},{5,7},{6,4},{7,5},{8,10},{9,11},{10,... | collective-permute-start | bytes 196616 | tf_op jit(solution)/shard_map/ppermute | solution.py:517
  22.2 14.5 %collective-permute-start.4 = (f32[16,1024]{1,0:T(8,128)S(1)}, f32[16,1024]{1,0:T(8,128)S(1)}, u32[]{:S(2)}, u32[]{:S(2)}) collective-permute-start(f32[16,1024]{1,0:T(8,128)S(1)} %constant_dynamic-update-slice_fusion.refs_0_), channel_id=1, source_target_pairs={{0,4},{1,5},{2,6},{3,7},{4,0},{5,1},{6,2},{7,3},{8,12},{9,13},{10,... | collective-permute-start | bytes 196616 | tf_op jit(solution)/shard_map/ppermute | solution.py:517
  25.2 11.5 %collective-permute-start.5 = (f32[16,1024]{1,0:T(8,128)S(1)}, f32[16,1024]{1,0:T(8,128)S(1)}, u32[]{:S(2)}, u32[]{:S(2)}) collective-permute-start(f32[16,1024]{1,0:T(8,128)S(1)} %constant_dynamic-update-slice_fusion.refs_0_), channel_id=1, source_target_pairs={{0,6},{1,7},{2,4},{3,5},{4,2},{5,3},{6,0},{7,1},{8,14},{9,15},{10,... | collective-permute-start | bytes 196616 | tf_op jit(solution)/shard_map/ppermute | solution.py:517

commit v6 on v5

--- a/solution.py
+++ b/solution.py
@@ -35,6 +35,10 @@
 PACK_VMEM = 60
 WEIGHT_VMEM = 24
 STEP_VMEM = 24
+
+def far_first(half):
+    return [*range(half // 2, half), *range(1, half // 2)]
+
 
 def fetch(refs, held, me, sem, order):
     half = held.shape[0] // 2
@@ -63,7 +67,7 @@
     me = own_index()
     scale = 1.0 / math.sqrt(slots)
     LINE, BURG, GHOST = slots, slots + 3, slots + 6
-    fetch(block_refs, pack, me, sem, [0, *range(domains // 2 - 1, 0, -1)])
+    fetch(block_refs, pack, me, sem, [0, *far_first(domains // 2)])
 
     row = lax.broadcasted_iota(jnp.int32, (ROWS, LANES), 0)
     x_rows = row < 2
@@ -323,7 +327,7 @@
 VMEM = pl.BlockSpec(memory_space=pltpu.VMEM)
 
 
-def pair_weights(blocks, slots, subs, own_index, most=4, most_owners=8):
+def pair_weights(blocks, slots, subs, own_index, most=6, most_owners=8):
     domains = len(blocks)
     rows, seg = blocks[0].shape
     levels = level_halves(domains, 2 * subs)
@@ -533,8 +537,7 @@
     block = packed(line_vectors, burgers, close_list, ghost_map)
     state = jnp.concatenate([positions, line_vectors, burgers, mobility[None]], 0)
     others = cycle_neighbours(state, "blk")
-    far_first = range(half - 1, 0, -1)
-    blocks = [matched(block, "dom", 2 * j) for j in far_first[:3]]
+    blocks = [matched(block, "dom", 2 * j) for j in far_first(half)]
     now, block = long_range(state, others, block)
     pair = jnp.concatenate([now, matched(now, "dom", 1)], 0)
     blocks, _ = lax.optimization_barrier((blocks, now))

time: 52.8 us -> 52.1 us (0.987)
  waiting for transfers between devices: 6 us -> 4.08 us
  starting transfers between devices: 14.5 us -> 16.1 us
    ppermute x12, waiting for transfers between devices: 3.77 us -> 1.99 us  [matched(): return lax.ppermute(value, axis, [(i, i ^ step) for i in range(count)])]
    ppermute x12, starting transfers between devices: 13 us -> 14.6 us  [matched(): return lax.ppermute(value, axis, [(i, i ^ step) for i in range(count)])]
  transfers between devices with their start and end apart: 13 -> 13, of which waited for: 3 -> 4; matrix products, arithmetic and copies ran while one was open for 2% -> 2% of each run, Pallas kernels for 23% -> 23%
where the time goes in v6:
time: 52.1 us; the launch traced here: 51.7 us
  Pallas kernels  28.9 us (55%)
  starting transfers between devices  16.1 us (31%)
  waiting for transfers between devices  4.08 us (8%)
  local copies, waits for them, and re-layouts  0.92 us (2%)
  between operations  0.86 us (2%)
  other arithmetic  0.79 us (2%)
    pallas_call x1, Pallas kernels, step(): pl.pallas_call(kernel, out_shape=[jax.ShapeDtypeStruct((3, seg), jnp.floa...  15.6 us
    ppermute x12, starting transfers between devices, matched(): return lax.ppermute(value, axis, [(i, i ^ step) for i in range(count)])  14.6 us
    pallas_call x1, Pallas kernels, pair_weights(): pl.pallas_call(kernel, out_shape=[jax.ShapeDtypeStruct((subs, domains, sl...  9.71 us
    ppermute x1, waiting for transfers between devices, cycle_neighbours(): lax.ppermute(value, axis, [(i, ((i - 1) % count ^ 1) + 1 if (i - 1) % cou...  2.09 us
    ppermute x12, waiting for transfers between devices, matched(): return lax.ppermute(value, axis, [(i, i ^ step) for i in range(count)])  1.99 us
    pallas_call x1, Pallas kernels, long_range(): pl.pallas_call(lambda *refs: long_kernel(len(others), seg, unroll, *refs)...  1.98 us
    pallas_call x1, Pallas kernels, packed(): pl.pallas_call(pack_kernel, out_shape=jax.ShapeDtypeStruct((slots + 6 + a...  1.66 us
    ppermute x1, starting transfers between devices, cycle_neighbours(): lax.ppermute(value, axis, [(i, ((i - 1) % count ^ 1) + 1 if (i - 1) % cou...  1.49 us
  transfers between devices with their start and end apart: 13, of which 4 were waited for; matrix products, arithmetic and copies ran while one was open for 2% of the time, Pallas kernels for 23%

profile of v6, /device:TPU:0, one launch (start us, length us, event | category | flops | bytes accessed | tf_op | source)
XLA Modules:
  0.0 51.7 jit_solution(5011482780842664848)
XLA Ops:
  0.6 1.7 %pack.1.refs_3_ = f32[40,1024]{1,0:T(8,128)} custom-call(f32[3,1024]{1,0:T(4,128)} %refs_0_.1, f32[3,1024]{1,0:T(4,128)} %refs_1_.1, s32[32,1024]{1,0:T(8,128)} %refs_2_.1, s32[4,512]{1,0:T(4,128)} %refs_3_.1), custom_call_target="tpu_custom_call" | custom-call | tf_op jit(solution)/shard_map/pack/pallas_call | solution.py:420
  2.3 4.1 %collective-permute-start.6 = (f32[40,1024]{1,0:T(8,128)}, f32[40,1024]{1,0:T(8,128)S(1)}, u32[]{:S(2)}, u32[]{:S(2)}) collective-permute-start(f32[40,1024]{1,0:T(8,128)} %pack.1.refs_3_), channel_id=1, source_target_pairs={{0,4},{1,5},{2,6},{3,7},{4,0},{5,1},{6,2},{7,3},{8,12},{9,13},{10,... | collective-permute-start | bytes 491528 | tf_op jit(solution)/shard_map/ppermute | solution.py:521
  6.4 1.3 %collective-permute-start.7 = (f32[40,1024]{1,0:T(8,128)}, f32[40,1024]{1,0:T(8,128)S(1)}, u32[]{:S(2)}, u32[]{:S(2)}) collective-permute-start(f32[40,1024]{1,0:T(8,128)} %pack.1.refs_3_), channel_id=1, source_target_pairs={{0,6},{1,7},{2,4},{3,5},{4,2},{5,3},{6,0},{7,1},{8,14},{9,15},{10,... | collective-permute-start | bytes 491528 | tf_op jit(solution)/shard_map/ppermute | solution.py:521
  7.7 0.2 collective-permute-start.8
  8.0 0.8 %pad_maximum_fusion.refs_0_ = f32[10,1024]{1,0:T(8,128)S(1)} fusion(f32[1,1024]{1,0:T(1,128)} %bitcast.1, f32[3,1024]{1,0:T(4,128)} %refs_1_.1, f32[3,1024]{1,0:T(4,128)} %refs_0_.1, f32[3,1024]{1,0:T(4,128)} %param.6), kind=kLoop, calls=%fused_computation | loop fusion | flops 30720 | bytes 81920 | tf_op jit(solution)/shard_map/concatenate | solution.py:538
  8.8 1.6 %collective-permute-start = (f32[10,1024]{1,0:T(8,128)S(1)}, f32[10,1024]{1,0:T(8,128)S(1)}, u32[]{:S(2)}, u32[]{:S(2)}) collective-permute-start(f32[10,1024]{1,0:T(8,128)S(1)} %pad_maximum_fusion.refs_0_), channel_id=1, source_target_pairs={{0,8},{8,0},{16,24},{24,16},{1,9},{9,1},{17,25},{25,17},{2,10},{10... | collective-permute-start | bytes 122888 | tf_op jit(solution)/shard_map/ppermute | solution.py:521
  10.3 1.5 %collective-permute-start.1 = (f32[10,1024]{1,0:T(8,128)S(1)}, f32[10,1024]{1,0:T(8,128)S(1)}, u32[]{:S(2)}, u32[]{:S(2)}) collective-permute-start(f32[10,1024]{1,0:T(8,128)S(1)} %pad_maximum_fusion.refs_0_), channel_id=1, source_target_pairs={{0,24},{8,16},{16,8},{24,0},{1,25},{9,17},{17,9},{25,1},{2,26},{10... | collective-permute-start | bytes 122888 | tf_op jit(solution)/shard_map/ppermute | solution.py:526
  11.8 1.6 %collective-permute-done.refs_1_ = f32[10,1024]{1,0:T(8,128)S(1)} collective-permute-done((f32[10,1024]{1,0:T(8,128)S(1)}, f32[10,1024]{1,0:T(8,128)S(1)}, u32[]{:S(2)}, u32[]{:S(2)}) %collective-permute-start) | collective-permute-done | bytes 40992 | tf_op jit(solution)/shard_map/ppermute | solution.py:521
  13.4 2.1 %collective-permute-done.1.refs_2_ = f32[10,1024]{1,0:T(8,128)S(1)} collective-permute-done((f32[10,1024]{1,0:T(8,128)S(1)}, f32[10,1024]{1,0:T(8,128)S(1)}, u32[]{:S(2)}, u32[]{:S(2)}) %collective-permute-start.1) | collective-permute-done | bytes 40992 | tf_op jit(solution)/shard_map/ppermute | solution.py:526
  15.5 0.0 copy-start
  15.5 0.9 %copy-done = f32[40,1024]{1,0:T(8,128)S(1)} copy-done((f32[40,1024]{1,0:T(8,128)S(1)}, f32[40,1024]{1,0:T(8,128)}, u32[]{:S(2)}) %copy-start) | copy-done | bytes 163864
  16.4 2.0 %long_range.1 = (f32[8,1024]{1,0:T(8,128)S(1)}, f32[40,1024]{1,0:T(8,128)S(1)}) custom-call(f32[10,1024]{1,0:T(8,128)S(1)} %pad_maximum_fusion.refs_0_, f32[10,1024]{1,0:T(8,128)S(1)} %collective-permute-done.refs_1_, f32[10,1024]{1,0:T(8,128)S(1)} %collective-permute-done.1.refs_2_, f32[40,1024]{1,0:T(8,128)S(1)} %copy-done), custom_call_target="tpu_custom_call" | custom-call | flops 10000000 | bytes 20000000 | tf_op jit(solution)/shard_map/long_range/pallas_call | solution.py:502
  18.4 0.1 collective-permute-start.9
  18.5 0.5 collective-permute-start.2
  19.0 0.0 collective-permute-done.6.refs_1_
  19.0 0.0 collective-permute-done.7.refs_2_
  19.0 0.2 collective-permute-done.8.refs_3_
  19.2 0.0 collective-permute-start.10
  19.2 0.5 collective-permute-start.11
  19.7 0.0 collective-permute-start.12
  19.8 0.2 collective-permute-done.2
  19.9 2.9 %collective-permute-start.3 = (f32[16,1024]{1,0:T(8,128)S(1)}, f32[16,1024]{1,0:T(8,128)S(1)}, u32[]{:S(2)}, u32[]{:S(2)}) collective-permute-start(f32[16,1024]{1,0:T(8,128)S(1)} %constant_dynamic-update-slice_fusion.refs_0_), channel_id=1, source_target_pairs={{0,2},{1,3},{2,0},{3,1},{4,6},{5,7},{6,4},{7,5},{8,10},{9,11},{10,... | collective-permute-start | bytes 196616 | tf_op jit(solution)/shard_map/ppermute | solution.py:521
  22.9 0.0 collective-permute-done.9.refs_4_
  22.9 1.9 %collective-permute-start.4 = (f32[16,1024]{1,0:T(8,128)S(1)}, f32[16,1024]{1,0:T(8,128)S(1)}, u32[]{:S(2)}, u32[]{:S(2)}) collective-permute-start(f32[16,1024]{1,0:T(8,128)S(1)} %constant_dynamic-update-slice_fusion.refs_0_), channel_id=1, source_target_pairs={{0,4},{1,5},{2,6},{3,7},{4,0},{5,1},{6,2},{7,3},{8,12},{9,13},{10,... | collective-permute-start | bytes 196616 | tf_op jit(solution)/shard_map/ppermute | solution.py:521
  24.8 0.0 collective-permute-done.10.refs_5_
  24.8 1.4 %collective-permute-start.5 = (f32[16,1024]{1,0:T(8,128)S(1)}, f32[16,1024]{1,0:T(8,128)S(1)}, u32[]{:S(2)}, u32[]{:S(2)}) collective-permute-start(f32[16,1024]{1,0:T(8,128)S(1)} %constant_dynamic-update-slice_fusion.refs_0_), channel_id=1, source_target_pairs={{0,6},{1,7},{2,4},{3,5},{4,2},{5,3},{6,0},{7,1},{8,14},{9,15},{10,... | collective-permute-start | bytes 196616 | tf_op jit(solution)/shard_map/ppermute | solution.py:521
  26.2 0.0 collective-permute-done.11.refs_6_
  26.2 0.0 collective-permute-done.12.refs_7_
  26.2 9.7 %weights.1 = (f32[4,8,32,1024]{3,2,1,0:T(8,128)S(1)}, s32[8,32,1024]{2,1,0:T(8,128)S(1)}, s32[8,8,1024]{2,1,0:T(8,128)S(1)}) custom-call(f32[40,1024]{1,0:T(8,128)S(1)} %get-tuple-element.18.refs_0_, f32[40,1024]{1,0:T(8,128)S(1)} %collective-permute-done.6.refs_1_, f32[40,1024]{1,0:T(8,128)S(1)} %collective-permute-done.7.refs_2_, ...), custom_call_target="tpu_custom_call" | custom-call | flops 10000000 | bytes 40000000 | tf_op jit(solution)/shard_map/weights/pallas_call | solution.py:344
  35.9 0.0 collective-permute-done.3.refs_1_
  35.9 0.0 collective-permute-done.4.refs_2_
  35.9 0.0 collective-permute-done.5.refs_3_
  36.0 15.6 %step.1 = (f32[3,1024]{1,0:T(4,128)}, f32[3,1024]{1,0:T(4,128)}) custom-call(f32[16,1024]{1,0:T(8,128)S(1)} %constant_dynamic-update-slice_fusion.refs_0_, f32[16,1024]{1,0:T(8,128)S(1)} %collective-permute-done.3.refs_1_, f32[16,1024]{1,0:T(8,128)S(1)} %collective-permute-done.4.refs_2_, f32[16,1024]{1,0:T(8,128)S(1)} %collective-permute-done.5.refs_3_, ...), custom_call_target="tpu_custom_call" | custom-call | flops 10000000 | bytes 60000000 | tf_op jit(solution)/shard_map/step/pallas_call | solution.py:380
  (2 shorter events, 0.0 us)
Async XLA Ops:
  2.3 16.7 %collective-permute-start.6 = (f32[40,1024]{1,0:T(8,128)}, f32[40,1024]{1,0:T(8,128)S(1)}, u32[]{:S(2)}, u32[]{:S(2)}) collective-permute-start(f32[40,1024]{1,0:T(8,128)} %pack.1.refs_3_), channel_id=1, source_target_pairs={{0,4},{1,5},{2,6},{3,7},{4,0},{5,1},{6,2},{7,3},{8,12},{9,13},{10,... | collective-permute-start | bytes 491528 | tf_op jit(solution)/shard_map/ppermute | solution.py:521
  6.4 12.6 %collective-permute-start.7 = (f32[40,1024]{1,0:T(8,128)}, f32[40,1024]{1,0:T(8,128)S(1)}, u32[]{:S(2)}, u32[]{:S(2)}) collective-permute-start(f32[40,1024]{1,0:T(8,128)} %pack.1.refs_3_), channel_id=1, source_target_pairs={{0,6},{1,7},{2,4},{3,5},{4,2},{5,3},{6,0},{7,1},{8,14},{9,15},{10,... | collective-permute-start | bytes 491528 | tf_op jit(solution)/shard_map/ppermute | solution.py:521
  7.7 11.5 %collective-permute-start.8 = (f32[40,1024]{1,0:T(8,128)}, f32[40,1024]{1,0:T(8,128)S(1)}, u32[]{:S(2)}, u32[]{:S(2)}) collective-permute-start(f32[40,1024]{1,0:T(8,128)} %pack.1.refs_3_), channel_id=1, source_target_pairs={{0,2},{1,3},{2,0},{3,1},{4,6},{5,7},{6,4},{7,5},{8,10},{9,11},{10,... | collective-permute-start | bytes 491528 | tf_op jit(solution)/shard_map/ppermute | solution.py:521
  8.8 4.6 %collective-permute-start = (f32[10,1024]{1,0:T(8,128)S(1)}, f32[10,1024]{1,0:T(8,128)S(1)}, u32[]{:S(2)}, u32[]{:S(2)}) collective-permute-start(f32[10,1024]{1,0:T(8,128)S(1)} %pad_maximum_fusion.refs_0_), channel_id=1, source_target_pairs={{0,8},{8,0},{16,24},{24,16},{1,9},{9,1},{17,25},{25,17},{2,10},{10... | collective-permute-start | bytes 122888 | tf_op jit(solution)/shard_map/ppermute | solution.py:521
  10.3 5.2 %collective-permute-start.1 = (f32[10,1024]{1,0:T(8,128)S(1)}, f32[10,1024]{1,0:T(8,128)S(1)}, u32[]{:S(2)}, u32[]{:S(2)}) collective-permute-start(f32[10,1024]{1,0:T(8,128)S(1)} %pad_maximum_fusion.refs_0_), channel_id=1, source_target_pairs={{0,24},{8,16},{16,8},{24,0},{1,25},{9,17},{17,9},{25,1},{2,26},{10... | collective-permute-start | bytes 122888 | tf_op jit(solution)/shard_map/ppermute | solution.py:526
  15.5 0.9 %copy-start = (f32[40,1024]{1,0:T(8,128)S(1)}, f32[40,1024]{1,0:T(8,128)}, u32[]{:S(2)}) copy-start(f32[40,1024]{1,0:T(8,128)} %pack.1.refs_3_) | copy-start | bytes 491524
  18.4 4.5 %collective-permute-start.9 = (f32[40,1024]{1,0:T(8,128)S(1)}, f32[40,1024]{1,0:T(8,128)S(1)}, u32[]{:S(2)}, u32[]{:S(2)}) collective-permute-start(f32[40,1024]{1,0:T(8,128)S(1)} %get-tuple-element.18.refs_0_), channel_id=1, source_target_pairs={{0,1},{1,0},{2,3},{3,2},{4,5},{5,4},{6,7},{7,6},{8,9},{9,8},{10,11... | collective-permute-start | bytes 491528 | tf_op jit(solution)/shard_map/ppermute | solution.py:521
  18.5 1.4 %collective-permute-start.2 = (f32[8,1024]{1,0:T(8,128)S(1)}, f32[8,1024]{1,0:T(8,128)S(1)}, u32[]{:S(2)}, u32[]{:S(2)}) collective-permute-start(f32[8,1024]{1,0:T(8,128)S(1)} %get-tuple-element.17), channel_id=1, source_target_pairs={{0,1},{1,0},{2,3},{3,2},{4,5},{5,4},{6,7},{7,6},{8,9},{9,8},{10,11... | collective-permute-start | bytes 98312 | tf_op jit(solution)/shard_map/ppermute | solution.py:521
  19.2 5.6 %collective-permute-start.10 = (f32[40,1024]{1,0:T(8,128)S(1)}, f32[40,1024]{1,0:T(8,128)S(1)}, u32[]{:S(2)}, u32[]{:S(2)}) collective-permute-start(f32[40,1024]{1,0:T(8,128)S(1)} %collective-permute-done.6.refs_1_), channel_id=1, source_target_pairs={{0,1},{1,0},{2,3},{3,2},{4,5},{5,4},{6,7},{7,6},{8,9},{9,8},{10,11... | collective-permute-start | bytes 491528 | tf_op jit(solution)/shard_map/ppermute | solution.py:521
  19.2 7.0 %collective-permute-start.11 = (f32[40,1024]{1,0:T(8,128)S(1)}, f32[40,1024]{1,0:T(8,128)S(1)}, u32[]{:S(2)}, u32[]{:S(2)}) collective-permute-start(f32[40,1024]{1,0:T(8,128)S(1)} %collective-permute-done.7.refs_2_), channel_id=1, source_target_pairs={{0,1},{1,0},{2,3},{3,2},{4,5},{5,4},{6,7},{7,6},{8,9},{9,8},{10,11... | collective-permute-start | bytes 491528 | tf_op jit(solution)/shard_map/ppermute | solution.py:521
  19.7 6.5 %collective-permute-start.12 = (f32[40,1024]{1,0:T(8,128)S(1)}, f32[40,1024]{1,0:T(8,128)S(1)}, u32[]{:S(2)}, u32[]{:S(2)}) collective-permute-start(f32[40,1024]{1,0:T(8,128)S(1)} %collective-permute-done.8.refs_3_), channel_id=1, source_target_pairs={{0,1},{1,0},{2,3},{3,2},{4,5},{5,4},{6,7},{7,6},{8,9},{9,8},{10,11... | collective-permute-start | bytes 491528 | tf_op jit(solution)/shard_map/ppermute | solution.py:521
  19.9 16.0 %collective-permute-start.3 = (f32[16,1024]{1,0:T(8,128)S(1)}, f32[16,1024]{1,0:T(8,128)S(1)}, u32[]{:S(2)}, u32[]{:S(2)}) collective-permute-start(f32[16,1024]{1,0:T(8,128)S(1)} %constant_dynamic-update-slice_fusion.refs_0_), channel_id=1, source_target_pairs={{0,2},{1,3},{2,0},{3,1},{4,6},{5,7},{6,4},{7,5},{8,10},{9,11},{10,... | collective-permute-start | bytes 196616 | tf_op jit(solution)/shard_map/ppermute | solution.py:521
  22.9 13.1 %collective-permute-start.4 = (f32[16,1024]{1,0:T(8,128)S(1)}, f32[16,1024]{1,0:T(8,128)S(1)}, u32[]{:S(2)}, u32[]{:S(2)}) collective-permute-start(f32[16,1024]{1,0:T(8,128)S(1)} %constant_dynamic-update-slice_fusion.refs_0_), channel_id=1, source_target_pairs={{0,4},{1,5},{2,6},{3,7},{4,0},{5,1},{6,2},{7,3},{8,12},{9,13},{10,... | collective-permute-start | bytes 196616 | tf_op jit(solution)/shard_map/ppermute | solution.py:521
  24.8 11.2 %collective-permute-start.5 = (f32[16,1024]{1,0:T(8,128)S(1)}, f32[16,1024]{1,0:T(8,128)S(1)}, u32[]{:S(2)}, u32[]{:S(2)}) collective-permute-start(f32[16,1024]{1,0:T(8,128)S(1)} %constant_dynamic-update-slice_fusion.refs_0_), channel_id=1, source_target_pairs={{0,6},{1,7},{2,4},{3,5},{4,2},{5,3},{6,0},{7,1},{8,14},{9,15},{10,... | collective-permute-start | bytes 196616 | tf_op jit(solution)/shard_map/ppermute | solution.py:521
